TPU v7x, 256 devices: a whole 4x4x8 slice. The times are simulated.
256 devices in a mesh: ctx: 16 (over x, y), tp: 16 (over z, core).
Axes of the slice: x: 4, y: 4, z: 8, core: 2. Of those that a mesh axis runs over, the one named last changes fastest.
Arguments:
- tokens: bfloat16 [32768, 2304], P(('ctx', 'tp')), may hold values from -5 to 5
- query_weight: bfloat16 [2304, 4096], P(None, 'tp'), may hold values from -0.125 to 0.125
- key_weight: bfloat16 [2304, 4096], P(None, 'tp'), may hold values from -0.125 to 0.125
- values_projector_matrix: bfloat16 [2304, 4096], P(None, 'tp'), may hold values from -0.125 to 0.125
- gate_weight: bfloat16 [2304, 4096], P(None, 'tp'), may hold values from -0.125 to 0.125
- beta_weight: bfloat16 [2304, 32], P(None, 'tp'), may hold values from -0.125 to 0.125
- beta_bias: float32 [32], P('tp'), may hold values from -5 to 1
- log_decay: float32 [32768, 4096], P('ctx', 'tp'), may hold values from -1 to 0
- head_gain: float32 [128], replicated, may hold values from 0.25 to 1.75
- output_weight: bfloat16 [4096, 2304], P('tp'), may hold values from -0.09375 to 0.09375
- kv_weight: bfloat16 [2304, 512], replicated, may hold values from -0.125 to 0.125
- kv_gain: float32 [512], replicated, may hold values from 0.25 to 1.75
- owner: int32 [16, 16], P(None, 'tp'), may hold values from 0 to 15, as said below
Outputs:
- mixed: bfloat16 [32768, 2304], P(('ctx', 'tp'))
- latent_cache: bfloat16 [64, 2048, 512], P('ctx', 'tp')
Inputs may be any that keep to these rules, and one draw needn't show every extreme that they name: In each column t, each owner receives at most 4 tiles, and some owner receives exactly 4.
All inputs are finite; a program needn't handle non-finite values.
Results may differ from a plain program's by a relative error of at most 0.029.
Values may be sent and summed in bfloat16 or wider, within the bound.
No kernel may reach another device: no remote copies, remote signals or barrier semaphores. Data moves between devices by JAX's collectives and lax.ppermute only.
A program may use at most 128 MiB of HBM per device.

v0:
```python
import jax
import jax.numpy as jnp
from jax import lax
from jax.sharding import PartitionSpec as P

TILE = 128
BLK = 128


EXACT_MATMUL = lax.Precision.HIGHEST
SMALL_GUARD = 1e-06


def passed_along(array, axis, by):
    peers = lax.axis_size(axis)
    pairs = [(i, i + by) for i in range(peers) if 0 <= i + by < peers]
    return lax.ppermute(array, axis, pairs)


def unit_rows(vectors):
    return vectors * lax.rsqrt(jnp.sum(vectors * vectors, axis=-1, keepdims=True) + SMALL_GUARD)


def block_terms(queries, key_rows, values, beta_rate, decay_factor):
    hidden_feature_size = queries.shape[-2]
    per_group_channel_size = values.shape[-1]
    cumul = jnp.cumsum(decay_factor, axis=2)
    final = cumul[:, :, -1:, :]
    growth = jnp.exp(cumul)
    key_up = key_rows * growth
    key_down = key_rows * jnp.exp(-cumul)
    query_expansion = queries * growth
    final_key_position = key_rows * jnp.exp(final - cumul)
    row_pos = jnp.arange(hidden_feature_size)[:, None]
    col_pos = jnp.arange(hidden_feature_size)[None, :]
    strict = (row_pos > col_pos).astype(jnp.float32)
    inclusive = (row_pos >= col_pos).astype(jnp.float32)
    rising_low = key_up.astype(jnp.bfloat16)
    falling_low = key_down.astype(jnp.bfloat16)
    query_low = query_expansion.astype(jnp.bfloat16)
    mixing = (
        jnp.einsum("nhik,nhjk->nhij", rising_low, falling_low, preferred_element_type=jnp.float32)
        * strict
    )
    scores = (
        jnp.einsum("nhik,nhjk->nhij", query_low, falling_low, preferred_element_type=jnp.float32)
        * inclusive
    )
    system = jnp.eye(hidden_feature_size, dtype=jnp.float32) + beta_rate[..., None] * mixing
    target = beta_rate[..., None] * jnp.concatenate([values, key_up], axis=-1)
    solved = jax.scipy.linalg.solve_triangular(system, target, lower=True, unit_diagonal=True)
    return (
        query_expansion,
        scores,
        final_key_position,
        jnp.exp(final[:, :, 0, :]),
        solved[..., :per_group_channel_size],
        solved[..., per_group_channel_size:],
    )


def emit_block(recurrent_state, block):
    query_expansion, scores, final_key_position, retain_mask, first_weight, second_weight = block
    state_update = first_weight - jnp.einsum(
        "nrb,nbf->nrf", second_weight, recurrent_state, precision=EXACT_MATMUL
    )
    layer_output = jnp.einsum(
        "nrb,nbf->nrf", query_expansion, recurrent_state, precision=EXACT_MATMUL
    )
    layer_output = layer_output + jnp.einsum(
        "hcj,hjv->hcv", scores, state_update, precision=EXACT_MATMUL
    )
    recurrent_state = retain_mask[:, :, None] * recurrent_state + jnp.einsum(
        "nps,npo->nso", final_key_position, state_update, precision=EXACT_MATMUL
    )
    return (recurrent_state, layer_output)


def compose_block(combined_latent_pieces, block):
    query_expansion, scores, final_key_position, retain_mask, first_weight, second_weight = block
    per_group_channel_size = first_weight.shape[-1]
    fetched_tiles = jnp.einsum(
        "nrb,nbf->nrf", second_weight, combined_latent_pieces, precision=EXACT_MATMUL
    )
    combined_latent_pieces = retain_mask[:, :, None] * combined_latent_pieces - jnp.einsum(
        "nps,npo->nso", final_key_position, fetched_tiles, precision=EXACT_MATMUL
    )
    present_item_boost = jnp.einsum(
        "nps,npo->nso", final_key_position, first_weight, precision=EXACT_MATMUL
    )
    combined_latent_pieces = combined_latent_pieces.at[:, :, per_group_channel_size:].add(
        present_item_boost
    )
    return (combined_latent_pieces, None)


def body(
    tokens,
    query_weight,
    key_weight,
    values_projector_matrix,
    gate_weight,
    beta_weight,
    beta_bias,
    log_decay,
    head_gain,
    output_weight,
    kv_weight,
    kv_gain,
    owner,
):
    tile_rows = tokens.shape[0]
    head_width = query_weight.shape[1]
    local_heads = beta_weight.shape[1]
    per_group_channel_size = head_width // local_heads
    stacked = jnp.concatenate(
        [query_weight, key_weight, values_projector_matrix, gate_weight, beta_weight], axis=1
    )
    gathered = lax.all_gather(tokens, "tp", axis=0, tiled=True)
    projected = jnp.dot(gathered, stacked, preferred_element_type=jnp.float32)
    seq_rows = projected.shape[0]
    blocks = seq_rows // BLK

    def heads_of(array):
        return array.reshape(seq_rows, local_heads, per_group_channel_size)

    def split(array):
        return array.reshape(blocks, BLK, local_heads, per_group_channel_size).transpose(0, 2, 1, 3)

    queries = split(unit_rows(heads_of(projected[:, :head_width])))
    key_rows = split(unit_rows(heads_of(projected[:, head_width : 2 * head_width])))
    values = split(heads_of(projected[:, 2 * head_width : 3 * head_width]))
    gate_logit = heads_of(projected[:, 3 * head_width : 4 * head_width])
    beta_rate = jax.nn.sigmoid(projected[:, 4 * head_width :] + beta_bias)
    beta_rate = beta_rate.reshape(blocks, BLK, local_heads).transpose(0, 2, 1)
    decay_factor = split(log_decay)
    terms = block_terms(queries, key_rows, values, beta_rate, decay_factor)
    identity = jnp.broadcast_to(
        jnp.eye(per_group_channel_size, dtype=jnp.float32),
        (local_heads, per_group_channel_size, per_group_channel_size),
    )
    nothing = jnp.zeros((local_heads, per_group_channel_size, per_group_channel_size), jnp.float32)
    combined_latent_pieces, unused = lax.scan(
        compose_block, jnp.concatenate([identity, nothing], axis=-1), terms
    )
    carried_mapping = combined_latent_pieces[:, :, :per_group_channel_size]
    carried_addition = combined_latent_pieces[:, :, per_group_channel_size:]

    def relay(step, recurrent_state):
        departing_tiles = (
            jnp.einsum("lme,leo->lmo", carried_mapping, recurrent_state, precision=EXACT_MATMUL)
            + carried_addition
        )
        return passed_along(departing_tiles.astype(jnp.bfloat16), "ctx", 1).astype(
            departing_tiles.dtype
        )

    entering = lax.fori_loop(0, lax.axis_size("ctx") - 1, relay, nothing)
    unused_state, attended = lax.scan(emit_block, entering, terms)
    attended = attended.transpose(0, 2, 1, 3).reshape(seq_rows, local_heads, per_group_channel_size)
    scale = lax.rsqrt(jnp.mean(attended * attended, axis=-1, keepdims=True) + SMALL_GUARD)
    normed = (
        (attended * scale * head_gain * jax.nn.sigmoid(gate_logit))
        .reshape(seq_rows, head_width)
        .astype(jnp.bfloat16)
    )
    mixed = lax.psum_scatter(
        jnp.dot(normed, output_weight, preferred_element_type=jnp.float32).astype(jnp.bfloat16),
        "tp",
        scatter_dimension=0,
        tiled=True,
    )
    latent_width = kv_weight.shape[1]
    latent = jnp.dot(tokens, kv_weight, preferred_element_type=jnp.float32)
    latent = (
        latent
        * lax.rsqrt(jnp.mean(latent * latent, axis=-1, keepdims=True) + SMALL_GUARD)
        * kv_gain
    ).astype(jnp.bfloat16)
    local_tiles = tile_rows // TILE
    tiles_here = latent.reshape(local_tiles, TILE, latent_width)
    owner_col = owner.reshape(-1)
    count = owner_col.shape[0]
    same = owner_col[:, None] == owner_col[None, :]
    earlier = (
        jnp.arange(count, dtype=jnp.int32)[None, :] < jnp.arange(count, dtype=jnp.int32)[:, None]
    )
    rank = jnp.sum((same & earlier).astype(jnp.int32), axis=1)
    capacity = min(4, lax.axis_size("ctx") // 2) * local_tiles
    myself = lax.axis_index("ctx")
    slots = jnp.arange(capacity, dtype=jnp.int32)[:, None]
    picker_mask = ((owner_col[None, :] == myself) & (rank[None, :] == slots)).astype(jnp.bfloat16)
    cache = jnp.einsum(
        "si,iab->sab",
        picker_mask,
        lax.all_gather(tiles_here, "ctx", axis=0, tiled=True),
        preferred_element_type=jnp.float32,
    )
    return (mixed, cache.astype(jnp.bfloat16))


def solution(mesh):
    in_specs = (
        P(("ctx", "tp"), None),
        P(None, "tp"),
        P(None, "tp"),
        P(None, "tp"),
        P(None, "tp"),
        P(None, "tp"),
        P("tp"),
        P("ctx", "tp"),
        P(),
        P("tp", None),
        P(),
        P(),
        P(None, "tp"),
    )
    out_specs = (P(("ctx", "tp"), None), P("ctx", "tp", None))
    return jax.shard_map(body, mesh=mesh, in_specs=in_specs, out_specs=out_specs, check_vma=False)
```

profile of v0, /device:TPU:7, one launch (start us, length us, event | category | flops | bytes accessed | tf_op | source)
XLA Modules:
  0.0 849.2 jit_solution(14595642600143189636)
XLA Ops:
  11.3 3.3 reshape.171
  14.6 1.9 fusion.42
  21.6 2.6 constant_dynamic-update-slice_fusion.3
  27.5 46.6 %all-gather.4.cloned.1.call-done = bf16[2048,2304]{1,0:T(8,128)(2,1)} async-done(((bf16[128,2304]{1,0:T(8,128)(2,1)}), bf16[2048,2304]{1,0:T(8,128)(2,1)}) %all-gather.4.cloned.1.call-update) | async-done | bytes 9437200 | tf_op jit(solution)/shard_map/all_gather | solution.py:119
  74.1 15.5 %convolution_bitcast_fusion = f32[2048,1026]{0,1:T(8,128)S(1)} fusion(bf16[2304,1026]{1,0:T(8,128)(2,1)} %constant_dynamic-update-slice_fusion, bf16[2048,2304]{1,0:T(8,128)(2,1)} %all-gather.4.cloned.1.call-done), kind=kOutput, calls=%fused_computation.43 | convolution fusion | flops 9682550784 | bytes 22569984 | tf_op jit(solution)/shard_map/dot_general | solution.py:120
  89.6 2.7 slice_bitcast_fusion.1
  92.3 1.9 copy-done.2
  96.4 3.4 copy.85
  99.9 3.3 copy.110
  103.2 3.4 copy.96
  106.7 5.8 fusion.71
  112.5 3.0 copy.94
  115.5 3.3 copy.109
  118.8 3.6 copy.90
  123.5 4.1 add_bitcast_fusion
  127.6 315.8 %custom-call.4 = f32[16,2,1,128,128]{3,4,2,1,0:T(8,128)} custom-call(f32[16,2,1,128,128]{4,3,2,1,0:T(8,128)} %add_bitcast_fusion), custom_call_target="InvertDiagBlocksLowerTriangular" | custom-call | tf_op jit(solution)/shard_map/jit(_solve_triangular)/vmap(vmap())/triangular_solve | solution.py:51
  443.4 2.7 maximum_multiply_fusion
  446.3 6.4 fusion.32
  452.7 2.5 fusion.72
  455.2 72.0 %while.39 = (s32[]{:T(128)}, f32[2,128,256]{2,1,0:T(8,128)S(1)}, f32[16,2,128]{2,1,0:T(2,128)}, f32[16,2,128,128]{2,3,1,0:T(8,128)}, f32[16,2,128,128]{3,2,1,0:T(8,128)}, /*index=5*/f32[16,2,128,128]{3,2,1,0:T(8,128)}) while((s32[]{:T(128)}, f32[2,128,256]{2,1,0:T(8,128)S(1)}, f32[16,2,128]{2,1,0:T(2,128)}, ...), condition=%wide.region_3.4_spmd.clone, body=%wide.region_2.0_spmd.sunk.clone | while | flops 251822080 | bytes 2101337 | solution.py:143
  527.2 2.6 convolution_multiply_fusion
  529.8 112.4 %while.41 = (s32[]{:T(128)}, f32[2,128,128]{2,1,0:T(8,128)S(1)}, f32[2,128,128]{2,1,0:T(8,128)S(1)}, f32[2,128,128]{2,1,0:T(8,128)S(1)}) while((s32[]{:T(128)}, f32[2,128,128]{2,1,0:T(8,128)S(1)}, f32[2,128,128]{2,1,0:T(8,128)S(1)}, f32[2,128,128]{2,1,0:T(8,128)S(1)}) %tuple.103), condition=%wide.region_5.6_spmd.clone.clone, body=%wide.region_4.5_spmd.clone.sunk.clone | while | flops 50462720 | bytes 917607 | solution.py:158
  530.1 3.1 collective-permute-start
  533.2 4.4 collective-permute-done
  537.9 1.9 collective-permute-start
  539.8 5.2 collective-permute-done
  545.3 1.9 collective-permute-start
  547.2 5.2 collective-permute-done
  552.7 1.9 collective-permute-start
  554.7 5.2 collective-permute-done
  560.2 1.9 collective-permute-start
  562.1 5.2 collective-permute-done
  567.6 1.9 collective-permute-start
  569.5 5.2 collective-permute-done
  575.0 1.9 collective-permute-start
  577.0 5.2 collective-permute-done
  582.5 1.9 collective-permute-start
  584.4 5.8 collective-permute-done
  590.5 1.9 collective-permute-start
  592.5 5.2 collective-permute-done
  598.0 1.9 collective-permute-start
  599.9 5.2 collective-permute-done
  605.4 1.9 collective-permute-start
  607.3 5.2 collective-permute-done
  612.8 1.9 collective-permute-start
  614.8 5.2 collective-permute-done
  620.3 1.9 collective-permute-start
  622.2 5.2 collective-permute-done
  627.7 1.9 collective-permute-start
  629.6 5.2 collective-permute-done
  635.1 1.9 collective-permute-start
  637.0 5.2 collective-permute-done
  642.3 104.3 %while.40 = (s32[]{:T(128)}, f32[2,128,128]{2,1,0:T(8,128)S(1)}, f32[16,2,128,128]{3,2,1,0:T(8,128)}, f32[16,2,128]{2,1,0:T(2,128)}, f32[16,2,128,128]{2,3,1,0:T...) while((s32[]{:T(128)}, f32[2,128,128]{2,1,0:T(8,128)S(1)}, ...), condition=%wide.region_8.9_spmd.clone, body=%wide.region_7.8_spmd.sunk.clone | while | flops 201457664 | bytes 2233457 | solution.py:159
  673.0 1.8 fusion.149
  686.1 1.8 fusion.149
  692.6 1.8 fusion.149
  705.6 1.8 fusion.149
  718.6 1.8 fusion.149
  731.7 1.8 fusion.149
  746.5 3.2 copy.102
  751.4 3.0 fusion.36
  754.4 5.1 convolution_convert_fusion
  760.4 2.9 fusion.47
  764.2 78.5 %reduce-scatter.2.cloned.1.call-done = bf16[128,2304]{1,0:T(8,128)(2,1)} async-done(((bf16[2048,2304]{1,0:T(8,128)(2,1)}), bf16[128,2304]{1,0:T(8,128)(2,1)}) %reduce-scatter.2.cloned.1.call-update) | async-done | bytes 589840 | tf_op jit(solution)/shard_map/reduce_scatter | solution.py:167
  (267 shorter events, 187.9 us)
Async XLA Ops:
  7.2 1.7 copy-start
  7.2 3.3 copy-start.17
  7.2 66.9 %all-gather.4.cloned.1.call-start = ((), (), s32[]{:S(2)}) async-start(), calls=%async_computation.1 | async-start | bytes 10027008 | tf_op jit(solution)/shard_map/all_gather | solution.py:119
  7.9 752.5 %all-gather.6.cloned.1.call-start = ((), (), s32[]{:S(2)}) async-start(), calls=%async_computation.3 | async-start | bytes 2228224 | tf_op jit(solution)/shard_map/all_gather | solution.py:196
  11.3 831.5 %reduce-scatter.2.cloned.1.call-start = ((), (), s32[]{:S(2)}) async-start(), calls=%async_computation.2 | async-start | bytes 10027008 | tf_op jit(solution)/shard_map/reduce_scatter | solution.py:167
  14.6 4.5 copy-start.8
  16.4 4.2 copy-start.3
  16.4 3.8 copy-start.16
  16.5 4.2 copy-start.19
  20.6 3.6 copy-start.9
  21.6 3.7 copy-start.10
  89.6 4.6 copy-start.2
  118.8 3.6 copy-start.18
  118.8 4.7 copy-start.12
  118.8 4.7 copy-start.13
  118.8 4.7 copy-start.14
  118.8 4.7 copy-start.15
  443.4 2.9 copy-start.6
  455.2 72.0 %copy-start.11 = (f32[128,128]{1,0:T(8,128)S(1)}, f32[128,128]{1,0:T(8,128)}, u32[]{:S(2)}) copy-start(f32[128,128]{1,0:T(8,128)} %fusion.57) | copy-start | bytes 196612
  530.1 7.5 collective-permute-start
  537.9 7.1 collective-permute-start
  545.3 7.1 collective-permute-start
  552.7 7.1 collective-permute-start
  560.2 7.1 collective-permute-start
  567.6 7.1 collective-permute-start
  575.0 7.1 collective-permute-start
  582.5 7.8 collective-permute-start
  590.5 7.1 collective-permute-start
  598.0 7.1 collective-permute-start
  605.4 7.1 collective-permute-start
  612.8 7.1 collective-permute-start
  620.3 7.1 collective-permute-start
  627.7 7.1 collective-permute-start
  635.1 7.1 collective-permute-start
  746.5 3.2 copy-start.4
  749.8 1.6 copy-start.5
  751.3 3.0 copy-start.7
  759.5 0.7 copy-start.20
  759.6 83.1 %copy-start.1 = (bf16[2304,512]{1,0:T(8,128)(2,1)S(1)}, bf16[2304,512]{1,0:T(8,128)(2,1)}, u32[]{:S(2)}) copy-start(bf16[2304,512]{1,0:T(8,128)(2,1)} %param.31) | copy-start | bytes 7077892
Sparse Core Ops, SparseCore 0:
  9.9 64.1 all-gather.3
  77.1 46.9 all-gather.5
  759.7 82.9 reduce-scatter.1
where the time goes:
time: 856 us; the launch traced here: 849 us
  other arithmetic  334 us (39%)
  waiting for transfers between devices  204 us (24%)
  matrix products  175 us (20%)
  local copies, waits for them, and re-layouts  90.2 us (11%)
  starting transfers between devices  30.1 us (4%)
  between operations  14.1 us (2%)
    another operation x4, other arithmetic, block_terms(): jax.scipy.linalg.solve_triangular(system, target, lower=True, unit_diagon...  317 us
    reduce_scatter x1, waiting for transfers between devices, body(): lax.psum_scatter(jnp.dot(normed, output_weight, preferred_element_type=jn...  78.5 us
    ppermute x15, waiting for transfers between devices, passed_along(): return lax.ppermute(array, axis, pairs)  77.7 us
    all_gather x1, waiting for transfers between devices, body(): gathered = lax.all_gather(tokens, 'tp', axis=0, tiled=True)  46.6 us
    ppermute x15, starting transfers between devices, passed_along(): return lax.ppermute(array, axis, pairs)  30 us
    dot_general x16, matrix products, emit_block(): jnp.einsum('hcj,hjv->hcv', scores, state_update, precision=EXACT_MATMUL)  29.3 us
    unnamed x54, local copies, waits for them, and re-layouts  22.8 us
    dynamic_slice x16, local copies, waits for them, and re-layouts, body(): lax.scan(compose_block, jnp.concatenate([identity, nothing], axis=-1), te...  21.1 us
  transfers between devices with their start and end apart: 18, of which 17 were waited for; matrix products, arithmetic and copies ran while one was open for 70% of the time, Pallas kernels for 0%

commit v1 on v0

v1 whole, which is shorter than its diff:
```python
import functools
import jax
import jax.numpy as jnp
from jax import lax
from jax.experimental import pallas as pl
from jax.experimental.pallas import tpu as pltpu
from jax.sharding import PartitionSpec as P

BLK = 128
GUARD = 1e-06
BF = jnp.bfloat16
F32 = jnp.float32
VMEM_BYTES = 48 * 1024 * 1024


def dot(a, b, contract=((1,), (0,))):
    return lax.dot_general(a, b, (contract, ((), ())), preferred_element_type=F32)


def halves(a):
    high = a.astype(BF)
    return high, (a - high.astype(F32)).astype(BF)


def wide_left(a):
    return jnp.concatenate(halves(a), axis=1)


def wide_right(b):
    row = jnp.concatenate(halves(b), axis=1)
    return jnp.concatenate([row, row], axis=0)


def wide_dot(left, right):
    both = dot(left, right)
    n = both.shape[1] // 2
    return both[:, :n] + both[:, n:]


def indices(shape):
    return lax.broadcasted_iota(jnp.int32, shape, 0), lax.broadcasted_iota(jnp.int32, shape, 1)


def inverses(systems, row, col, exact):
    eye = (row == col).astype(F32)
    joins = (row // 2 == col // 2) & (row > col)
    out = [eye - jnp.where(joins, s, 0.0) for s in systems]
    size = 2
    while size < BLK:
        joins = (row // (2 * size) == col // (2 * size)) & (row // size > col // size)
        parts = [jnp.where(joins, s, 0.0) for s in systems]
        if exact:
            lefts = [wide_left(t) for t in out]
            rights = [wide_right(t) for t in out]
            inner = [wide_dot(wide_left(p), r) for p, r in zip(parts, rights)]
            out = [t - wide_dot(l, wide_right(x)) for t, l, x in zip(out, lefts, inner)]
        else:
            low = [t.astype(BF) for t in out]
            inner = [dot(p.astype(BF), t).astype(BF) for p, t in zip(parts, low)]
            out = [t - dot(l, x) for t, l, x in zip(out, low, inner)]
        size *= 2
    if not exact:
        rest = [-wide_dot(wide_left(s), wide_right(t)) for s, t in zip(systems, out)]
        rest = [(eye - t) + r for t, r in zip(out, rest)]
        out = [t + dot(t.astype(BF), r.astype(BF)) for t, r in zip(out, rest)]
    return out


def terms_kernel(group, at_once, exact, tok, ld, wq, wk, wv, wb, bias, ab_out, po_out, proj, rate):
    rows = tok[...]
    proj[0] = dot(rows, wq[...])
    proj[1] = dot(rows, wk[...])
    proj[2] = dot(rows, wv[...])
    rate[...] = jax.nn.sigmoid(dot(rows, wb[...]) + bias[...])
    row, col = indices((BLK, BLK))
    ones = (row >= col).astype(BF)
    ones2 = jnp.concatenate([ones, ones], axis=1)

    def some(step, carry):
        pairs, wide = [], []
        for j in range(at_once):
            blk = step * at_once + j
            at = pl.ds(pl.multiple_of(blk * BLK, BLK), BLK)
            decay = ld[at, :]
            high = decay.astype(BF)
            rest = decay - high.astype(F32)
            mid = rest.astype(BF)
            low = (rest - mid.astype(F32)).astype(BF)
            cum = dot(ones2, jnp.concatenate([high, mid], axis=0)) + dot(ones, low)
            for h in range(2):
                lanes = slice(h * BLK, (h + 1) * BLK)
                pairs.append((blk, at, h, lanes, cum[:, lanes]))
        systems, targets, scores, ends, firsts, finals = [], [], [], [], [], []
        for blk, at, h, lanes, c in pairs:
            q = proj[0, at, lanes]
            k = proj[1, at, lanes]
            v = proj[2, at, lanes]
            q = q * lax.rsqrt(jnp.sum(q * q, axis=-1, keepdims=True) + GUARD)
            k = k * lax.rsqrt(jnp.sum(k * k, axis=-1, keepdims=True) + GUARD)
            beta = rate[at, h : h + 1]
            final = c[BLK - 1 : BLK, :]
            grow = jnp.exp(c)
            k_up = k * grow
            q_up = q * grow
            k_down = (k * jnp.exp(-c)).astype(BF)
            k_end = k * jnp.exp(final - c)
            gram = dot(jnp.concatenate([k_up, q_up], axis=0).astype(BF), k_down, ((1,), (1,)))
            systems.append(jnp.where(row > col, beta * gram[:BLK], 0.0))
            scores.append(jnp.where(row >= col, gram[BLK:], 0.0).astype(BF))
            targets.append(jnp.concatenate([(beta * k_up).astype(BF), (beta * v).astype(BF)], axis=1))
            ends.append(k_end.T.astype(BF))
            firsts.append(q_up)
            finals.append(jnp.exp(final))
        solved = inverses(systems, row, col, exact)
        solved = [dot(t.astype(BF), g).astype(BF) for t, g in zip(solved, targets)]
        for (blk, at, h, lanes, c), w, s, e, f, last in zip(pairs, solved, scores, ends, firsts, finals):
            both = dot(jnp.concatenate([s, e], axis=0), w)
            po_out[blk, h, :, :BLK] = f - both[:BLK, :BLK]
            po_out[blk, h, :, BLK:] = both[:BLK, BLK:]
            ab_out[blk, h, :, :BLK] = jnp.where(row == col, last, 0.0) - both[BLK:, :BLK]
            ab_out[blk, h, :, BLK:] = both[BLK:, BLK:]
        return carry

    if group == at_once:
        some(0, 0)
    else:
        lax.fori_loop(0, group // at_once, some, 0)


def block_terms(tokens, ld, wq, wk, wv, wb, bias, group=4, at_once=2, exact=True):
    rows, width = tokens.shape
    blocks = rows // BLK
    lanes = wq.shape[1]
    whole = lambda a: pl.BlockSpec(a.shape, lambda i: (0,) * a.ndim)
    out = jax.ShapeDtypeStruct((blocks, 2, BLK, 2 * BLK), F32)
    out_spec = pl.BlockSpec((group, 2, BLK, 2 * BLK), lambda i: (i, 0, 0, 0))
    return pl.pallas_call(
        functools.partial(terms_kernel, group, at_once, exact),
        grid=(blocks // group,),
        in_specs=[
            pl.BlockSpec((group * BLK, width), lambda i: (i, 0)),
            pl.BlockSpec((group * BLK, lanes), lambda i: (i, 0)),
            whole(wq), whole(wk), whole(wv), whole(wb), whole(bias),
        ],
        out_specs=[out_spec, out_spec],
        out_shape=[out, out],
        scratch_shapes=[pltpu.VMEM((3, group * BLK, lanes), F32), pltpu.VMEM((group * BLK, BLK), F32)],
        compiler_params=pltpu.CompilerParams(vmem_limit_bytes=VMEM_BYTES),
        name="block_terms",
    )(tokens, ld, wq, wk, wv, wb, bias)


def narrow_left(a):
    high, low = halves(a)
    return jnp.concatenate([high, low], axis=1), high


def compose(a, x):
    left, high = narrow_left(a)
    x_high, x_low = halves(x)
    return dot(left, jnp.concatenate([x_high, x_high], axis=0)) + dot(high, x_low)


def chain_kernel(group, ab, po, z_out, y_out, x_out, held):
    step = pl.program_id(0)
    row, col = indices((BLK, 2 * BLK))

    @pl.when(step == 0)
    def start():
        for h in range(2):
            held[h] = (row == col).astype(F32)

    x = [held[h] for h in range(2)]
    for j in range(group):
        at = slice(j * BLK, (j + 1) * BLK)
        for h in range(2):
            lanes = slice(h * BLK, (h + 1) * BLK)
            both = dot(po[j, h, :, :BLK].astype(BF), x[h].astype(BF))
            z_out[at, lanes] = both[:, :BLK].astype(BF)
            y_out[at, lanes] = both[:, BLK:] + po[j, h, :, BLK:]
            moved = compose(ab[j, h, :, :BLK], x[h])
            x[h] = jnp.concatenate([moved[:, :BLK], moved[:, BLK:] + ab[j, h, :, BLK:]], axis=1)
    for h in range(2):
        held[h] = x[h]
        x_out[h] = x[h]


def chain(ab, po, group=4):
    blocks = ab.shape[0]
    spec = pl.BlockSpec((group, 2, BLK, 2 * BLK), lambda i: (i, 0, 0, 0))
    rows = pl.BlockSpec((group * BLK, 2 * BLK), lambda i: (i, 0))
    return pl.pallas_call(
        functools.partial(chain_kernel, group),
        grid=(blocks // group,),
        in_specs=[spec, spec],
        out_specs=[rows, rows, pl.BlockSpec((2, BLK, 2 * BLK), lambda i: (0, 0, 0))],
        out_shape=[
            jax.ShapeDtypeStruct((blocks * BLK, 2 * BLK), BF),
            jax.ShapeDtypeStruct((blocks * BLK, 2 * BLK), F32),
            jax.ShapeDtypeStruct((2, BLK, 2 * BLK), F32),
        ],
        scratch_shapes=[pltpu.VMEM((2, BLK, 2 * BLK), F32)],
        compiler_params=pltpu.CompilerParams(vmem_limit_bytes=VMEM_BYTES),
        name="chain",
    )(ab, po)


def side_kernel(place, own, one, two, three, before, total, slots):
    me = place[0]
    for h in range(2):
        slots[0, h] = own[h]
        for d, got in enumerate((one, two, three)):
            slots[d + 1, h] = got[h].astype(F32)
    row, col = indices((BLK, 2 * BLK))
    maps = [None, None]
    for j in range(4):

        @pl.when(me == j)
        def keep():
            for h in range(2):
                before[h] = (row == col).astype(F32) if j == 0 else maps[h]

        at = (me + 4 - j) % 4
        for h in range(2):
            if j == 0:
                maps[h] = slots[at, h]
            else:
                moved = compose(slots[at, h, :, :BLK], maps[h])
                maps[h] = jnp.concatenate(
                    [moved[:, :BLK], moved[:, BLK:] + slots[at, h, :, BLK:]], axis=1
                )
    for h in range(2):
        total[h] = maps[h].astype(BF)


def side_maps(place, own, received):
    whole = pl.BlockSpec(memory_space=pltpu.VMEM)
    return pl.pallas_call(
        side_kernel,
        in_specs=[pl.BlockSpec(memory_space=pltpu.SMEM)] + [whole] * 4,
        out_specs=[whole, whole],
        out_shape=[jax.ShapeDtypeStruct(own.shape, F32), jax.ShapeDtypeStruct(own.shape, BF)],
        scratch_shapes=[pltpu.VMEM((4,) + own.shape, F32)],
        compiler_params=pltpu.CompilerParams(vmem_limit_bytes=VMEM_BYTES),
        name="side_maps",
    )(place, own, *received)


def emit_kernel(place, before, own, one, two, three, z, y, gate, gain, out, slots, state):
    me = place[0]

    @pl.when(pl.program_id(0) == 0)
    def enter():
        for d, got in enumerate((own, one, two, three)):
            slots[d] = got[...]
        for h in range(2):
            s = jnp.zeros((BLK, BLK), F32)
            for j in range(3):
                at = (me + 4 - j) % 4
                moved = slots[at, h, :, BLK:].astype(F32)
                if j > 0:
                    moved = moved + compose(slots[at, h, :, :BLK].astype(F32), s)
                s = jnp.where(j < me, moved, s)
            s = compose(before[h, :, :BLK], s) + before[h, :, BLK:]
            state[h] = s.astype(BF)

    for h in range(2):
        lanes = slice(h * BLK, (h + 1) * BLK)
        a = y[:, lanes] + dot(z[:, lanes], state[h])
        scale = lax.rsqrt(jnp.mean(a * a, axis=-1, keepdims=True) + GUARD)
        a = a * scale * gain[...] * jax.nn.sigmoid(gate[:, lanes].astype(F32))
        out[:, lanes] = a.astype(BF)


def emit(place, before, own, received, z, y, gate, gain, rows=512):
    small = pl.BlockSpec(own.shape, lambda i: (0, 0, 0))
    tall = pl.BlockSpec((rows, 2 * BLK), lambda i: (i, 0))
    return pl.pallas_call(
        emit_kernel,
        grid=(z.shape[0] // rows,),
        in_specs=[pl.BlockSpec(memory_space=pltpu.SMEM)]
        + [small] * 5
        + [tall] * 3
        + [pl.BlockSpec((1, BLK), lambda i: (0, 0))],
        out_specs=tall,
        out_shape=jax.ShapeDtypeStruct(z.shape, BF),
        scratch_shapes=[pltpu.VMEM((4,) + own.shape, BF), pltpu.VMEM((2, BLK, BLK), BF)],
        compiler_params=pltpu.CompilerParams(vmem_limit_bytes=VMEM_BYTES),
        name="emit",
    )(place, before, own, *received, z, y, gate, gain)


def turn(array, axis, pairs):
    return lax.ppermute(array, axis, pairs)


def along_y(d):
    return [(4 * x + y, 4 * x + (y + d) % 4) for x in range(4) for y in range(4)]


def along_x(d):
    return [(4 * x + y, 4 * ((x + d) % 4) + y) for x in range(4) for y in range(4)]


def latent_part(tokens, kv_weight, kv_gain, owner):
    latent = dot(tokens, kv_weight)
    latent = (
        latent * lax.rsqrt(jnp.mean(latent * latent, axis=-1, keepdims=True) + GUARD) * kv_gain
    ).astype(BF)
    owners = owner.reshape(-1)
    count = owners.shape[0]
    order = jnp.arange(count, dtype=jnp.int32)
    same = owners[:, None] == owners[None, :]
    rank = jnp.sum((same & (order[None, :] < order[:, None])).astype(jnp.int32), axis=1)
    slots = jnp.arange(4, dtype=jnp.int32)[:, None]
    picks = ((owners[None, :] == lax.axis_index("ctx")) & (rank[None, :] == slots)).astype(BF)
    tiles = lax.all_gather(latent[None], "ctx", axis=0, tiled=True)
    return jnp.einsum("si,iab->sab", picks, tiles, preferred_element_type=F32).astype(BF)


def body(
    tokens,
    query_weight,
    key_weight,
    values_projector_matrix,
    gate_weight,
    beta_weight,
    beta_bias,
    log_decay,
    head_gain,
    output_weight,
    kv_weight,
    kv_gain,
    owner,
):
    spare = BLK - beta_weight.shape[1]
    rate_weight = jnp.pad(beta_weight, ((0, 0), (0, spare)))
    rate_bias = jnp.pad(beta_bias, (0, spare))[None]
    gathered = lax.all_gather(tokens, "tp", axis=0, tiled=True)
    ab, po = block_terms(
        gathered, log_decay, query_weight, key_weight, values_projector_matrix, rate_weight, rate_bias,
        group=4, at_once=4,
    )
    z, y, maps = chain(ab, po)
    low = maps.astype(BF)
    ctx = lax.axis_index("ctx").astype(jnp.int32)
    received = [turn(low, "ctx", along_y(d)) for d in (1, 2, 3)]
    before, total = side_maps((ctx % 4)[None], maps, received)
    received = [turn(total, "ctx", along_x(d)) for d in (1, 2, 3)]
    gate = dot(gathered, gate_weight).astype(BF)
    normed = emit((ctx // 4)[None], before, total, received, z, y, gate, head_gain[None])
    mixed = lax.psum_scatter(
        dot(normed, output_weight).astype(BF), "tp", scatter_dimension=0, tiled=True
    )
    return mixed, latent_part(tokens, kv_weight, kv_gain, owner)


def solution(mesh):
    in_specs = (
        P(("ctx", "tp"), None),
        P(None, "tp"),
        P(None, "tp"),
        P(None, "tp"),
        P(None, "tp"),
        P(None, "tp"),
        P("tp"),
        P("ctx", "tp"),
        P(),
        P("tp", None),
        P(),
        P(),
        P(None, "tp"),
    )
    out_specs = (P(("ctx", "tp"), None), P("ctx", "tp", None))
    return jax.shard_map(body, mesh=mesh, in_specs=in_specs, out_specs=out_specs, check_vma=False)
```

time: 856 us -> 227 us (0.27)
  other arithmetic: 334 us -> 1.61 us
  matrix products: 175 us -> 16.2 us
  local copies, waits for them, and re-layouts: 90.2 us -> 9.66 us
  waiting for transfers between devices: 204 us -> 138 us
  Pallas kernels: 0 us -> 37.7 us
  starting transfers between devices: 30.1 us -> 7.04 us
    another operation x5 -> x0, other arithmetic: 318 us -> none  [the longest x4 317 us: block_terms(): jax.scipy.linalg.solve_triangular(system, target, lower=True, unit_diagon...]
    dot_general x133 -> x4, matrix products: 169 us -> 16.2 us  [the longest x3 13.3 us: dot(): lax.dot_general(a, b, (contract, ((), ())), preferred_element_type=F32)]
    ppermute x15 -> x6, waiting for transfers between devices: 77.7 us -> 10.7 us  [turn(): return lax.ppermute(array, axis, pairs)]
    pallas_call x0 -> x4, Pallas kernels: none -> 37.7 us  [the longest x1 27.3 us: block_terms(): pl.pallas_call(functools.partial(terms_kernel, group, at_once, exact), gr...]
    ppermute x15 -> x6, starting transfers between devices: 30 us -> 6.92 us  [turn(): return lax.ppermute(array, axis, pairs)]
    mul x33 -> x0, local copies, waits for them, and re-layouts: 21.1 us -> none  [the longest x16 10.5 us: compose_block(): retain_mask[:, :, None] * combined_latent_pieces]
    dynamic_slice x16 -> x0, local copies, waits for them, and re-layouts: 21.1 us -> none  [body(): lax.scan(compose_block, jnp.concatenate([identity, nothing], axis=-1), te...]
    all_gather x1, waiting for transfers between devices: 46.6 us -> 62.2 us  [body(): gathered = lax.all_gather(tokens, 'tp', axis=0, tiled=True)]
  transfers between devices with their start and end apart: 18 -> 9, of which waited for: 17 -> 5; matrix products, arithmetic and copies ran while one was open for 70% -> 9% of each run, Pallas kernels for 0% -> 17%
where the time goes in v1:
time: 227 us; the launch traced here: 224 us
  waiting for transfers between devices  138 us (61%)
  Pallas kernels  37.7 us (17%)
  matrix products  16.2 us (7%)
  between operations  14 us (6%)
  local copies, waits for them, and re-layouts  9.66 us (4%)
  starting transfers between devices  7.04 us (3%)
    reduce_scatter x1, waiting for transfers between devices, body(): lax.psum_scatter(dot(normed, output_weight).astype(BF), 'tp', scatter_dim...  64.5 us
    all_gather x1, waiting for transfers between devices, body(): gathered = lax.all_gather(tokens, 'tp', axis=0, tiled=True)  62.2 us
    pallas_call x1, Pallas kernels, block_terms(): pl.pallas_call(functools.partial(terms_kernel, group, at_once, exact), gr...  27.3 us
    dot_general x3, matrix products, dot(): lax.dot_general(a, b, (contract, ((), ())), preferred_element_type=F32)  13.3 us
    ppermute x6, waiting for transfers between devices, turn(): return lax.ppermute(array, axis, pairs)  10.7 us
    unnamed x30, local copies, waits for them, and re-layouts  9.53 us
    ppermute x6, starting transfers between devices, turn(): return lax.ppermute(array, axis, pairs)  6.92 us
    pallas_call x1, Pallas kernels, chain(): pl.pallas_call(functools.partial(chain_kernel, group), grid=(blocks // gr...  6.2 us
  transfers between devices with their start and end apart: 9, of which 5 were waited for; matrix products, arithmetic and copies ran while one was open for 9% of the time, Pallas kernels for 17%

profile of v1, /device:TPU:7, one launch (start us, length us, event | category | flops | bytes accessed | tf_op | source)
XLA Modules:
  0.0 224.2 jit_solution(16545454703580948554)
XLA Ops:
  7.2 0.0 copy-start
  7.2 0.0 copy-start.11
  7.2 0.0 copy-start.10
  7.2 0.0 all-gather.4.cloned.1.call-start
  7.2 0.7 all-gather.4.cloned.1.call-update
  7.9 0.0 copy-start.12
  7.9 0.0 all-gather.6.cloned.1.call-start
  8.0 0.8 copy-done
  8.8 1.6 multiply_reduce_fusion
  10.5 0.0 copy-done.11
  10.5 0.7 multiply_convert_fusion
  11.2 0.0 all-gather.6.cloned.1.call-update
  11.2 0.0 reduce-scatter.2.cloned.1.call-start
  11.3 0.0 copy-done.10
  11.3 0.4 copy.18
  11.7 0.1 pad.8.wb
  11.8 0.0 copy-done.12
  11.8 62.2 %all-gather.4.cloned.1.call-done.tok = bf16[2048,2304]{1,0:T(8,128)(2,1)} async-done(((bf16[128,2304]{1,0:T(8,128)(2,1)}), bf16[2048,2304]{1,0:T(8,128)(2,1)}) %all-gather.4.cloned.1.call-update) | async-done | bytes 9437200 | tf_op jit(solution)/shard_map/all_gather | solution.py:339
  74.1 0.0 copy-start.3
  74.1 1.3 copy-done.3
  75.3 0.0 copy-start.4
  75.3 1.3 copy-done.4
  76.6 0.0 copy-start.5
  76.6 1.3 copy-done.5
  77.9 27.3 %block_terms.1 = (f32[16,2,128,256]{3,2,1,0:T(8,128)}, f32[16,2,128,256]{3,2,1,0:T(8,128)}) custom-call(bf16[2048,2304]{1,0:T(8,128)(2,1)} %all-gather.4.cloned.1.call-done.tok, f32[2048,256]{1,0:T(8,128)} %ld.1, bf16[2304,256]{1,0:T(8,128)(2,1)S(1)} %copy-done.3, bf16[2304,256]{1,0:T(8,128)(2,1)S(1)} %copy-done.4, bf16[2304,256]{1,0:T(8,128)(2,1)S(1)} %copy-done.5, ...), custom_call_target="tpu_custom_call" | custom-call | tf_op jit(solution)/shard_map/block_terms/pallas_call | solution.py:137
  105.2 6.2 %chain.1 = (bf16[2048,256]{1,0:T(8,128)(2,1)S(1)}, f32[2048,256]{1,0:T(8,128)S(1)}, f32[2,128,256]{2,1,0:T(8,128)S(1)}) custom-call(f32[16,2,128,256]{3,2,1,0:T(8,128)} %get-tuple-element.9.ab, f32[16,2,128,256]{3,2,1,0:T(8,128)} %get-tuple-element.10.po), custom_call_target="tpu_custom_call" | custom-call | tf_op jit(solution)/shard_map/chain/pallas_call | solution.py:192
  111.4 0.0 copy-start.1
  111.4 1.3 copy-done.1
  112.7 0.7 convert_element_type.23
  113.4 0.0 copy-start.6
  113.4 0.7 copy-done.6
  114.1 2.5 %collective-permute-start.2 = (bf16[2,128,256]{2,1,0:T(8,128)(2,1)}, bf16[2,128,256]{2,1,0:T(8,128)(2,1)S(1)}, u32[]{:S(2)}, u32[]{:S(2)}) collective-permute-start(bf16[2,128,256]{2,1,0:T(8,128)(2,1)} %convert_element_type.23), channel_id=1, source_target_pairs={{0,48},{16,0},{32,16},{48,32},{64,112},{80,64},{96,80},{112,96},{1... | collective-permute-start | bytes 393224 | tf_op jit(solution)/shard_map/ppermute | solution.py:294
  116.5 0.5 collective-permute-start.1
  117.0 0.6 collective-permute-start
  117.7 4.7 %collective-permute-done.2.three = bf16[2,128,256]{2,1,0:T(8,128)(2,1)S(1)} collective-permute-done((bf16[2,128,256]{2,1,0:T(8,128)(2,1)}, bf16[2,128,256]{2,1,0:T(8,128)(2,1)S(1)}, u32[]{:S(2)}, u32[]{:S(2)}) %collective-permute-start.2) | collective-permute-done | bytes 131104 | tf_op jit(solution)/shard_map/ppermute | solution.py:294
  122.3 2.7 %collective-permute-done.1.two = bf16[2,128,256]{2,1,0:T(8,128)(2,1)} collective-permute-done((bf16[2,128,256]{2,1,0:T(8,128)(2,1)}, bf16[2,128,256]{2,1,0:T(8,128)(2,1)}, u32[]{:S(2)}, u32[]{:S(2)}) %collective-permute-start.1) | collective-permute-done | bytes 131104 | tf_op jit(solution)/shard_map/ppermute | solution.py:294
  125.0 3.3 %collective-permute-done.one = bf16[2,128,256]{2,1,0:T(8,128)(2,1)} collective-permute-done((bf16[2,128,256]{2,1,0:T(8,128)(2,1)}, bf16[2,128,256]{2,1,0:T(8,128)(2,1)}, u32[]{:S(2)}, u32[]{:S(2)}) %collective-permute-start) | collective-permute-done | bytes 131104 | tf_op jit(solution)/shard_map/ppermute | solution.py:294
  128.3 0.0 copy-start.7
  128.3 0.9 copy-done.7
  129.3 1.8 side_maps.1
  131.1 0.0 copy-start.2
  131.1 0.0 copy-start.8
  131.1 0.6 collective-permute-start.5
  131.7 1.1 collective-permute-start.4
  132.8 1.6 collective-permute-start.3
  134.4 6.6 %convolution_convert_fusion.1.gate = bf16[2048,256]{1,0:T(8,128)(2,1)S(1)} fusion(bf16[2048,2304]{1,0:T(8,128)(2,1)} %all-gather.4.cloned.1.call-done.tok, bf16[2304,256]{1,0:T(8,128)(2,1)} %param.17), kind=kOutput, calls=%fused_computation.1 | convolution fusion | flops 2416443392 | bytes 11665408 | tf_op jit(solution)/shard_map/dot_general | solution.py:17
  141.0 0.0 collective-permute-done.5.three
  141.0 0.0 collective-permute-done.4.two
  141.0 0.0 collective-permute-done.3.one
  141.0 0.0 copy-done.2
  141.0 0.0 copy-done.8
  141.0 0.0 copy-start.9
  141.1 2.4 %emit.1 = bf16[2048,256]{1,0:T(8,128)(2,1)S(1)} custom-call(s32[1]{0:T(128)} %bitcast.place, f32[2,128,256]{2,1,0:T(8,128)S(1)} %get-tuple-element.12.before, bf16[2,128,256]{2,1,0:T(8,128)(2,1)S(1)} %get-tuple-element.13.own, bf16[2,128,256]{2,1,0:T(8,128)(2,1)S(1)} %collective-permute-done.3.one, bf16[2,128,256]{2,1,0:T(8,128)(2,1)S(1)} %collective-permute-done.4.two, ...), custom_call_target="tpu_custom_call" | custom-call | tf_op jit(solution)/shard_map/emit/pallas_call | solution.py:278
  143.5 0.0 copy-done.9
  143.5 5.1 %convolution_convert_fusion = bf16[2048,2304]{1,0:T(8,128)(2,1)} fusion(bf16[2048,256]{1,0:T(8,128)(2,1)S(1)} %emit.1, bf16[256,2304]{1,0:T(8,128)(2,1)S(1)} %copy-done.9), kind=kOutput, calls=%fused_computation | convolution fusion | flops 2420637696 | bytes 11665408 | tf_op jit(solution)/shard_map/dot_general | solution.py:17
  148.6 0.0 copy-start.13
  148.6 0.0 reduce-scatter.2.cloned.1.call-update
  148.6 0.6 copy-done.13
  149.2 0.2 convert_reduce_fusion
  149.4 0.0 all-gather.6.cloned.1.call-done
  149.5 2.9 %fusion.2 = bf16[4,128,512]{2,0,1:T(4,128)(2,1)S(1)} fusion(bf16[16,128,512]{2,1,0:T(8,128)(2,1)} %bitcast.18, s32[16]{0:T(128)S(1)} %convert_reduce_fusion, pred[16]{0:T(512)(128)(4,1)S(1)} %broadcast_compare_fusion), kind=kOutput, calls=%fused_computation.4 | convolution fusion | flops 8650880 | bytes 2621520 | tf_op jit(solution)/shard_map/si,iab->sab/dot_general | solution.py:318
  152.3 0.9 copy.20
  153.2 64.5 %reduce-scatter.2.cloned.1.call-done = bf16[128,2304]{1,0:T(8,128)(2,1)} async-done(((bf16[2048,2304]{1,0:T(8,128)(2,1)}), bf16[128,2304]{1,0:T(8,128)(2,1)}) %reduce-scatter.2.cloned.1.call-update) | async-done | bytes 589840 | tf_op jit(solution)/shard_map/reduce_scatter | solution.py:352
  (3 shorter events, 0.0 us)
Async XLA Ops:
  7.2 1.7 copy-start
  7.2 3.3 %copy-start.11 = (f32[512]{0:T(512)S(1)}, f32[512]{0:T(512)}, u32[]{:S(2)}) copy-start(f32[512]{0:T(512)} %param.24) | copy-start | bytes 6148
  7.2 4.1 %copy-start.10 = (bf16[2304,2]{0,1:T(2,128)(2,1)S(1)}, bf16[2304,2]{0,1:T(2,128)(2,1)}, u32[]{:S(2)}) copy-start(bf16[2304,2]{0,1:T(2,128)(2,1)} %param.18) | copy-start | bytes 27652
  7.2 66.9 %all-gather.4.cloned.1.call-start = ((), (), s32[]{:S(2)}) async-start(), calls=%async_computation.1 | async-start | bytes 10027008 | tf_op jit(solution)/shard_map/all_gather | solution.py:339
  7.9 3.9 %copy-start.12 = (f32[2]{0:T(128)S(1)}, f32[2]{0:T(128)}, u32[]{:S(2)}) copy-start(f32[2]{0:T(128)} %param.19) | copy-start | bytes 28
  7.9 141.5 %all-gather.6.cloned.1.call-start = ((), (), s32[]{:S(2)}) async-start(), calls=%async_computation.3 | async-start | bytes 2228224 | tf_op jit(solution)/shard_map/all_gather | solution.py:317
  11.2 206.5 %reduce-scatter.2.cloned.1.call-start = ((), (), s32[]{:S(2)}) async-start(), calls=%async_computation.2 | async-start | bytes 10027008 | tf_op jit(solution)/shard_map/reduce_scatter | solution.py:352
  74.1 1.3 copy-start.3
  75.3 1.3 copy-start.4
  76.6 1.3 copy-start.5
  111.4 1.3 copy-start.1
  113.4 0.7 copy-start.6
  114.1 8.3 %collective-permute-start.2 = (bf16[2,128,256]{2,1,0:T(8,128)(2,1)}, bf16[2,128,256]{2,1,0:T(8,128)(2,1)S(1)}, u32[]{:S(2)}, u32[]{:S(2)}) collective-permute-start(bf16[2,128,256]{2,1,0:T(8,128)(2,1)} %convert_element_type.23), channel_id=1, source_target_pairs={{0,48},{16,0},{32,16},{48,32},{64,112},{80,64},{96,80},{112,96},{1... | collective-permute-start | bytes 393224 | tf_op jit(solution)/shard_map/ppermute | solution.py:294
  116.5 8.5 %collective-permute-start.1 = (bf16[2,128,256]{2,1,0:T(8,128)(2,1)}, bf16[2,128,256]{2,1,0:T(8,128)(2,1)}, u32[]{:S(2)}, u32[]{:S(2)}) collective-permute-start(bf16[2,128,256]{2,1,0:T(8,128)(2,1)} %convert_element_type.23), channel_id=1, source_target_pairs={{0,32},{16,48},{32,0},{48,16},{64,96},{80,112},{96,64},{112,80},{1... | collective-permute-start | bytes 393224 | tf_op jit(solution)/shard_map/ppermute | solution.py:294
  117.0 11.3 %collective-permute-start = (bf16[2,128,256]{2,1,0:T(8,128)(2,1)}, bf16[2,128,256]{2,1,0:T(8,128)(2,1)}, u32[]{:S(2)}, u32[]{:S(2)}) collective-permute-start(bf16[2,128,256]{2,1,0:T(8,128)(2,1)} %convert_element_type.23), channel_id=1, source_target_pairs={{0,16},{16,32},{32,48},{48,0},{64,80},{80,96},{96,112},{112,64},{1... | collective-permute-start | bytes 393224 | tf_op jit(solution)/shard_map/ppermute | solution.py:294
  128.3 1.0 copy-start.7
  131.1 10.0 %copy-start.2 = (f32[2048,256]{1,0:T(8,128)S(1)}, f32[2048,256]{1,0:T(8,128)}, u32[]{:S(2)}) copy-start(f32[2048,256]{1,0:T(8,128)} %copy-done.1) | copy-start | bytes 6291460
  131.1 10.0 %copy-start.8 = (f32[128]{0:T(128)S(1)}, f32[128]{0:T(128)}, u32[]{:S(2)}) copy-start(f32[128]{0:T(128)} %param.21) | copy-start | bytes 1540
  131.1 9.9 %collective-permute-start.5 = (bf16[2,128,256]{2,1,0:T(8,128)(2,1)S(1)}, bf16[2,128,256]{2,1,0:T(8,128)(2,1)S(1)}, u32[]{:S(2)}, u32[]{:S(2)}) collective-permute-start(bf16[2,128,256]{2,1,0:T(8,128)(2,1)S(1)} %get-tuple-element.13.own), channel_id=1, source_target_pairs={{0,192},{16,208},{32,224},{48,240},{64,0},{80,16},{96,32},{112,48}... | collective-permute-start | bytes 393224 | tf_op jit(solution)/shard_map/ppermute | solution.py:294
  131.7 9.3 %collective-permute-start.4 = (bf16[2,128,256]{2,1,0:T(8,128)(2,1)S(1)}, bf16[2,128,256]{2,1,0:T(8,128)(2,1)S(1)}, u32[]{:S(2)}, u32[]{:S(2)}) collective-permute-start(bf16[2,128,256]{2,1,0:T(8,128)(2,1)S(1)} %get-tuple-element.13.own), channel_id=1, source_target_pairs={{0,128},{16,144},{32,160},{48,176},{64,192},{80,208},{96,224},{112... | collective-permute-start | bytes 393224 | tf_op jit(solution)/shard_map/ppermute | solution.py:294
  132.8 8.3 %collective-permute-start.3 = (bf16[2,128,256]{2,1,0:T(8,128)(2,1)S(1)}, bf16[2,128,256]{2,1,0:T(8,128)(2,1)S(1)}, u32[]{:S(2)}, u32[]{:S(2)}) collective-permute-start(bf16[2,128,256]{2,1,0:T(8,128)(2,1)S(1)} %get-tuple-element.13.own), channel_id=1, source_target_pairs={{0,64},{16,80},{32,96},{48,112},{64,128},{80,144},{96,160},{112,17... | collective-permute-start | bytes 393224 | tf_op jit(solution)/shard_map/ppermute | solution.py:294
  141.0 2.4 %copy-start.9 = (bf16[256,2304]{1,0:T(8,128)(2,1)S(1)}, bf16[256,2304]{1,0:T(8,128)(2,1)}, u32[]{:S(2)}) copy-start(bf16[256,2304]{1,0:T(8,128)(2,1)} %param.22) | copy-start | bytes 3538948
  148.6 0.7 copy-start.13
Sparse Core Ops, SparseCore 0:
  9.9 64.1 all-gather.3
  76.5 50.3 all-gather.5
  148.7 68.9 reduce-scatter.1

commit v2 on v1

v2 whole, which is shorter than its diff:
```python
import functools
import jax
import jax.numpy as jnp
from jax import lax
from jax.experimental import pallas as pl
from jax.experimental.pallas import tpu as pltpu
from jax.sharding import PartitionSpec as P

BLK = 128
GUARD = 1e-06
BF = jnp.bfloat16
F32 = jnp.float32
VMEM_BYTES = 36 * 1024 * 1024


def dot(a, b, contract=((1,), (0,))):
    return lax.dot_general(a, b, (contract, ((), ())), preferred_element_type=F32)


def halves(a):
    high = a.astype(BF)
    return high, (a - high.astype(F32)).astype(BF)


def wide_left(a):
    return jnp.concatenate(halves(a), axis=1)


def wide_right(b):
    row = jnp.concatenate(halves(b), axis=1)
    return jnp.concatenate([row, row], axis=0)


def wide_dot(left, right):
    both = dot(left, right)
    n = both.shape[1] // 2
    return both[:, :n] + both[:, n:]


def indices(shape):
    return lax.broadcasted_iota(jnp.int32, shape, 0), lax.broadcasted_iota(jnp.int32, shape, 1)


def inverses(systems, row, col):
    eye = (row == col).astype(F32)
    joins = (row // 2 == col // 2) & (row > col)
    out = [eye - jnp.where(joins, s, 0.0) for s in systems]
    size = 2
    while size < BLK:
        joins = (row // (2 * size) == col // (2 * size)) & (row // size > col // size)
        parts = [jnp.where(joins, s, 0.0) for s in systems]
        lefts = [wide_left(t) for t in out]
        rights = [wide_right(t) for t in out]
        inner = [wide_dot(wide_left(p), r) for p, r in zip(parts, rights)]
        out = [t - wide_dot(l, wide_right(x)) for t, l, x in zip(out, lefts, inner)]
        size *= 2
    return out


def delta_kernel(group, toks, ld, w, bias, z_out, y_out, x_out, low_out, proj, rate, held):
    rows = jnp.concatenate([toks[j, :BLK] for j in range(group)], axis=0)
    lanes2 = 2 * BLK
    for j in range(3):
        proj[j] = dot(rows, w[:, j * lanes2 : (j + 1) * lanes2])
    rate[...] = jax.nn.sigmoid(dot(rows, w[:, 3 * lanes2 :]) + bias[...])

    @pl.when(pl.program_id(0) == 0)
    def start():
        across, along = indices((BLK, lanes2))
        for h in range(2):
            held[h] = (across == along).astype(F32)

    row, col = indices((BLK, BLK))
    ones = (row >= col).astype(BF)
    ones2 = jnp.concatenate([ones, ones], axis=1)
    pairs = []
    for blk in range(group):
        at = slice(blk * BLK, (blk + 1) * BLK)
        decay = ld[at, :]
        high = decay.astype(BF)
        rest = decay - high.astype(F32)
        mid = rest.astype(BF)
        low = (rest - mid.astype(F32)).astype(BF)
        cum = dot(ones2, jnp.concatenate([high, mid], axis=0)) + dot(ones, low)
        for h in range(2):
            lanes = slice(h * BLK, (h + 1) * BLK)
            pairs.append((blk, at, h, lanes, cum[:, lanes]))
    systems, targets, scores, ends, firsts, finals = [], [], [], [], [], []
    for blk, at, h, lanes, c in pairs:
        q = proj[0, at, lanes]
        k = proj[1, at, lanes]
        v = proj[2, at, lanes]
        q = q * lax.rsqrt(jnp.sum(q * q, axis=-1, keepdims=True) + GUARD)
        k = k * lax.rsqrt(jnp.sum(k * k, axis=-1, keepdims=True) + GUARD)
        beta = rate[at, h : h + 1]
        final = c[BLK - 1 : BLK, :]
        grow = jnp.exp(c)
        k_up = k * grow
        q_up = q * grow
        k_down = (k * jnp.exp(-c)).astype(BF)
        k_end = k * jnp.exp(final - c)
        gram = dot(jnp.concatenate([k_up, q_up], axis=0).astype(BF), k_down, ((1,), (1,)))
        systems.append(jnp.where(row > col, beta * gram[:BLK], 0.0))
        scores.append(jnp.where(row >= col, gram[BLK:], 0.0).astype(BF))
        targets.append(jnp.concatenate([(beta * k_up).astype(BF), (beta * v).astype(BF)], axis=1))
        ends.append(k_end.T.astype(BF))
        firsts.append(q_up)
        finals.append(jnp.exp(final))
    solved = inverses(systems, row, col)
    solved = [dot(t.astype(BF), g).astype(BF) for t, g in zip(solved, targets)]
    earlier, rises, adds, maps = {}, {}, {}, {}
    for (blk, at, h, lanes, c), w_, s, e, f, last in zip(pairs, solved, scores, ends, firsts, finals):
        both = dot(jnp.concatenate([s, e], axis=0), w_)
        p, o = f - both[:BLK, :BLK], both[:BLK, BLK:]
        m, n = jnp.where(row == col, last, 0.0) - both[BLK:, :BLK], both[BLK:, BLK:]
        if blk % 2 == 0:
            earlier[h] = p.astype(BF), o, jnp.concatenate([m, n], axis=1)
        else:
            p0, o0, before = earlier[h]
            seen = dot(p.astype(BF), before.astype(BF))
            rises[blk // 2, h] = jnp.concatenate([p0, seen[:, :BLK].astype(BF)], axis=0)
            adds[blk // 2, h] = jnp.concatenate([o0, seen[:, BLK:] + o], axis=0)
            moved = compose(m, before)
            maps[blk // 2, h] = moved[:, :BLK], moved[:, BLK:] + n
    x = [held[h] for h in range(2)]
    for pair in range(group // 2):
        at = slice(pair * lanes2, (pair + 1) * lanes2)
        for h in range(2):
            lanes = slice(h * BLK, (h + 1) * BLK)
            both = dot(rises[pair, h], x[h].astype(BF))
            z_out[at, lanes] = both[:, :BLK].astype(BF)
            y_out[at, lanes] = both[:, BLK:] + adds[pair, h]
            m, n = maps[pair, h]
            moved = compose(m, x[h])
            x[h] = jnp.concatenate([moved[:, :BLK], moved[:, BLK:] + n], axis=1)
    for h in range(2):
        held[h] = x[h]
        x_out[h] = x[h]
        low_out[h] = x[h].astype(BF)


def narrow_left(a):
    high, low = halves(a)
    return jnp.concatenate([high, low], axis=1), high


def compose(a, x):
    left, high = narrow_left(a)
    x_high, x_low = halves(x)
    return dot(left, jnp.concatenate([x_high, x_high], axis=0)) + dot(high, x_low)


def delta_blocks(tokens, ld, weights, bias, group=4):
    blocks, rows, width = tokens.shape
    lanes = 2 * BLK
    out = pl.BlockSpec((group * BLK, lanes), lambda i: (i, 0))
    last = pl.BlockSpec((2, BLK, lanes), lambda i: (0, 0, 0))
    return pl.pallas_call(
        functools.partial(delta_kernel, group),
        grid=(blocks // group,),
        in_specs=[
            pl.BlockSpec((group, rows, width), lambda i: (i, 0, 0)),
            pl.BlockSpec((group * BLK, lanes), lambda i: (i, 0)),
            pl.BlockSpec(memory_space=pltpu.VMEM),
            pl.BlockSpec(memory_space=pltpu.VMEM),
        ],
        out_specs=[out, out, last, last],
        out_shape=[
            jax.ShapeDtypeStruct((blocks * BLK, lanes), BF),
            jax.ShapeDtypeStruct((blocks * BLK, lanes), F32),
            jax.ShapeDtypeStruct((2, BLK, lanes), F32),
            jax.ShapeDtypeStruct((2, BLK, lanes), BF),
        ],
        scratch_shapes=[
            pltpu.VMEM((3, group * BLK, lanes), F32),
            pltpu.VMEM((group * BLK, BLK), F32),
            pltpu.VMEM((2, BLK, lanes), F32),
        ],
        compiler_params=pltpu.CompilerParams(vmem_limit_bytes=VMEM_BYTES),
        cost_estimate=pl.CostEstimate(
            flops=blocks * BLK * 12 * 10**6, bytes_accessed=blocks * BLK * 12000, transcendentals=0
        ),
        name="delta_blocks",
    )(tokens, ld, weights, bias)


def side_kernel(place, own, one, two, three, before, total, slots):
    me = place[0]
    for h in range(2):
        slots[0, h] = own[h]
        for d, got in enumerate((one, two, three)):
            slots[d + 1, h] = got[h].astype(F32)
    row, col = indices((BLK, 2 * BLK))
    maps = [None, None]
    for j in range(4):

        @pl.when(me == j)
        def keep():
            for h in range(2):
                before[h] = (row == col).astype(F32) if j == 0 else maps[h]

        at = (me + 4 - j) % 4
        for h in range(2):
            if j == 0:
                maps[h] = slots[at, h]
            else:
                moved = compose(slots[at, h, :, :BLK], maps[h])
                maps[h] = jnp.concatenate(
                    [moved[:, :BLK], moved[:, BLK:] + slots[at, h, :, BLK:]], axis=1
                )
    for h in range(2):
        total[h] = maps[h].astype(BF)


def side_maps(place, own, received):
    whole = pl.BlockSpec(own.shape, lambda i: (0, 0, 0))
    return pl.pallas_call(
        side_kernel,
        grid=(1,),
        in_specs=[pl.BlockSpec(memory_space=pltpu.SMEM)] + [whole] * 4,
        out_specs=[whole, whole],
        out_shape=[jax.ShapeDtypeStruct(own.shape, F32), jax.ShapeDtypeStruct(own.shape, BF)],
        scratch_shapes=[pltpu.VMEM((4,) + own.shape, F32)],
        compiler_params=pltpu.CompilerParams(vmem_limit_bytes=VMEM_BYTES),
        name="side_maps",
    )(place, own, *received)


def emit_kernel(group, place, before, own, one, two, three, z, y, gate, gain, out, slots, state):
    me = place[0]

    @pl.when(pl.program_id(0) == 0)
    def enter():
        for d, got in enumerate((own, one, two, three)):
            slots[d] = got[...]
        for h in range(2):
            s = jnp.zeros((BLK, BLK), F32)
            for j in range(3):
                at = (me + 4 - j) % 4
                moved = slots[at, h, :, BLK:].astype(F32)
                if j > 0:
                    moved = moved + compose(slots[at, h, :, :BLK].astype(F32), s)
                s = jnp.where(j < me, moved, s)
            s = compose(before[h, :, :BLK], s) + before[h, :, BLK:]
            state[h] = s.astype(BF)

    for j in range(group):
        at = slice(j * BLK, (j + 1) * BLK)
        for h in range(2):
            lanes = slice(h * BLK, (h + 1) * BLK)
            a = y[at, lanes] + dot(z[at, lanes], state[h])
            scale = lax.rsqrt(jnp.mean(a * a, axis=-1, keepdims=True) + GUARD)
            a = a * scale * gain[...] * jax.nn.sigmoid(gate[j, :BLK, lanes].astype(F32))
            out[at, lanes] = a.astype(BF)


def emit(place, before, own, received, z, y, gate, gain, group=4):
    small = pl.BlockSpec(own.shape, lambda i: (0, 0, 0))
    tall = pl.BlockSpec((group * BLK, 2 * BLK), lambda i: (i, 0))
    return pl.pallas_call(
        functools.partial(emit_kernel, group),
        grid=(z.shape[0] // (group * BLK),),
        in_specs=[pl.BlockSpec(memory_space=pltpu.SMEM)]
        + [small] * 5
        + [tall] * 2
        + [pl.BlockSpec((group,) + gate.shape[1:], lambda i: (i, 0, 0))]
        + [pl.BlockSpec((1, BLK), lambda i: (0, 0))],
        out_specs=tall,
        out_shape=jax.ShapeDtypeStruct(z.shape, BF),
        scratch_shapes=[pltpu.VMEM((4,) + own.shape, BF), pltpu.VMEM((2, BLK, BLK), BF)],
        compiler_params=pltpu.CompilerParams(vmem_limit_bytes=VMEM_BYTES),
        name="emit",
    )(place, before, own, *received, z, y, gate, gain)


def output_kernel(info, a, w, mine, theirs, total):
    core = info[0]
    parts, levels, rows, width = w.shape
    depth = parts * rows
    for i in range(levels):
        at = pl.ds(pl.multiple_of(info[1 + i] * depth, depth), depth)
        more = dot(a[:, at], w[:, i].reshape(depth, width))
        total[...] = more if i == 0 else total[...] + more
    mine[...] = total[pl.ds(pl.multiple_of(core * BLK, BLK), BLK), :]
    theirs[...] = total[pl.ds(pl.multiple_of((1 - core) * BLK, BLK), BLK), :].astype(BF)


def fetch_kernel(far, near, sem):
    copy = pltpu.make_async_copy(far, near, sem)
    copy.start()
    copy.wait()


def fetched(array):
    return pl.pallas_call(
        fetch_kernel,
        in_specs=[pl.BlockSpec(memory_space=pl.ANY)],
        out_specs=pl.BlockSpec(memory_space=pltpu.VMEM),
        out_shape=jax.ShapeDtypeStruct(array.shape, array.dtype),
        scratch_shapes=[pltpu.SemaphoreType.DMA(())],
        compiler_params=pltpu.CompilerParams(vmem_limit_bytes=16 * 1024 * 1024),
        cost_estimate=pl.CostEstimate(flops=0, bytes_accessed=2 * array.size, transcendentals=0),
        name="fetched",
    )(array)


def output_rows(info, normed, weight):
    parts, levels, rows, width = weight.shape
    here = pl.BlockSpec(memory_space=pltpu.VMEM)
    return pl.pallas_call(
        output_kernel,
        in_specs=[pl.BlockSpec(memory_space=pltpu.SMEM), here, here],
        out_specs=[here, here],
        scratch_shapes=[pltpu.VMEM((2 * BLK, width), F32)],
        out_shape=[
            jax.ShapeDtypeStruct((BLK, width), F32),
            jax.ShapeDtypeStruct((BLK, width), BF),
        ],
        compiler_params=pltpu.CompilerParams(vmem_limit_bytes=VMEM_BYTES),
        cost_estimate=pl.CostEstimate(
            flops=4 * BLK * parts * levels * rows * width,
            bytes_accessed=2 * parts * levels * rows * width,
            transcendentals=0,
        ),
        name="output_rows",
    )(info, normed, weight)


def turn(array, axis, pairs):
    return lax.ppermute(array, axis, pairs)


def along_y(d):
    return [(4 * x + y, 4 * x + (y + d) % 4) for x in range(4) for y in range(4)]


def along_x(d):
    return [(4 * x + y, 4 * ((x + d) % 4) + y) for x in range(4) for y in range(4)]


def across():
    return [(t, t ^ 1) for t in range(16)]


def after(array, *others):
    return lax.optimization_barrier((array,) + others)[0]


SAME_CORE = [[2 * z + k for z in range(8)] for k in range(2)]


def latent_rows(tokens, kv_weight, kv_gain):
    latent = dot(tokens, kv_weight)
    scale = lax.rsqrt(jnp.mean(latent * latent, axis=-1, keepdims=True) + GUARD)
    return (latent * scale * kv_gain).astype(BF)


def pick_kernel(info, tile, out):
    out[...] = jnp.where(info[4 + pl.program_id(0)] > 0, tile[...], jnp.zeros_like(out))


def picked(tiles, owner, ctx):
    owners = owner.reshape(-1)
    count = owners.shape[0]
    order = jnp.arange(count, dtype=jnp.int32)
    same = owners[:, None] == owners[None, :]
    rank = jnp.sum((same & (order[None, :] < order[:, None])).astype(jnp.int32), axis=1)
    slots = jnp.arange(4, dtype=jnp.int32)[:, None]
    wanted = ((owners[None, :] == ctx) & (rank[None, :] == slots)).astype(jnp.int32)
    source = jnp.sum(wanted * order[None, :], axis=1)
    place = 4 * ((ctx // 4 - source // 4 + 4) % 4) + (ctx % 4 - source % 4 + 4) % 4
    info = jnp.concatenate([place, jnp.sum(wanted, axis=1)]).astype(jnp.int32)
    shape = tiles.shape[1:]
    return pl.pallas_call(
        pick_kernel,
        grid_spec=pltpu.PrefetchScalarGridSpec(
            num_scalar_prefetch=1,
            grid=(4,),
            in_specs=[pl.BlockSpec((1,) + shape, lambda i, info: (info[i], 0, 0))],
            out_specs=pl.BlockSpec((1,) + shape, lambda i, info: (i, 0, 0)),
        ),
        out_shape=jax.ShapeDtypeStruct((4,) + shape, tiles.dtype),
        compiler_params=pltpu.CompilerParams(vmem_limit_bytes=VMEM_BYTES),
        name="picked",
    )(info, tiles)


def body(
    tokens,
    query_weight,
    key_weight,
    values_projector_matrix,
    gate_weight,
    beta_weight,
    beta_bias,
    log_decay,
    head_gain,
    output_weight,
    kv_weight,
    kv_gain,
    owner,
):
    ctx = lax.axis_index("ctx").astype(jnp.int32)
    tp = lax.axis_index("tp").astype(jnp.int32)
    core = tp % 2
    spare = BLK - beta_weight.shape[1]
    wide = BLK + 16

    part = lax.dynamic_slice_in_dim(output_weight, ctx * 16, 16, 0)
    gathered = lax.all_gather(jnp.concatenate([tokens, part], axis=0), "tp", axis=0)
    weights = jnp.concatenate(
        [query_weight, key_weight, values_projector_matrix, jnp.pad(beta_weight, ((0, 0), (0, spare)))],
        axis=1,
    )
    bias = jnp.pad(beta_bias, (0, spare))[None]
    latent = after(latent_rows(tokens, kv_weight, kv_gain), weights)
    tiles = jnp.stack([latent] + [turn(latent, "ctx", along_y(d)) for d in (1, 2, 3)])
    tiles = jnp.concatenate([tiles] + [turn(tiles, "ctx", along_x(d)) for d in (1, 2, 3)])
    cache = picked(tiles, owner, ctx)
    gathered = after(gathered, cache)
    part = gathered.reshape(8, 2 * wide, -1)
    part = lax.dynamic_slice_in_dim(part, core * wide + BLK, 16, 1).reshape(BLK, -1)
    gathered = after(gathered, part)
    all_parts = lax.all_gather(part, "ctx", axis=0, tiled=True)
    all_parts = all_parts.reshape(16, 8, 16, output_weight.shape[1])

    z, y, maps, low = delta_blocks(gathered, log_decay, weights, bias)
    received = [turn(low, "ctx", along_y(d)) for d in (1, 2, 3)]
    before, total = side_maps((ctx % 4)[None], maps, received)
    received = [turn(total, "ctx", along_x(d)) for d in (1, 2, 3)]
    gate = dot(gathered, gate_weight, ((2,), (0,))).astype(BF)
    normed = emit((ctx // 4)[None], before, total, received, z, y, gate, head_gain[None])

    normed = lax.all_to_all(normed, "tp", 0, 1, tiled=True, axis_index_groups=SAME_CORE)
    info = jnp.stack([core] + [jnp.int32(i) for i in range(8)])
    mine, theirs = output_rows(info, normed, fetched(all_parts))
    theirs = turn(theirs, "tp", across())
    return (mine + theirs.astype(F32)).astype(BF), cache


def solution(mesh):
    in_specs = (
        P(("ctx", "tp"), None),
        P(None, "tp"),
        P(None, "tp"),
        P(None, "tp"),
        P(None, "tp"),
        P(None, "tp"),
        P("tp"),
        P("ctx", "tp"),
        P(),
        P("tp", None),
        P(),
        P(),
        P(None, "tp"),
    )
    out_specs = (P(("ctx", "tp"), None), P("ctx", "tp", None))
    return jax.shard_map(body, mesh=mesh, in_specs=in_specs, out_specs=out_specs, check_vma=False)
```

time: 227 us -> 202 us (0.89)
  waiting for transfers between devices: 138 us -> 90.9 us
  starting transfers between devices: 7.04 us -> 22.9 us
  matrix products: 16.2 us -> 3.49 us
  local copies, waits for them, and re-layouts: 9.66 us -> 21.3 us
  other arithmetic: 1.61 us -> 5.6 us
    reduce_scatter x1 -> x0, waiting for transfers between devices: 64.5 us -> none  [body(): lax.psum_scatter(dot(normed, output_weight).astype(BF), 'tp', scatter_dim...]
    all_gather x2, waiting for transfers between devices: 62.3 us -> 24.2 us  [the longest x1 24.2 us: body(): lax.all_gather(jnp.concatenate([tokens, part], axis=0), 'tp', axis=0)]
    ppermute x6 -> x13, waiting for transfers between devices: 10.7 us -> 40.6 us  [turn(): return lax.ppermute(array, axis, pairs)]
    all_to_all x0 -> x1, waiting for transfers between devices: none -> 26 us  [body(): lax.all_to_all(normed, 'tp', 0, 1, tiled=True, axis_index_groups=SAME_CORE)]
    ppermute x6 -> x13, starting transfers between devices: 6.92 us -> 18.6 us  [turn(): return lax.ppermute(array, axis, pairs)]
    dot_general x3 -> x2, matrix products: 13.3 us -> 3.49 us  [dot(): lax.dot_general(a, b, (contract, ((), ())), preferred_element_type=F32)]
    unnamed x30 -> x41, local copies, waits for them, and re-layouts: 9.53 us -> 16 us
    all_to_all x0 -> x1, starting transfers between devices: none -> 4.21 us  [body(): lax.all_to_all(normed, 'tp', 0, 1, tiled=True, axis_index_groups=SAME_CORE)]
  transfers between devices with their start and end apart: 9 -> 16, of which waited for: 5 -> 13; matrix products, arithmetic and copies ran while one was open for 9% -> 7% of each run, Pallas kernels for 17% -> 18%
where the time goes in v2:
time: 202 us; the launch traced here: 198 us
  waiting for transfers between devices  90.9 us (45%)
  Pallas kernels  39.9 us (20%)
  starting transfers between devices  22.9 us (11%)
  local copies, waits for them, and re-layouts  21.3 us (11%)
  between operations  14.3 us (7%)
  other arithmetic  5.6 us (3%)
  matrix products  3.49 us (2%)
    ppermute x13, waiting for transfers between devices, turn(): return lax.ppermute(array, axis, pairs)  40.6 us
    pallas_call x1, Pallas kernels, delta_blocks(): pl.pallas_call(functools.partial(delta_kernel, group), grid=(blocks // gr...  29.8 us
    all_to_all x1, waiting for transfers between devices, body(): lax.all_to_all(normed, 'tp', 0, 1, tiled=True, axis_index_groups=SAME_CORE)  26 us
    all_gather x1, waiting for transfers between devices, body(): lax.all_gather(jnp.concatenate([tokens, part], axis=0), 'tp', axis=0)  24.2 us
    ppermute x13, starting transfers between devices, turn(): return lax.ppermute(array, axis, pairs)  18.6 us
    unnamed x41, local copies, waits for them, and re-layouts  16 us
    all_to_all x1, starting transfers between devices, body(): lax.all_to_all(normed, 'tp', 0, 1, tiled=True, axis_index_groups=SAME_CORE)  4.21 us
  transfers between devices with their start and end apart: 16, of which 13 were waited for; matrix products, arithmetic and copies ran while one was open for 7% of the time, Pallas kernels for 18%

profile of v2, /device:TPU:7, one launch (start us, length us, event | category | flops | bytes accessed | tf_op | source)
XLA Modules:
  0.0 198.3 jit_solution(17746940888118132229)
XLA Ops:
  7.2 0.0 all-gather.6.cloned.1.call-start
  7.3 1.0 constant_dynamic-slice_fusion.1
  8.3 2.0 pad_maximum_fusion
  10.3 0.0 all-gather.4.cloned.1.call-start
  10.4 0.4 copy.19
  10.8 0.6 multiply_reduce_fusion
  11.4 0.1 multiply_convert_fusion
  11.5 0.6 copy-done.8
  12.1 0.4 copy-done.9
  12.4 0.4 copy-done.10
  12.8 2.1 %fusion.1.w = bf16[2304,896]{1,0:T(8,128)(2,1)} fusion(bf16[2304,2]{1,0:T(8,128)(2,1)S(1)} %copy.19, bf16[2304,256]{1,0:T(8,128)(2,1)S(1)} %copy-done.8, bf16[2304,256]{1,0:T(8,128)(2,1)S(1)} %copy-done.9, bf16[2304,256]{1,0:T(8,128)(2,1)S(1)} %copy-done.10), kind=kLoop, calls=%fused_computation.2 | loop fusion | flops 20643840 | bytes 7676928 | tf_op jit(solution)/shard_map/concatenate | solution.py:411
  14.9 1.3 collective-permute-start
  16.2 2.6 %collective-permute-start.1 = (bf16[128,512]{1,0:T(8,128)(2,1)S(1)}, bf16[128,512]{1,0:T(8,128)(2,1)S(1)}, u32[]{:S(2)}, u32[]{:S(2)}) collective-permute-start(bf16[128,512]{1,0:T(8,128)(2,1)S(1)} %multiply_convert_fusion), channel_id=1, source_target_pairs={{0,32},{16,48},{32,0},{48,16},{64,96},{80,112},{96,64},{112,80},{1... | collective-permute-start | bytes 393224 | tf_op jit(solution)/shard_map/ppermute | solution.py:330
  18.8 1.1 collective-permute-start.2
  19.9 0.2 convert_reduce_fusion
  20.1 0.2 select_reduce_fusion
  20.2 0.7 constant_dynamic-update-slice_fusion.6
  20.9 0.1 pad_add_fusion.info
  21.0 3.5 %collective-permute-done.1 = bf16[128,512]{1,0:T(8,128)(2,1)S(1)} collective-permute-done((bf16[128,512]{1,0:T(8,128)(2,1)S(1)}, bf16[128,512]{1,0:T(8,128)(2,1)S(1)}, u32[]{:S(2)}, u32[]{:S(2)}) %collective-permute-start.1) | collective-permute-done | bytes 131104 | tf_op jit(solution)/shard_map/ppermute | solution.py:330
  24.5 0.1 pad_maximum_fusion.1
  24.6 0.3 collective-permute-start.3
  24.9 2.1 %collective-permute-start.4 = (bf16[4,128,512]{2,1,0:T(8,128)(2,1)S(1)}, bf16[4,128,512]{2,1,0:T(8,128)(2,1)S(1)}, u32[]{:S(2)}, u32[]{:S(2)}) collective-permute-start(bf16[4,128,512]{2,1,0:T(8,128)(2,1)S(1)} %pad_maximum_fusion.1), channel_id=1, source_target_pairs={{0,128},{16,144},{32,160},{48,176},{64,192},{80,208},{96,224},{112... | collective-permute-start | bytes 1572872 | tf_op jit(solution)/shard_map/ppermute | solution.py:330
  27.0 0.6 constant_dynamic-update-slice_fusion.5
  27.7 0.6 constant_dynamic-update-slice_fusion.4
  28.3 0.7 constant_dynamic-update-slice_fusion.3
  29.0 7.7 %collective-permute-done.3 = bf16[4,128,512]{2,1,0:T(8,128)(2,1)S(1)} collective-permute-done((bf16[4,128,512]{2,1,0:T(8,128)(2,1)S(1)}, bf16[4,128,512]{2,1,0:T(8,128)(2,1)S(1)}, u32[]{:S(2)}, u32[]{:S(2)}) %collective-permute-start.3) | collective-permute-done | bytes 524320 | tf_op jit(solution)/shard_map/ppermute | solution.py:330
  36.6 0.8 constant_dynamic-update-slice_fusion.2
  37.5 0.3 collective-permute-done.4
  37.8 0.8 constant_dynamic-update-slice_fusion.1
  38.6 12.9 %collective-permute-done.5 = bf16[4,128,512]{2,1,0:T(8,128)(2,1)S(1)} collective-permute-done((bf16[4,128,512]{2,1,0:T(8,128)(2,1)S(1)}, bf16[4,128,512]{2,1,0:T(8,128)(2,1)S(1)}, u32[]{:S(2)}, u32[]{:S(2)}) %collective-permute-start.5) | collective-permute-done | bytes 524320 | tf_op jit(solution)/shard_map/ppermute | solution.py:330
  51.6 0.9 constant_dynamic-update-slice_fusion.tile
  52.4 1.6 copy-done.3
  54.0 2.0 picked.1
  56.0 24.2 %all-gather.6.cloned.1.call-done = bf16[2304,2304]{1,0:T(8,128)(2,1)} async-done(((bf16[144,2304]{1,0:T(8,128)(2,1)}), bf16[2304,2304]{1,0:T(8,128)(2,1)}) %all-gather.6.cloned.1.call-update) | async-done | bytes 10616848 | tf_op jit(solution)/shard_map/all_gather | solution.py:410
  80.2 1.9 constant_dynamic-slice_fusion
  82.2 2.2 %copy-done.2 = bf16[2304,896]{1,0:T(8,128)(2,1)S(1)} copy-done((bf16[2304,896]{1,0:T(8,128)(2,1)S(1)}, bf16[2304,896]{1,0:T(8,128)(2,1)}, u32[]{:S(2)}) %copy-start.2) | copy-done | bytes 4128792
  84.3 1.6 copy-done.5
  85.9 29.8 %delta_blocks.1 = (bf16[2048,256]{1,0:T(8,128)(2,1)S(1)}, f32[2048,256]{1,0:T(8,128)S(1)}, f32[2,128,256]{2,1,0:T(8,128)S(1)}, bf16[2,128,256]{2,1,0:T(8,128)(2,1)S(1)}) custom-call(bf16[16,144,2304]{2,1,0:T(8,128)(2,1)} %bitcast.40, f32[2048,256]{1,0:T(8,128)S(1)} %copy-done.5, bf16[2304,896]{1,0:T(8,128)(2,1)S(1)} %copy-done.2, ...), custom_call_target="tpu_custom_call" | custom-call | flops 24576000000 | bytes 24576000 | tf_op jit(solution)/shard_map/delta_blocks/pallas_call | solution.py:158
  115.7 1.5 collective-permute-start.6
  117.2 2.4 %collective-permute-start.7 = (bf16[2,128,256]{2,1,0:T(8,128)(2,1)S(1)}, bf16[2,128,256]{2,1,0:T(8,128)(2,1)S(1)}, u32[]{:S(2)}, u32[]{:S(2)}) collective-permute-start(bf16[2,128,256]{2,1,0:T(8,128)(2,1)S(1)} %get-tuple-element.17), channel_id=1, source_target_pairs={{0,32},{16,48},{32,0},{48,16},{64,96},{80,112},{96,64},{112,80},{1... | collective-permute-start | bytes 393224 | tf_op jit(solution)/shard_map/ppermute | solution.py:330
  119.6 1.2 collective-permute-start.8
  120.8 1.3 collective-permute-done.6.one
  122.0 5.2 %collective-permute-done.7.two = bf16[2,128,256]{2,1,0:T(8,128)(2,1)S(1)} collective-permute-done((bf16[2,128,256]{2,1,0:T(8,128)(2,1)S(1)}, bf16[2,128,256]{2,1,0:T(8,128)(2,1)S(1)}, u32[]{:S(2)}, u32[]{:S(2)}) %collective-permute-start.7) | collective-permute-done | bytes 131104 | tf_op jit(solution)/shard_map/ppermute | solution.py:330
  127.2 0.4 collective-permute-done.8.three
  127.6 0.8 side_maps.1
  128.4 0.4 collective-permute-start.9
  128.8 2.1 %collective-permute-start.10 = (bf16[2,128,256]{2,1,0:T(8,128)(2,1)S(1)}, bf16[2,128,256]{2,1,0:T(8,128)(2,1)S(1)}, u32[]{:S(2)}, u32[]{:S(2)}) collective-permute-start(bf16[2,128,256]{2,1,0:T(8,128)(2,1)S(1)} %get-tuple-element.19.own), channel_id=1, source_target_pairs={{0,128},{16,144},{32,160},{48,176},{64,192},{80,208},{96,224},{112... | collective-permute-start | bytes 393224 | tf_op jit(solution)/shard_map/ppermute | solution.py:330
  130.9 2.9 %convolution_convert_fusion.gate = bf16[16,144,256]{2,1,0:T(8,128)(2,1)S(1)} fusion(bf16[16,144,2304]{2,1,0:T(8,128)(2,1)S(1)} %bitcast.41, bf16[2304,256]{1,0:T(8,128)(2,1)S(1)} %copy-done.14), kind=kOutput, calls=%fused_computation.3 | convolution fusion | flops 2718498816 | bytes 12976128 | tf_op jit(solution)/shard_map/dot_general | solution.py:17
  133.8 1.9 collective-permute-done.9.one
  135.7 1.6 collective-permute-done.10.two
  137.3 4.2 %collective-permute-done.11.three = bf16[2,128,256]{2,1,0:T(8,128)(2,1)S(1)} collective-permute-done((bf16[2,128,256]{2,1,0:T(8,128)(2,1)S(1)}, bf16[2,128,256]{2,1,0:T(8,128)(2,1)S(1)}, u32[]{:S(2)}, u32[]{:S(2)}) %collective-permute-start.11) | collective-permute-done | bytes 131104 | tf_op jit(solution)/shard_map/ppermute | solution.py:330
  141.5 3.4 %emit.1 = bf16[2048,256]{1,0:T(8,128)(2,1)} custom-call(s32[1]{0:T(128)} %bitcast.1.place, f32[2,128,256]{2,1,0:T(8,128)S(1)} %get-tuple-element.18.before, bf16[2,128,256]{2,1,0:T(8,128)(2,1)S(1)} %get-tuple-element.19.own, bf16[2,128,256]{2,1,0:T(8,128)(2,1)S(1)} %collective-permute-done.9.one, bf16[2,128,256]{2,1,0:T(8,128)(2,1)S(1)} %collective-permute-done.10.two, ...), custom_call_target="tpu_custom_call" | custom-call | tf_op jit(solution)/shard_map/emit/pallas_call | solution.py:260
  144.9 4.2 %all-to-all-start = ((bf16[8,256,256]{2,1,0:T(8,128)(2,1)}), bf16[8,256,256]{2,1,0:T(8,128)(2,1)S(1)}, u32[]{:S(2)}, u32[]{:S(2)}) async-start(bf16[8,256,256]{2,1,0:T(8,128)(2,1)} %bitcast.14), calls=%async_computation | async-start | bytes 2097152 | tf_op jit(solution)/shard_map/all_to_all | solution.py:434
  149.1 0.1 stack.22.info
  149.2 26.0 %all-to-all-done = bf16[8,256,256]{2,1,0:T(8,128)(2,1)S(1)} async-done(((bf16[8,256,256]{2,1,0:T(8,128)(2,1)}), bf16[8,256,256]{2,1,0:T(8,128)(2,1)S(1)}, u32[]{:S(2)}, u32[]{:S(2)}) %all-to-all-start) | async-done | bytes 1048608 | tf_op jit(solution)/shard_map/all_to_all | solution.py:434
  175.3 1.0 copy-done.6
  176.2 1.3 copy.21
  177.6 0.0 all-gather.4.cloned.1.call-done
  177.6 3.7 %copy-done.1 = bf16[2048,2304]{1,0:T(8,128)(2,1)S(1)} copy-done((bf16[2048,2304]{1,0:T(8,128)(2,1)S(1)}, bf16[2048,2304]{1,0:T(8,128)(2,1)}, u32[]{:S(2)}) %copy-start.1) | copy-done | bytes 9437208
  181.3 0.6 fetched.1.w
  181.9 3.3 %output_rows.1 = (f32[128,2304]{1,0:T(8,128)S(1)}, bf16[128,2304]{1,0:T(8,128)(2,1)S(1)}) custom-call(s32[9]{0:T(128)S(1)} %stack.22.info, bf16[256,2048]{1,0:T(8,128)(2,1)S(1)} %bitcast.31, bf16[16,8,16,2304]{3,2,1,0:T(8,128)(2,1)S(1)} %fetched.1.w), custom_call_target="tpu_custom_call" | custom-call | flops 2415919104 | bytes 9437184 | tf_op jit(solution)/shard_map/output_rows/pallas_call | solution.py:310
  185.2 3.7 %collective-permute-start.12 = (bf16[128,2304]{1,0:T(8,128)(2,1)S(1)}, bf16[128,2304]{1,0:T(8,128)(2,1)S(1)}, u32[]{:S(2)}, u32[]{:S(2)}) collective-permute-start(bf16[128,2304]{1,0:T(8,128)(2,1)S(1)} %get-tuple-element.23), channel_id=1, source_target_pairs={{0,1},{1,0},{2,3},{3,2},{4,5},{5,4},{6,7},{7,6},{8,9},{9,8},{10,11... | collective-permute-start | bytes 1769480 | tf_op jit(solution)/shard_map/ppermute | solution.py:330
  188.9 1.6 collective-permute-done.12
  190.6 0.9 add_convert_fusion
  (36 shorter events, 0.1 us)
Async XLA Ops:
  7.2 3.6 %copy-start = (bf16[2304,512]{1,0:T(8,128)(2,1)S(1)}, bf16[2304,512]{1,0:T(8,128)(2,1)}, u32[]{:S(2)}) copy-start(bf16[2304,512]{1,0:T(8,128)(2,1)} %param.23) | copy-start | bytes 7077892
  7.2 3.6 %copy-start.7 = (bf16[128,2304]{1,0:T(8,128)(2,1)S(1)}, bf16[128,2304]{1,0:T(8,128)(2,1)}, u32[]{:S(2)}) copy-start(bf16[128,2304]{1,0:T(8,128)(2,1)} %param.13) | copy-start | bytes 1769476
  7.2 3.2 %copy-start.12 = (bf16[2304,2]{0,1:T(2,128)(2,1)S(1)}, bf16[2304,2]{0,1:T(2,128)(2,1)}, u32[]{:S(2)}) copy-start(bf16[2304,2]{0,1:T(2,128)(2,1)} %param.18) | copy-start | bytes 27652
  7.2 73.0 %all-gather.6.cloned.1.call-start = ((), (), s32[]{:S(2)}) async-start(), calls=%async_computation.2 | async-start | bytes 11280384 | tf_op jit(solution)/shard_map/all_gather | solution.py:410
  10.3 1.1 copy-start.13
  10.3 167.3 %all-gather.4.cloned.1.call-start = ((), (), s32[]{:S(2)}) async-start(), calls=%async_computation.1 | async-start | bytes 10027008 | tf_op jit(solution)/shard_map/all_gather | solution.py:424
  10.8 1.3 copy-start.8
  10.8 1.6 copy-start.9
  10.8 2.0 copy-start.10
  12.8 7.1 %copy-start.15 = (s32[16,1]{0,1:T(1,128)S(1)}, s32[16,1]{0,1:T(1,128)}, u32[]{:S(2)}) copy-start(s32[16,1]{0,1:T(1,128)} %param.25) | copy-start | bytes 196
  14.9 6.1 %collective-permute-start = (bf16[128,512]{1,0:T(8,128)(2,1)S(1)}, bf16[128,512]{1,0:T(8,128)(2,1)S(1)}, u32[]{:S(2)}, u32[]{:S(2)}) collective-permute-start(bf16[128,512]{1,0:T(8,128)(2,1)S(1)} %multiply_convert_fusion), channel_id=1, source_target_pairs={{0,16},{16,32},{32,48},{48,0},{64,80},{80,96},{96,112},{112,64},{1... | collective-permute-start | bytes 393224 | tf_op jit(solution)/shard_map/ppermute | solution.py:330
  16.2 8.3 %collective-permute-start.1 = (bf16[128,512]{1,0:T(8,128)(2,1)S(1)}, bf16[128,512]{1,0:T(8,128)(2,1)S(1)}, u32[]{:S(2)}, u32[]{:S(2)}) collective-permute-start(bf16[128,512]{1,0:T(8,128)(2,1)S(1)} %multiply_convert_fusion), channel_id=1, source_target_pairs={{0,32},{16,48},{32,0},{48,16},{64,96},{80,112},{96,64},{112,80},{1... | collective-permute-start | bytes 393224 | tf_op jit(solution)/shard_map/ppermute | solution.py:330
  18.8 5.7 %collective-permute-start.2 = (bf16[128,512]{1,0:T(8,128)(2,1)S(1)}, bf16[128,512]{1,0:T(8,128)(2,1)S(1)}, u32[]{:S(2)}, u32[]{:S(2)}) collective-permute-start(bf16[128,512]{1,0:T(8,128)(2,1)S(1)} %multiply_convert_fusion), channel_id=1, source_target_pairs={{0,48},{16,0},{32,16},{48,32},{64,112},{80,64},{96,80},{112,96},{1... | collective-permute-start | bytes 393224 | tf_op jit(solution)/shard_map/ppermute | solution.py:330
  24.6 12.1 %collective-permute-start.3 = (bf16[4,128,512]{2,1,0:T(8,128)(2,1)S(1)}, bf16[4,128,512]{2,1,0:T(8,128)(2,1)S(1)}, u32[]{:S(2)}, u32[]{:S(2)}) collective-permute-start(bf16[4,128,512]{2,1,0:T(8,128)(2,1)S(1)} %pad_maximum_fusion.1), channel_id=1, source_target_pairs={{0,64},{16,80},{32,96},{48,112},{64,128},{80,144},{96,160},{112,17... | collective-permute-start | bytes 1572872 | tf_op jit(solution)/shard_map/ppermute | solution.py:330
  24.9 12.9 %collective-permute-start.4 = (bf16[4,128,512]{2,1,0:T(8,128)(2,1)S(1)}, bf16[4,128,512]{2,1,0:T(8,128)(2,1)S(1)}, u32[]{:S(2)}, u32[]{:S(2)}) collective-permute-start(bf16[4,128,512]{2,1,0:T(8,128)(2,1)S(1)} %pad_maximum_fusion.1), channel_id=1, source_target_pairs={{0,128},{16,144},{32,160},{48,176},{64,192},{80,208},{96,224},{112... | collective-permute-start | bytes 1572872 | tf_op jit(solution)/shard_map/ppermute | solution.py:330
  27.0 24.6 %collective-permute-start.5 = (bf16[4,128,512]{2,1,0:T(8,128)(2,1)S(1)}, bf16[4,128,512]{2,1,0:T(8,128)(2,1)S(1)}, u32[]{:S(2)}, u32[]{:S(2)}) collective-permute-start(bf16[4,128,512]{2,1,0:T(8,128)(2,1)S(1)} %pad_maximum_fusion.1), channel_id=1, source_target_pairs={{0,192},{16,208},{32,224},{48,240},{64,0},{80,16},{96,32},{112,48}... | collective-permute-start | bytes 1572872 | tf_op jit(solution)/shard_map/ppermute | solution.py:330
  52.4 1.6 copy-start.3
  54.0 28.1 %copy-start.16 = (f32[2]{0:T(128)S(1)}, f32[2]{0:T(128)}, u32[]{:S(2)}) copy-start(f32[2]{0:T(128)} %param.19) | copy-start | bytes 28
  82.1 2.2 %copy-start.2 = (bf16[2304,896]{1,0:T(8,128)(2,1)S(1)}, bf16[2304,896]{1,0:T(8,128)(2,1)}, u32[]{:S(2)}) copy-start(bf16[2304,896]{1,0:T(8,128)(2,1)} %fusion.1.w) | copy-start | bytes 12386308
  84.3 1.6 copy-start.5
  85.9 45.0 %copy-start.11 = (bf16[2304,2304]{1,0:T(8,128)(2,1)S(1)}, bf16[2304,2304]{1,0:T(8,128)(2,1)}, u32[]{:S(2)}) copy-start(bf16[2304,2304]{1,0:T(8,128)(2,1)} %all-gather.6.cloned.1.call-done) | copy-start | bytes 31850500
  85.9 45.0 %copy-start.14 = (bf16[2304,256]{1,0:T(8,128)(2,1)S(1)}, bf16[2304,256]{1,0:T(8,128)(2,1)}, u32[]{:S(2)}) copy-start(bf16[2304,256]{1,0:T(8,128)(2,1)} %param.17) | copy-start | bytes 3538948
  115.7 6.3 %collective-permute-start.6 = (bf16[2,128,256]{2,1,0:T(8,128)(2,1)S(1)}, bf16[2,128,256]{2,1,0:T(8,128)(2,1)S(1)}, u32[]{:S(2)}, u32[]{:S(2)}) collective-permute-start(bf16[2,128,256]{2,1,0:T(8,128)(2,1)S(1)} %get-tuple-element.17), channel_id=1, source_target_pairs={{0,16},{16,32},{32,48},{48,0},{64,80},{80,96},{96,112},{112,64},{1... | collective-permute-start | bytes 393224 | tf_op jit(solution)/shard_map/ppermute | solution.py:330
  117.2 10.1 %collective-permute-start.7 = (bf16[2,128,256]{2,1,0:T(8,128)(2,1)S(1)}, bf16[2,128,256]{2,1,0:T(8,128)(2,1)S(1)}, u32[]{:S(2)}, u32[]{:S(2)}) collective-permute-start(bf16[2,128,256]{2,1,0:T(8,128)(2,1)S(1)} %get-tuple-element.17), channel_id=1, source_target_pairs={{0,32},{16,48},{32,0},{48,16},{64,96},{80,112},{96,64},{112,80},{1... | collective-permute-start | bytes 393224 | tf_op jit(solution)/shard_map/ppermute | solution.py:330
  119.6 8.0 %collective-permute-start.8 = (bf16[2,128,256]{2,1,0:T(8,128)(2,1)S(1)}, bf16[2,128,256]{2,1,0:T(8,128)(2,1)S(1)}, u32[]{:S(2)}, u32[]{:S(2)}) collective-permute-start(bf16[2,128,256]{2,1,0:T(8,128)(2,1)S(1)} %get-tuple-element.17), channel_id=1, source_target_pairs={{0,48},{16,0},{32,16},{48,32},{64,112},{80,64},{96,80},{112,96},{1... | collective-permute-start | bytes 393224 | tf_op jit(solution)/shard_map/ppermute | solution.py:330
  128.4 13.1 %copy-start.4 = (f32[128]{0:T(128)S(1)}, f32[128]{0:T(128)}, u32[]{:S(2)}) copy-start(f32[128]{0:T(128)} %param.21) | copy-start | bytes 1540
  128.4 7.3 %collective-permute-start.9 = (bf16[2,128,256]{2,1,0:T(8,128)(2,1)S(1)}, bf16[2,128,256]{2,1,0:T(8,128)(2,1)S(1)}, u32[]{:S(2)}, u32[]{:S(2)}) collective-permute-start(bf16[2,128,256]{2,1,0:T(8,128)(2,1)S(1)} %get-tuple-element.19.own), channel_id=1, source_target_pairs={{0,64},{16,80},{32,96},{48,112},{64,128},{80,144},{96,160},{112,17... | collective-permute-start | bytes 393224 | tf_op jit(solution)/shard_map/ppermute | solution.py:330
  128.8 8.5 %collective-permute-start.10 = (bf16[2,128,256]{2,1,0:T(8,128)(2,1)S(1)}, bf16[2,128,256]{2,1,0:T(8,128)(2,1)S(1)}, u32[]{:S(2)}, u32[]{:S(2)}) collective-permute-start(bf16[2,128,256]{2,1,0:T(8,128)(2,1)S(1)} %get-tuple-element.19.own), channel_id=1, source_target_pairs={{0,128},{16,144},{32,160},{48,176},{64,192},{80,208},{96,224},{112... | collective-permute-start | bytes 393224 | tf_op jit(solution)/shard_map/ppermute | solution.py:330
  130.9 10.6 %collective-permute-start.11 = (bf16[2,128,256]{2,1,0:T(8,128)(2,1)S(1)}, bf16[2,128,256]{2,1,0:T(8,128)(2,1)S(1)}, u32[]{:S(2)}, u32[]{:S(2)}) collective-permute-start(bf16[2,128,256]{2,1,0:T(8,128)(2,1)S(1)} %get-tuple-element.19.own), channel_id=1, source_target_pairs={{0,192},{16,208},{32,224},{48,240},{64,0},{80,16},{96,32},{112,48}... | collective-permute-start | bytes 393224 | tf_op jit(solution)/shard_map/ppermute | solution.py:330
  144.9 30.3 %all-to-all-start = ((bf16[8,256,256]{2,1,0:T(8,128)(2,1)}), bf16[8,256,256]{2,1,0:T(8,128)(2,1)S(1)}, u32[]{:S(2)}, u32[]{:S(2)}) async-start(bf16[8,256,256]{2,1,0:T(8,128)(2,1)} %bitcast.14), calls=%async_computation | async-start | bytes 2097152 | tf_op jit(solution)/shard_map/all_to_all | solution.py:434
  175.3 1.0 copy-start.6
  177.6 3.7 %copy-start.1 = (bf16[2048,2304]{1,0:T(8,128)(2,1)S(1)}, bf16[2048,2304]{1,0:T(8,128)(2,1)}, u32[]{:S(2)}) copy-start(bf16[2048,2304]{1,0:T(8,128)(2,1)} %all-gather.4.cloned.1.call-done) | copy-start | bytes 28311556
  185.2 5.3 %collective-permute-start.12 = (bf16[128,2304]{1,0:T(8,128)(2,1)S(1)}, bf16[128,2304]{1,0:T(8,128)(2,1)S(1)}, u32[]{:S(2)}, u32[]{:S(2)}) collective-permute-start(bf16[128,2304]{1,0:T(8,128)(2,1)S(1)} %get-tuple-element.23), channel_id=1, source_target_pairs={{0,1},{1,0},{2,3},{3,2},{4,5},{5,4},{6,7},{7,6},{8,9},{9,8},{10,11... | collective-permute-start | bytes 1769480 | tf_op jit(solution)/shard_map/ppermute | solution.py:330
Sparse Core Ops, SparseCore 0:
  10.4 69.7 all-gather.5
  83.2 82.5 all-gather.3

commit v3 on v2

--- a/solution.py
+++ b/solution.py
@@ -57,14 +57,30 @@
     return out
 
 
-def delta_kernel(group, toks, ld, w, bias, z_out, y_out, x_out, low_out, proj, rate, held):
-    rows = jnp.concatenate([toks[j, :BLK] for j in range(group)], axis=0)
+def running(decay, ones):
+    high = decay.astype(BF)
+    rest = decay - high.astype(F32)
+    mid = rest.astype(BF)
+    low = (rest - mid.astype(F32)).astype(BF)
+    both = dot(jnp.concatenate([ones, ones], axis=1), jnp.concatenate([high, mid], axis=0))
+    return both + dot(ones, low)
+
+
+def unit(rows):
+    return rows * lax.rsqrt(jnp.sum(rows * rows, axis=-1, keepdims=True) + GUARD)
+
+
+def delta_kernel(
+    group, toks, ld, wk, wv, wb, bias, k_out, w_out, s_out, x_out, low_out, proj, rate, held
+):
+    first = pl.program_id(0) == 0
     lanes2 = 2 * BLK
-    for j in range(3):
-        proj[j] = dot(rows, w[:, j * lanes2 : (j + 1) * lanes2])
-    rate[...] = jax.nn.sigmoid(dot(rows, w[:, 3 * lanes2 :]) + bias[...])
-
-    @pl.when(pl.program_id(0) == 0)
+    rows = toks[...]
+    proj[0] = dot(rows, wk[...])
+    proj[1] = dot(rows, wv[...])
+    rate[...] = jax.nn.sigmoid(dot(rows, wb[...]) + bias[...])
+
+    @pl.when(first)
     def start():
         across, along = indices((BLK, lanes2))
         for h in range(2):
@@ -72,67 +88,49 @@
 
     row, col = indices((BLK, BLK))
     ones = (row >= col).astype(BF)
-    ones2 = jnp.concatenate([ones, ones], axis=1)
     pairs = []
     for blk in range(group):
         at = slice(blk * BLK, (blk + 1) * BLK)
         decay = ld[at, :]
-        high = decay.astype(BF)
-        rest = decay - high.astype(F32)
-        mid = rest.astype(BF)
-        low = (rest - mid.astype(F32)).astype(BF)
-        cum = dot(ones2, jnp.concatenate([high, mid], axis=0)) + dot(ones, low)
+        cum = running(decay, ones)
         for h in range(2):
             lanes = slice(h * BLK, (h + 1) * BLK)
             pairs.append((blk, at, h, lanes, cum[:, lanes]))
-    systems, targets, scores, ends, firsts, finals = [], [], [], [], [], []
+    systems, targets, ends, finals = [], [], [], []
     for blk, at, h, lanes, c in pairs:
-        q = proj[0, at, lanes]
-        k = proj[1, at, lanes]
-        v = proj[2, at, lanes]
-        q = q * lax.rsqrt(jnp.sum(q * q, axis=-1, keepdims=True) + GUARD)
-        k = k * lax.rsqrt(jnp.sum(k * k, axis=-1, keepdims=True) + GUARD)
+        k = unit(proj[0, at, lanes])
+        v = proj[1, at, lanes]
         beta = rate[at, h : h + 1]
         final = c[BLK - 1 : BLK, :]
         grow = jnp.exp(c)
         k_up = k * grow
-        q_up = q * grow
         k_down = (k * jnp.exp(-c)).astype(BF)
         k_end = k * jnp.exp(final - c)
-        gram = dot(jnp.concatenate([k_up, q_up], axis=0).astype(BF), k_down, ((1,), (1,)))
-        systems.append(jnp.where(row > col, beta * gram[:BLK], 0.0))
-        scores.append(jnp.where(row >= col, gram[BLK:], 0.0).astype(BF))
+        k_out[at, lanes] = k_down
+        gram = dot(k_up.astype(BF), k_down, ((1,), (1,)))
+        systems.append(jnp.where(row > col, beta * gram, 0.0))
         targets.append(jnp.concatenate([(beta * k_up).astype(BF), (beta * v).astype(BF)], axis=1))
         ends.append(k_end.T.astype(BF))
-        firsts.append(q_up)
         finals.append(jnp.exp(final))
     solved = inverses(systems, row, col)
     solved = [dot(t.astype(BF), g).astype(BF) for t, g in zip(solved, targets)]
-    earlier, rises, adds, maps = {}, {}, {}, {}
-    for (blk, at, h, lanes, c), w_, s, e, f, last in zip(pairs, solved, scores, ends, firsts, finals):
-        both = dot(jnp.concatenate([s, e], axis=0), w_)
-        p, o = f - both[:BLK, :BLK], both[:BLK, BLK:]
-        m, n = jnp.where(row == col, last, 0.0) - both[BLK:, :BLK], both[BLK:, BLK:]
-        if blk % 2 == 0:
-            earlier[h] = p.astype(BF), o, jnp.concatenate([m, n], axis=1)
-        else:
-            p0, o0, before = earlier[h]
-            seen = dot(p.astype(BF), before.astype(BF))
-            rises[blk // 2, h] = jnp.concatenate([p0, seen[:, :BLK].astype(BF)], axis=0)
-            adds[blk // 2, h] = jnp.concatenate([o0, seen[:, BLK:] + o], axis=0)
-            moved = compose(m, before)
-            maps[blk // 2, h] = moved[:, :BLK], moved[:, BLK:] + n
+    maps = {}
+    for (blk, at, h, lanes, c), w_, e, last in zip(pairs, solved, ends, finals):
+        w_out[blk, h] = w_
+        both = dot(e, w_)
+        m, n = jnp.where(row == col, last, 0.0) - both[:, :BLK], both[:, BLK:]
+        maps[blk, h] = m, n
+    joint = {}
+    for pair in range(group // 2):
+        for h in range(2):
+            joint[pair, h] = follow(maps[2 * pair + 1, h], jnp.concatenate(maps[2 * pair, h], axis=1))
     x = [held[h] for h in range(2)]
     for pair in range(group // 2):
-        at = slice(pair * lanes2, (pair + 1) * lanes2)
-        for h in range(2):
-            lanes = slice(h * BLK, (h + 1) * BLK)
-            both = dot(rises[pair, h], x[h].astype(BF))
-            z_out[at, lanes] = both[:, :BLK].astype(BF)
-            y_out[at, lanes] = both[:, BLK:] + adds[pair, h]
-            m, n = maps[pair, h]
-            moved = compose(m, x[h])
-            x[h] = jnp.concatenate([moved[:, :BLK], moved[:, BLK:] + n], axis=1)
+        for h in range(2):
+            s_out[2 * pair, h] = x[h].astype(BF)
+            s_out[2 * pair + 1, h] = follow(maps[2 * pair, h], x[h]).astype(BF)
+            m, n = joint[pair, h][:, :BLK], joint[pair, h][:, BLK:]
+            x[h] = follow((m, n), x[h])
     for h in range(2):
         held[h] = x[h]
         x_out[h] = x[h]
@@ -150,38 +148,84 @@
     return dot(left, jnp.concatenate([x_high, x_high], axis=0)) + dot(high, x_low)
 
 
-def delta_blocks(tokens, ld, weights, bias, group=4):
-    blocks, rows, width = tokens.shape
+def follow(step, x):
+    moved = compose(step[0], x)
+    return jnp.concatenate([moved[:, :BLK], moved[:, BLK:] + step[1]], axis=1)
+
+
+def delta_blocks(tokens, ld, wk, wv, wb, bias, group=4):
+    rows, width = tokens.shape
+    blocks = rows // BLK
     lanes = 2 * BLK
-    out = pl.BlockSpec((group * BLK, lanes), lambda i: (i, 0))
+    tall = pl.BlockSpec((group * BLK, lanes), lambda i: (i, 0))
+    square = pl.BlockSpec((group, 2, BLK, lanes), lambda i: (i, 0, 0, 0))
     last = pl.BlockSpec((2, BLK, lanes), lambda i: (0, 0, 0))
+    whole = lambda a: pl.BlockSpec(a.shape, lambda i: (0, 0))
     return pl.pallas_call(
         functools.partial(delta_kernel, group),
         grid=(blocks // group,),
         in_specs=[
-            pl.BlockSpec((group, rows, width), lambda i: (i, 0, 0)),
-            pl.BlockSpec((group * BLK, lanes), lambda i: (i, 0)),
-            pl.BlockSpec(memory_space=pltpu.VMEM),
-            pl.BlockSpec(memory_space=pltpu.VMEM),
+            pl.BlockSpec((group * BLK, width), lambda i: (i, 0)),
+            tall,
+            whole(wk),
+            whole(wv),
+            whole(wb),
+            whole(bias),
         ],
-        out_specs=[out, out, last, last],
+        out_specs=[tall, square, square, last, last],
         out_shape=[
-            jax.ShapeDtypeStruct((blocks * BLK, lanes), BF),
-            jax.ShapeDtypeStruct((blocks * BLK, lanes), F32),
+            jax.ShapeDtypeStruct((rows, lanes), BF),
+            jax.ShapeDtypeStruct((blocks, 2, BLK, lanes), BF),
+            jax.ShapeDtypeStruct((blocks, 2, BLK, lanes), BF),
             jax.ShapeDtypeStruct((2, BLK, lanes), F32),
             jax.ShapeDtypeStruct((2, BLK, lanes), BF),
         ],
         scratch_shapes=[
-            pltpu.VMEM((3, group * BLK, lanes), F32),
+            pltpu.VMEM((2, group * BLK, lanes), F32),
             pltpu.VMEM((group * BLK, BLK), F32),
             pltpu.VMEM((2, BLK, lanes), F32),
         ],
         compiler_params=pltpu.CompilerParams(vmem_limit_bytes=VMEM_BYTES),
         cost_estimate=pl.CostEstimate(
-            flops=blocks * BLK * 12 * 10**6, bytes_accessed=blocks * BLK * 12000, transcendentals=0
+            flops=rows * 12 * 10**6, bytes_accessed=rows * 12000, transcendentals=0
         ),
         name="delta_blocks",
-    )(tokens, ld, weights, bias)
+    )(tokens, ld, wk, wv, wb, bias)
+
+
+def rise_kernel(group, q, ld, k, w, s, z_out, y_out):
+    row, col = indices((BLK, BLK))
+    ones = (row >= col).astype(BF)
+    todo = [(j, h) for j in range(group) for h in range(2)]
+    places = [(slice(j * BLK, (j + 1) * BLK), slice(h * BLK, (h + 1) * BLK)) for j, h in todo]
+    grow = [jnp.exp(running(ld[j * BLK : (j + 1) * BLK], ones)) for j in range(group)]
+    ups = [unit(q[p]) * grow[j][:, p[1]] for p, (j, h) in zip(places, todo)]
+    grams = [dot(u.astype(BF), k[p], ((1,), (1,))) for u, p in zip(ups, places)]
+    grams = [jnp.where(row >= col, g, 0.0).astype(BF) for g in grams]
+    both = [dot(g, w[j, h]) for g, (j, h) in zip(grams, todo)]
+    rises = [(u - b[:, :BLK]).astype(BF) for u, b in zip(ups, both)]
+    for p, b, r, (j, h) in zip(places, both, rises, todo):
+        seen = dot(r, s[j, h])
+        z_out[p] = seen[:, :BLK].astype(BF)
+        y_out[p] = seen[:, BLK:] + b[:, BLK:]
+
+
+def rise(q, ld, k, w, s, group=4):
+    rows, lanes = q.shape
+    tall = pl.BlockSpec((group * BLK, lanes), lambda i: (i, 0))
+    square = pl.BlockSpec((group,) + w.shape[1:], lambda i: (i, 0, 0, 0))
+    return pl.pallas_call(
+        functools.partial(rise_kernel, group),
+        grid=(rows // (group * BLK),),
+        in_specs=[tall, tall, tall, square, square],
+        out_specs=[tall, tall],
+        out_shape=[jax.ShapeDtypeStruct((rows, lanes), BF), jax.ShapeDtypeStruct((rows, lanes), F32)],
+        compiler_params=pltpu.CompilerParams(vmem_limit_bytes=VMEM_BYTES),
+        cost_estimate=pl.CostEstimate(
+            flops=rows * 3 * 10**6, bytes_accessed=rows * 6000, transcendentals=0
+        ),
+        name="rise",
+    )(q, ld, k, w, s)
 
 
 def side_kernel(place, own, one, two, three, before, total, slots):
@@ -250,7 +294,7 @@
             lanes = slice(h * BLK, (h + 1) * BLK)
             a = y[at, lanes] + dot(z[at, lanes], state[h])
             scale = lax.rsqrt(jnp.mean(a * a, axis=-1, keepdims=True) + GUARD)
-            a = a * scale * gain[...] * jax.nn.sigmoid(gate[j, :BLK, lanes].astype(F32))
+            a = a * scale * gain[...] * jax.nn.sigmoid(gate[at, lanes].astype(F32))
             out[at, lanes] = a.astype(BF)
 
 
@@ -262,8 +306,7 @@
         grid=(z.shape[0] // (group * BLK),),
         in_specs=[pl.BlockSpec(memory_space=pltpu.SMEM)]
         + [small] * 5
-        + [tall] * 2
-        + [pl.BlockSpec((group,) + gate.shape[1:], lambda i: (i, 0, 0))]
+        + [tall] * 3
         + [pl.BlockSpec((1, BLK), lambda i: (0, 0))],
         out_specs=tall,
         out_shape=jax.ShapeDtypeStruct(z.shape, BF),
@@ -278,8 +321,7 @@
     parts, levels, rows, width = w.shape
     depth = parts * rows
     for i in range(levels):
-        at = pl.ds(pl.multiple_of(info[1 + i] * depth, depth), depth)
-        more = dot(a[:, at], w[:, i].reshape(depth, width))
+        more = dot(a[info[1 + i]], w[:, i].reshape(depth, width))
         total[...] = more if i == 0 else total[...] + more
     mine[...] = total[pl.ds(pl.multiple_of(core * BLK, BLK), BLK), :]
     theirs[...] = total[pl.ds(pl.multiple_of((1 - core) * BLK, BLK), BLK), :].astype(BF)
@@ -299,7 +341,9 @@
         out_shape=jax.ShapeDtypeStruct(array.shape, array.dtype),
         scratch_shapes=[pltpu.SemaphoreType.DMA(())],
         compiler_params=pltpu.CompilerParams(vmem_limit_bytes=16 * 1024 * 1024),
-        cost_estimate=pl.CostEstimate(flops=0, bytes_accessed=2 * array.size, transcendentals=0),
+        cost_estimate=pl.CostEstimate(
+            flops=10 * 10**9, bytes_accessed=4 * array.size, transcendentals=0
+        ),
         name="fetched",
     )(array)
 
@@ -311,7 +355,9 @@
         output_kernel,
         in_specs=[pl.BlockSpec(memory_space=pltpu.SMEM), here, here],
         out_specs=[here, here],
-        scratch_shapes=[pltpu.VMEM((2 * BLK, width), F32)],
+        scratch_shapes=[
+            pltpu.VMEM((2 * BLK, width), F32),
+        ],
         out_shape=[
             jax.ShapeDtypeStruct((BLK, width), F32),
             jax.ShapeDtypeStruct((BLK, width), BF),
@@ -340,6 +386,10 @@
 
 def across():
     return [(t, t ^ 1) for t in range(16)]
+
+
+def along_z(d):
+    return [(2 * z + k, 2 * ((z + d) % 8) + k) for z in range(8) for k in range(2)]
 
 
 def after(array, *others):
@@ -402,37 +452,42 @@
 ):
     ctx = lax.axis_index("ctx").astype(jnp.int32)
     tp = lax.axis_index("tp").astype(jnp.int32)
-    core = tp % 2
+    level, core = tp // 2, tp % 2
     spare = BLK - beta_weight.shape[1]
-    wide = BLK + 16
-
-    part = lax.dynamic_slice_in_dim(output_weight, ctx * 16, 16, 0)
-    gathered = lax.all_gather(jnp.concatenate([tokens, part], axis=0), "tp", axis=0)
-    weights = jnp.concatenate(
-        [query_weight, key_weight, values_projector_matrix, jnp.pad(beta_weight, ((0, 0), (0, spare)))],
-        axis=1,
-    )
+
+    gathered = lax.all_gather(tokens, "tp", axis=0, tiled=True)
+    rate_weight = jnp.pad(beta_weight, ((0, 0), (0, spare)))
     bias = jnp.pad(beta_bias, (0, spare))[None]
-    latent = after(latent_rows(tokens, kv_weight, kv_gain), weights)
+    latent = latent_rows(tokens, kv_weight, kv_gain)
     tiles = jnp.stack([latent] + [turn(latent, "ctx", along_y(d)) for d in (1, 2, 3)])
     tiles = jnp.concatenate([tiles] + [turn(tiles, "ctx", along_x(d)) for d in (1, 2, 3)])
     cache = picked(tiles, owner, ctx)
-    gathered = after(gathered, cache)
-    part = gathered.reshape(8, 2 * wide, -1)
-    part = lax.dynamic_slice_in_dim(part, core * wide + BLK, 16, 1).reshape(BLK, -1)
-    gathered = after(gathered, part)
+
+    part = lax.dynamic_slice_in_dim(output_weight, ctx * 16, 16, 0)
+    up, down = [part], [part]
+    for s in range(4):
+        up.append(turn(up[-1], "tp", along_z(1)))
+        if s < 3:
+            down.append(turn(down[-1], "tp", along_z(-1)))
+    part = jnp.concatenate(up + down[:0:-1], axis=0)
+    gathered = after(gathered, cache, part, rate_weight)
     all_parts = lax.all_gather(part, "ctx", axis=0, tiled=True)
     all_parts = all_parts.reshape(16, 8, 16, output_weight.shape[1])
 
-    z, y, maps, low = delta_blocks(gathered, log_decay, weights, bias)
-    received = [turn(low, "ctx", along_y(d)) for d in (1, 2, 3)]
-    before, total = side_maps((ctx % 4)[None], maps, received)
-    received = [turn(total, "ctx", along_x(d)) for d in (1, 2, 3)]
-    gate = dot(gathered, gate_weight, ((2,), (0,))).astype(BF)
-    normed = emit((ctx // 4)[None], before, total, received, z, y, gate, head_gain[None])
-
-    normed = lax.all_to_all(normed, "tp", 0, 1, tiled=True, axis_index_groups=SAME_CORE)
-    info = jnp.stack([core] + [jnp.int32(i) for i in range(8)])
+    fallen, solved, states, maps, low = delta_blocks(
+        gathered, log_decay, key_weight, values_projector_matrix, rate_weight, bias
+    )
+    z, y = rise(dot(gathered, query_weight), log_decay, fallen, solved, states)
+    two, one, three = [turn(low, "ctx", along_y(d)) for d in (2, 1, 3)]
+    before, total = side_maps((ctx % 4)[None], maps, (one, two, three))
+    two, one, three = [turn(total, "ctx", along_x(d)) for d in (2, 1, 3)]
+    gate = dot(gathered, gate_weight).astype(BF)
+    normed = emit((ctx // 4)[None], before, total, (one, two, three), z, y, gate, head_gain[None])
+
+    normed = lax.all_to_all(
+        normed.reshape(8, 2 * BLK, 2 * BLK), "tp", 0, 0, tiled=True, axis_index_groups=SAME_CORE
+    )
+    info = jnp.stack([core] + [(level + 8 - i) % 8 for i in range(8)])
     mine, theirs = output_rows(info, normed, fetched(all_parts))
     theirs = turn(theirs, "tp", across())
     return (mine + theirs.astype(F32)).astype(BF), cache

time: 202 us -> 190 us (0.941)
  waiting for transfers between devices: 90.9 us -> 69.7 us
  starting transfers between devices: 22.9 us -> 30.7 us
  matrix products: 3.49 us -> 5.81 us
    all_to_all x1, waiting for transfers between devices: 26 us -> 0.34 us  [body(): lax.all_to_all(normed.reshape(8, 2 * BLK, 2 * BLK), 'tp', 0, 0, tiled=Tru...]
    all_gather x1, waiting for transfers between devices: 0.02 us -> 20.8 us  [body(): all_parts = lax.all_gather(part, 'ctx', axis=0, tiled=True)]
    all_gather x1, waiting for transfers between devices: 24.2 us -> 7.79 us  [body(): gathered = lax.all_gather(tokens, 'tp', axis=0, tiled=True)]
    ppermute x13 -> x20, starting transfers between devices: 18.6 us -> 26.7 us  [turn(): return lax.ppermute(array, axis, pairs)]
    unnamed x41 -> x51, local copies, waits for them, and re-layouts: 16 us -> 20.2 us
    concatenate x2 -> x0, other arithmetic: 4.09 us -> none  [the longest x1 2.12 us: body(): jnp.concatenate([query_weight, key_weight, values_projector_matrix, jnp.p...]
    pallas_call x0 -> x1, Pallas kernels: none -> 3.19 us  [rise(): pl.pallas_call(functools.partial(rise_kernel, group), grid=(rows // (grou...]
    dynamic_slice x2 -> x0, local copies, waits for them, and re-layouts: 2.96 us -> none  [the longest x1 1.92 us: body(): lax.dynamic_slice_in_dim(part, core * wide + BLK, 16, 1).reshape(BLK, -1)]
  transfers between devices with their start and end apart: 16 -> 23, of which waited for: 13 -> 16; matrix products, arithmetic and copies ran while one was open for 7% -> 7% of each run, Pallas kernels for 18% -> 20%
where the time goes in v3:
time: 190 us; the launch traced here: 187 us
  waiting for transfers between devices  69.7 us (37%)
  Pallas kernels  41.6 us (22%)
  starting transfers between devices  30.7 us (16%)
  local copies, waits for them, and re-layouts  20.4 us (11%)
  between operations  14.4 us (8%)
  matrix products  5.81 us (3%)
  other arithmetic  4.63 us (2%)
    ppermute x20, waiting for transfers between devices, turn(): return lax.ppermute(array, axis, pairs)  40.1 us
    pallas_call x1, Pallas kernels, delta_blocks(): pl.pallas_call(functools.partial(delta_kernel, group), grid=(blocks // gr...  28.3 us
    ppermute x20, starting transfers between devices, turn(): return lax.ppermute(array, axis, pairs)  26.7 us
    all_gather x1, waiting for transfers between devices, body(): all_parts = lax.all_gather(part, 'ctx', axis=0, tiled=True)  20.8 us
    unnamed x51, local copies, waits for them, and re-layouts  20.2 us
    all_gather x1, waiting for transfers between devices, body(): gathered = lax.all_gather(tokens, 'tp', axis=0, tiled=True)  7.79 us
    dot_general x3, matrix products, dot(): lax.dot_general(a, b, (contract, ((), ())), preferred_element_type=F32)  5.81 us
    all_to_all x1, starting transfers between devices, body(): lax.all_to_all(normed.reshape(8, 2 * BLK, 2 * BLK), 'tp', 0, 0, tiled=Tru...  3.9 us
  transfers between devices with their start and end apart: 23, of which 16 were waited for; matrix products, arithmetic and copies ran while one was open for 7% of the time, Pallas kernels for 20%

profile of v3, /device:TPU:7, one launch (start us, length us, event | category | flops | bytes accessed | tf_op | source)
XLA Modules:
  0.0 187.2 jit_solution(4498046067105054993)
XLA Ops:
  7.2 0.7 all-gather.3.cloned.1.call-update
  8.0 1.0 constant_dynamic-update-slice_fusion.14
  9.0 1.7 collective-permute-start.6
  10.7 4.0 %collective-permute-start.10 = (bf16[16,2304]{1,0:T(8,128)(2,1)S(1)}, bf16[16,2304]{1,0:T(8,128)(2,1)S(1)}, u32[]{:S(2)}, u32[]{:S(2)}) collective-permute-start(bf16[16,2304]{1,0:T(8,128)(2,1)S(1)} %get-tuple-element.29), channel_id=1, source_target_pairs={{0,14},{1,15},{2,0},{3,1},{4,2},{5,3},{6,4},{7,5},{8,6},{9,7},{10,... | collective-permute-start | bytes 221192 | tf_op jit(solution)/shard_map/ppermute | solution.py:376
  14.7 1.7 collective-permute-done.6
  16.4 2.7 %collective-permute-start.11 = (bf16[16,2304]{1,0:T(8,128)(2,1)S(1)}, bf16[16,2304]{1,0:T(8,128)(2,1)S(1)}, u32[]{:S(2)}, u32[]{:S(2)}) collective-permute-start(bf16[16,2304]{1,0:T(8,128)(2,1)S(1)} %collective-permute-done.10), channel_id=1, source_target_pairs={{0,14},{1,15},{2,0},{3,1},{4,2},{5,3},{6,4},{7,5},{8,6},{9,7},{10,... | collective-permute-start | bytes 221192 | tf_op jit(solution)/shard_map/ppermute | solution.py:376
  19.1 1.6 collective-permute-done.7
  20.8 2.7 %collective-permute-start.12 = (bf16[16,2304]{1,0:T(8,128)(2,1)S(1)}, bf16[16,2304]{1,0:T(8,128)(2,1)S(1)}, u32[]{:S(2)}, u32[]{:S(2)}) collective-permute-start(bf16[16,2304]{1,0:T(8,128)(2,1)S(1)} %collective-permute-done.11), channel_id=1, source_target_pairs={{0,14},{1,15},{2,0},{3,1},{4,2},{5,3},{6,4},{7,5},{8,6},{9,7},{10,... | collective-permute-start | bytes 221192 | tf_op jit(solution)/shard_map/ppermute | solution.py:376
  23.5 1.6 collective-permute-done.8
  25.2 6.4 %collective-permute-done.9 = bf16[16,2304]{1,0:T(8,128)(2,1)S(1)} collective-permute-done((bf16[16,2304]{1,0:T(8,128)(2,1)S(1)}, bf16[16,2304]{1,0:T(8,128)(2,1)S(1)}, u32[]{:S(2)}, u32[]{:S(2)}) %collective-permute-start.9) | collective-permute-done | bytes 73760 | tf_op jit(solution)/shard_map/ppermute | solution.py:376
  31.7 0.8 copy-done.11
  32.5 0.6 multiply_reduce_fusion
  33.1 0.8 constant_dynamic-update-slice_fusion.6
  33.9 1.4 collective-permute-start
  35.3 2.6 %collective-permute-start.1 = (bf16[128,512]{1,0:T(8,128)(2,1)}, bf16[128,512]{1,0:T(8,128)(2,1)}, u32[]{:S(2)}, u32[]{:S(2)}) collective-permute-start(bf16[128,512]{1,0:T(8,128)(2,1)} %get-tuple-element.31), channel_id=1, source_target_pairs={{0,32},{16,48},{32,0},{48,16},{64,96},{80,112},{96,64},{112,80},{1... | collective-permute-start | bytes 393224 | tf_op jit(solution)/shard_map/ppermute | solution.py:376
  37.9 1.1 collective-permute-start.2
  39.0 0.2 convert_reduce_fusion
  39.2 0.2 select_reduce_fusion
  39.3 0.6 fusion.2
  39.9 0.4 copy.16
  40.3 0.1 pad.8.wb
  40.5 0.8 pad_add_fusion.info
  41.3 0.7 collective-permute-done.1
  42.0 0.4 collective-permute-done.2
  42.4 1.2 pad_maximum_fusion
  43.5 0.3 collective-permute-start.3
  43.8 2.1 %collective-permute-start.4 = (bf16[4,128,512]{2,1,0:T(8,128)(2,1)S(1)}, bf16[4,128,512]{2,1,0:T(8,128)(2,1)S(1)}, u32[]{:S(2)}, u32[]{:S(2)}) collective-permute-start(bf16[4,128,512]{2,1,0:T(8,128)(2,1)S(1)} %pad_maximum_fusion), channel_id=1, source_target_pairs={{0,128},{16,144},{32,160},{48,176},{64,192},{80,208},{96,224},{112... | collective-permute-start | bytes 1572872 | tf_op jit(solution)/shard_map/ppermute | solution.py:376
  45.9 0.9 constant_dynamic-update-slice_fusion.5
  46.9 0.9 constant_dynamic-update-slice_fusion.4
  47.8 0.9 constant_dynamic-update-slice_fusion.3
  48.7 3.3 %collective-permute-done.3 = bf16[4,128,512]{2,1,0:T(8,128)(2,1)S(1)} collective-permute-done((bf16[4,128,512]{2,1,0:T(8,128)(2,1)S(1)}, bf16[4,128,512]{2,1,0:T(8,128)(2,1)S(1)}, u32[]{:S(2)}, u32[]{:S(2)}) %collective-permute-start.3) | collective-permute-done | bytes 524320 | tf_op jit(solution)/shard_map/ppermute | solution.py:376
  52.1 1.4 collective-permute-done.4
  53.5 13.1 %collective-permute-done.5 = bf16[4,128,512]{2,1,0:T(8,128)(2,1)S(1)} collective-permute-done((bf16[4,128,512]{2,1,0:T(8,128)(2,1)S(1)}, bf16[4,128,512]{2,1,0:T(8,128)(2,1)S(1)}, u32[]{:S(2)}, u32[]{:S(2)}) %collective-permute-start.5) | collective-permute-done | bytes 524320 | tf_op jit(solution)/shard_map/ppermute | solution.py:376
  66.6 2.0 %picked.1 = bf16[4,128,512]{2,1,0:T(8,128)(2,1)} custom-call(s32[8]{0:T(128)S(1)} %pad_add_fusion.info, bf16[16,128,512]{2,1,0:T(8,128)(2,1)S(1)} %constant_dynamic-update-slice_fusion.tile), custom_call_target="tpu_custom_call" | custom-call | tf_op jit(solution)/shard_map/picked/pallas_call | solution.py:424
  68.5 7.8 %all-gather.3.cloned.1.call-done.toks = bf16[2048,2304]{1,0:T(8,128)(2,1)} async-done(((bf16[128,2304]{1,0:T(8,128)(2,1)}), bf16[2048,2304]{1,0:T(8,128)(2,1)}) %all-gather.3.cloned.1.call-update) | async-done | bytes 9437200 | tf_op jit(solution)/shard_map/all_gather | solution.py:458
  76.3 1.6 copy-done.6
  77.9 1.3 copy-done.8
  79.2 1.3 copy-done.9
  80.5 28.3 %delta_blocks.1 = (bf16[2048,256]{1,0:T(8,128)(2,1)S(1)}, bf16[16,2,128,256]{3,2,1,0:T(8,128)(2,1)S(1)}, bf16[16,2,128,256]{3,2,1,0:T(8,128)(2,1)S(1)}, f32[2,12...) custom-call(bf16[2048,2304]{1,0:T(8,128)(2,1)} %all-gather.3.cloned.1.call-done.toks, f32[2048,256]{1,0:T(8,128)S(1)} %copy-done.6, ...), custom_call_target="tpu_custom_call" | custom-call | flops 24576000000 | bytes 24576000 | tf_op jit(solution)/shard_map/delta_blocks/pallas_call | solution.py:164
  108.8 1.4 collective-permute-start.13
  110.1 2.5 %collective-permute-start.14 = (bf16[2,128,256]{2,1,0:T(8,128)(2,1)S(1)}, bf16[2,128,256]{2,1,0:T(8,128)(2,1)S(1)}, u32[]{:S(2)}, u32[]{:S(2)}) collective-permute-start(bf16[2,128,256]{2,1,0:T(8,128)(2,1)S(1)} %get-tuple-element.16), channel_id=1, source_target_pairs={{0,32},{16,48},{32,0},{48,16},{64,96},{80,112},{96,64},{112,80},{1... | collective-permute-start | bytes 393224 | tf_op jit(solution)/shard_map/ppermute | solution.py:376
  112.6 1.2 collective-permute-start.15
  113.8 2.6 %fusion.8.q = f32[2048,256]{1,0:T(8,128)S(1)} fusion(bf16[2048,2304]{1,0:T(8,128)(2,1)S(1)} %copy-done.14, bf16[2304,256]{1,0:T(8,128)(2,1)S(1)} %copy-done.15), kind=kOutput, calls=%fused_computation.49 | convolution fusion | flops 2415919104 | bytes 12713984 | tf_op jit(solution)/shard_map/dot_general | solution.py:17
  116.4 2.6 %convolution_convert_fusion.gate = bf16[2048,256]{1,0:T(8,128)(2,1)S(1)} fusion(bf16[2048,2304]{1,0:T(8,128)(2,1)S(1)} %copy-done.14, bf16[2304,256]{1,0:T(8,128)(2,1)S(1)} %copy-done.16), kind=kOutput, calls=%fused_computation | convolution fusion | flops 2416443392 | bytes 11665408 | tf_op jit(solution)/shard_map/dot_general | solution.py:17
  119.1 0.8 side_maps.1
  119.9 0.3 collective-permute-start.16
  120.2 2.1 %collective-permute-start.17 = (bf16[2,128,256]{2,1,0:T(8,128)(2,1)S(1)}, bf16[2,128,256]{2,1,0:T(8,128)(2,1)S(1)}, u32[]{:S(2)}, u32[]{:S(2)}) collective-permute-start(bf16[2,128,256]{2,1,0:T(8,128)(2,1)S(1)} %get-tuple-element.18.own), channel_id=1, source_target_pairs={{0,128},{16,144},{32,160},{48,176},{64,192},{80,208},{96,224},{112... | collective-permute-start | bytes 393224 | tf_op jit(solution)/shard_map/ppermute | solution.py:376
  122.3 3.2 %rise.1 = (bf16[2048,256]{1,0:T(8,128)(2,1)S(1)}, f32[2048,256]{1,0:T(8,128)S(1)}) custom-call(f32[2048,256]{1,0:T(8,128)S(1)} %fusion.8.q, f32[2048,256]{1,0:T(8,128)S(1)} %copy-done.7, bf16[2048,256]{1,0:T(8,128)(2,1)S(1)} %get-tuple-element.19.k, bf16[16,2,128,256]{3,2,1,0:T(8,128)(2,1)S(1)} %get-tuple-element.20.w, ...), custom_call_target="tpu_custom_call" | custom-call | flops 6144000000 | bytes 12288000 | tf_op jit(solution)/shard_map/rise/pallas_call | solution.py:217
  125.5 2.3 %collective-permute-done.16.one = bf16[2,128,256]{2,1,0:T(8,128)(2,1)S(1)} collective-permute-done((bf16[2,128,256]{2,1,0:T(8,128)(2,1)S(1)}, bf16[2,128,256]{2,1,0:T(8,128)(2,1)S(1)}, u32[]{:S(2)}, u32[]{:S(2)}) %collective-permute-start.16) | collective-permute-done | bytes 131104 | tf_op jit(solution)/shard_map/ppermute | solution.py:376
  127.9 1.6 collective-permute-done.17.two
  129.4 4.4 %collective-permute-done.18.three = bf16[2,128,256]{2,1,0:T(8,128)(2,1)S(1)} collective-permute-done((bf16[2,128,256]{2,1,0:T(8,128)(2,1)S(1)}, bf16[2,128,256]{2,1,0:T(8,128)(2,1)S(1)}, u32[]{:S(2)}, u32[]{:S(2)}) %collective-permute-start.18) | collective-permute-done | bytes 131104 | tf_op jit(solution)/shard_map/ppermute | solution.py:376
  133.8 3.4 %emit.1 = bf16[2048,256]{1,0:T(8,128)(2,1)} custom-call(s32[1]{0:T(128)} %bitcast.9.place, f32[2,128,256]{2,1,0:T(8,128)S(1)} %get-tuple-element.17.before, bf16[2,128,256]{2,1,0:T(8,128)(2,1)S(1)} %get-tuple-element.18.own, bf16[2,128,256]{2,1,0:T(8,128)(2,1)S(1)} %collective-permute-done.16.one, bf16[2,128,256]{2,1,0:T(8,128)(2,1)S(1)} %collective-permute-done.17.two, ...), custom_call_target="tpu_custom_call" | custom-call | tf_op jit(solution)/shard_map/emit/pallas_call | solution.py:304
  137.2 3.9 %all-to-all-start = ((bf16[8,256,256]{2,1,0:T(8,128)(2,1)}), bf16[8,256,256]{2,1,0:T(8,128)(2,1)S(1)}, u32[]{:S(2)}, u32[]{:S(2)}) async-start(bf16[8,256,256]{2,1,0:T(8,128)(2,1)} %bitcast.18), calls=%async_computation | async-start | bytes 2097152 | tf_op jit(solution)/shard_map/all_to_all | solution.py:487
  141.1 0.1 stack.54.info
  141.2 20.8 %all-gather.5.cloned.1.call-done = bf16[2048,2304]{1,0:T(8,128)(2,1)} async-done(((bf16[128,2304]{1,0:T(8,128)(2,1)}), bf16[2048,2304]{1,0:T(8,128)(2,1)}) %all-gather.5.cloned.1.call-update) | async-done | bytes 9437200 | tf_op jit(solution)/shard_map/all_gather | solution.py:474
  162.0 3.7 %copy-done.5 = bf16[2048,2304]{1,0:T(8,128)(2,1)S(1)} copy-done((bf16[2048,2304]{1,0:T(8,128)(2,1)S(1)}, bf16[2048,2304]{1,0:T(8,128)(2,1)}, u32[]{:S(2)}) %copy-start.5) | copy-done | bytes 9437208
  165.7 0.6 fetched.1.w
  166.3 3.6 %copy-done.1 = bf16[16,8,16,2304]{3,2,1,0:T(8,128)(2,1)} copy-done((bf16[16,8,16,2304]{3,2,1,0:T(8,128)(2,1)}, bf16[16,8,16,2304]{3,2,1,0:T(8,128)(2,1)S(1)}, u32[]{:S(2)}) %copy-start.1) | copy-done | bytes 9437208
  169.9 0.3 all-to-all-done.a
  170.3 3.7 %copy-done.2 = bf16[16,8,16,2304]{3,2,1,0:T(8,128)(2,1)S(1)} copy-done((bf16[16,8,16,2304]{3,2,1,0:T(8,128)(2,1)S(1)}, bf16[16,8,16,2304]{3,2,1,0:T(8,128)(2,1)}, u32[]{:S(2)}) %copy-start.2) | copy-done | bytes 9437208
  174.0 3.3 %output_rows.1 = (f32[128,2304]{1,0:T(8,128)S(1)}, bf16[128,2304]{1,0:T(8,128)(2,1)S(1)}) custom-call(s32[9]{0:T(128)S(1)} %stack.54.info, bf16[8,256,256]{2,1,0:T(8,128)(2,1)S(1)} %all-to-all-done.a, bf16[16,8,16,2304]{3,2,1,0:T(8,128)(2,1)S(1)} %copy-done.2), custom_call_target="tpu_custom_call" | custom-call | flops 2415919104 | bytes 9437184 | tf_op jit(solution)/shard_map/output_rows/pallas_call | solution.py:354
  177.3 0.6 collective-permute-start.19
  177.8 1.6 collective-permute-done.19
  179.5 0.9 add_convert_fusion
  (59 shorter events, 0.4 us)
Async XLA Ops:
  7.2 25.3 %copy-start = (bf16[2304,512]{1,0:T(8,128)(2,1)S(1)}, bf16[2304,512]{1,0:T(8,128)(2,1)}, u32[]{:S(2)}) copy-start(bf16[2304,512]{1,0:T(8,128)(2,1)} %param.23) | copy-start | bytes 7077892
  7.2 25.3 %copy-start.10 = (bf16[128,2304]{1,0:T(8,128)(2,1)S(1)}, bf16[128,2304]{1,0:T(8,128)(2,1)}, u32[]{:S(2)}) copy-start(bf16[128,2304]{1,0:T(8,128)(2,1)} %param.13) | copy-start | bytes 1769476
  7.2 69.1 %all-gather.3.cloned.1.call-start = ((), (), s32[]{:S(2)}) async-start(), calls=%async_computation.1 | async-start | bytes 10027008 | tf_op jit(solution)/shard_map/all_gather | solution.py:458
  7.9 154.1 %all-gather.5.cloned.1.call-start = ((), (), s32[]{:S(2)}) async-start(), calls=%async_computation.2 | async-start | bytes 10027008 | tf_op jit(solution)/shard_map/all_gather | solution.py:474
  9.0 7.4 %collective-permute-start.6 = (bf16[16,2304]{1,0:T(8,128)(2,1)S(1)}, bf16[16,2304]{1,0:T(8,128)(2,1)S(1)}, u32[]{:S(2)}, u32[]{:S(2)}) collective-permute-start(bf16[16,2304]{1,0:T(8,128)(2,1)S(1)} %get-tuple-element.29), channel_id=1, source_target_pairs={{0,2},{1,3},{2,4},{3,5},{4,6},{5,7},{6,8},{7,9},{8,10},{9,11},{10,... | collective-permute-start | bytes 221192 | tf_op jit(solution)/shard_map/ppermute | solution.py:376
  10.7 5.7 %collective-permute-start.10 = (bf16[16,2304]{1,0:T(8,128)(2,1)S(1)}, bf16[16,2304]{1,0:T(8,128)(2,1)S(1)}, u32[]{:S(2)}, u32[]{:S(2)}) collective-permute-start(bf16[16,2304]{1,0:T(8,128)(2,1)S(1)} %get-tuple-element.29), channel_id=1, source_target_pairs={{0,14},{1,15},{2,0},{3,1},{4,2},{5,3},{6,4},{7,5},{8,6},{9,7},{10,... | collective-permute-start | bytes 221192 | tf_op jit(solution)/shard_map/ppermute | solution.py:376
  16.4 4.4 %collective-permute-start.7 = (bf16[16,2304]{1,0:T(8,128)(2,1)S(1)}, bf16[16,2304]{1,0:T(8,128)(2,1)S(1)}, u32[]{:S(2)}, u32[]{:S(2)}) collective-permute-start(bf16[16,2304]{1,0:T(8,128)(2,1)S(1)} %collective-permute-done.6), channel_id=1, source_target_pairs={{0,2},{1,3},{2,4},{3,5},{4,6},{5,7},{6,8},{7,9},{8,10},{9,11},{10,... | collective-permute-start | bytes 221192 | tf_op jit(solution)/shard_map/ppermute | solution.py:376
  16.4 4.4 %collective-permute-start.11 = (bf16[16,2304]{1,0:T(8,128)(2,1)S(1)}, bf16[16,2304]{1,0:T(8,128)(2,1)S(1)}, u32[]{:S(2)}, u32[]{:S(2)}) collective-permute-start(bf16[16,2304]{1,0:T(8,128)(2,1)S(1)} %collective-permute-done.10), channel_id=1, source_target_pairs={{0,14},{1,15},{2,0},{3,1},{4,2},{5,3},{6,4},{7,5},{8,6},{9,7},{10,... | collective-permute-start | bytes 221192 | tf_op jit(solution)/shard_map/ppermute | solution.py:376
  20.8 4.4 %collective-permute-start.8 = (bf16[16,2304]{1,0:T(8,128)(2,1)S(1)}, bf16[16,2304]{1,0:T(8,128)(2,1)S(1)}, u32[]{:S(2)}, u32[]{:S(2)}) collective-permute-start(bf16[16,2304]{1,0:T(8,128)(2,1)S(1)} %collective-permute-done.7), channel_id=1, source_target_pairs={{0,2},{1,3},{2,4},{3,5},{4,6},{5,7},{6,8},{7,9},{8,10},{9,11},{10,... | collective-permute-start | bytes 221192 | tf_op jit(solution)/shard_map/ppermute | solution.py:376
  20.8 10.8 %collective-permute-start.12 = (bf16[16,2304]{1,0:T(8,128)(2,1)S(1)}, bf16[16,2304]{1,0:T(8,128)(2,1)S(1)}, u32[]{:S(2)}, u32[]{:S(2)}) collective-permute-start(bf16[16,2304]{1,0:T(8,128)(2,1)S(1)} %collective-permute-done.11), channel_id=1, source_target_pairs={{0,14},{1,15},{2,0},{3,1},{4,2},{5,3},{6,4},{7,5},{8,6},{9,7},{10,... | collective-permute-start | bytes 221192 | tf_op jit(solution)/shard_map/ppermute | solution.py:376
  25.2 6.4 %collective-permute-start.9 = (bf16[16,2304]{1,0:T(8,128)(2,1)S(1)}, bf16[16,2304]{1,0:T(8,128)(2,1)S(1)}, u32[]{:S(2)}, u32[]{:S(2)}) collective-permute-start(bf16[16,2304]{1,0:T(8,128)(2,1)S(1)} %collective-permute-done.8), channel_id=1, source_target_pairs={{0,2},{1,3},{2,4},{3,5},{4,6},{5,7},{6,8},{7,9},{8,10},{9,11},{10,... | collective-permute-start | bytes 221192 | tf_op jit(solution)/shard_map/ppermute | solution.py:376
  31.6 1.5 copy-start.13
  31.7 0.8 copy-start.11
  31.7 8.2 %copy-start.12 = (bf16[2304,2]{0,1:T(2,128)(2,1)S(1)}, bf16[2304,2]{0,1:T(2,128)(2,1)}, u32[]{:S(2)}) copy-start(bf16[2304,2]{0,1:T(2,128)(2,1)} %param.18) | copy-start | bytes 27652
  32.5 6.5 %copy-start.17 = (s32[16,1]{0,1:T(1,128)S(1)}, s32[16,1]{0,1:T(1,128)}, u32[]{:S(2)}) copy-start(s32[16,1]{0,1:T(1,128)} %param.25) | copy-start | bytes 196
  32.5 7.4 %copy-start.18 = (f32[2]{0:T(128)S(1)}, f32[2]{0:T(128)}, u32[]{:S(2)}) copy-start(f32[2]{0:T(128)} %param.19) | copy-start | bytes 28
  33.9 7.4 %collective-permute-start = (bf16[128,512]{1,0:T(8,128)(2,1)}, bf16[128,512]{1,0:T(8,128)(2,1)}, u32[]{:S(2)}, u32[]{:S(2)}) collective-permute-start(bf16[128,512]{1,0:T(8,128)(2,1)} %get-tuple-element.31), channel_id=1, source_target_pairs={{0,16},{16,32},{32,48},{48,0},{64,80},{80,96},{96,112},{112,64},{1... | collective-permute-start | bytes 393224 | tf_op jit(solution)/shard_map/ppermute | solution.py:376
  35.3 6.7 %collective-permute-start.1 = (bf16[128,512]{1,0:T(8,128)(2,1)}, bf16[128,512]{1,0:T(8,128)(2,1)}, u32[]{:S(2)}, u32[]{:S(2)}) collective-permute-start(bf16[128,512]{1,0:T(8,128)(2,1)} %get-tuple-element.31), channel_id=1, source_target_pairs={{0,32},{16,48},{32,0},{48,16},{64,96},{80,112},{96,64},{112,80},{1... | collective-permute-start | bytes 393224 | tf_op jit(solution)/shard_map/ppermute | solution.py:376
  37.9 4.4 %collective-permute-start.2 = (bf16[128,512]{1,0:T(8,128)(2,1)}, bf16[128,512]{1,0:T(8,128)(2,1)}, u32[]{:S(2)}, u32[]{:S(2)}) collective-permute-start(bf16[128,512]{1,0:T(8,128)(2,1)} %get-tuple-element.31), channel_id=1, source_target_pairs={{0,48},{16,0},{32,16},{48,32},{64,112},{80,64},{96,80},{112,96},{1... | collective-permute-start | bytes 393224 | tf_op jit(solution)/shard_map/ppermute | solution.py:376
  40.3 5.6 %copy-start.3 = (bf16[16,128,512]{2,1,0:T(8,128)(2,1)S(1)}, bf16[16,128,512]{2,1,0:T(8,128)(2,1)}, u32[]{:S(2)}) copy-start(bf16[16,128,512]{2,1,0:T(8,128)(2,1)} %get-tuple-element.30) | copy-start | bytes 6291460
  43.5 8.5 %collective-permute-start.3 = (bf16[4,128,512]{2,1,0:T(8,128)(2,1)S(1)}, bf16[4,128,512]{2,1,0:T(8,128)(2,1)S(1)}, u32[]{:S(2)}, u32[]{:S(2)}) collective-permute-start(bf16[4,128,512]{2,1,0:T(8,128)(2,1)S(1)} %pad_maximum_fusion), channel_id=1, source_target_pairs={{0,64},{16,80},{32,96},{48,112},{64,128},{80,144},{96,160},{112,17... | collective-permute-start | bytes 1572872 | tf_op jit(solution)/shard_map/ppermute | solution.py:376
  43.8 9.6 %collective-permute-start.4 = (bf16[4,128,512]{2,1,0:T(8,128)(2,1)S(1)}, bf16[4,128,512]{2,1,0:T(8,128)(2,1)S(1)}, u32[]{:S(2)}, u32[]{:S(2)}) collective-permute-start(bf16[4,128,512]{2,1,0:T(8,128)(2,1)S(1)} %pad_maximum_fusion), channel_id=1, source_target_pairs={{0,128},{16,144},{32,160},{48,176},{64,192},{80,208},{96,224},{112... | collective-permute-start | bytes 1572872 | tf_op jit(solution)/shard_map/ppermute | solution.py:376
  45.9 20.6 %collective-permute-start.5 = (bf16[4,128,512]{2,1,0:T(8,128)(2,1)S(1)}, bf16[4,128,512]{2,1,0:T(8,128)(2,1)S(1)}, u32[]{:S(2)}, u32[]{:S(2)}) collective-permute-start(bf16[4,128,512]{2,1,0:T(8,128)(2,1)S(1)} %pad_maximum_fusion), channel_id=1, source_target_pairs={{0,192},{16,208},{32,224},{48,240},{64,0},{80,16},{96,32},{112,48}... | collective-permute-start | bytes 1572872 | tf_op jit(solution)/shard_map/ppermute | solution.py:376
  76.3 1.6 copy-start.6
  77.9 1.3 copy-start.8
  79.2 1.3 copy-start.9
  80.5 33.3 %copy-start.14 = (bf16[2048,2304]{1,0:T(8,128)(2,1)S(1)}, bf16[2048,2304]{1,0:T(8,128)(2,1)}, u32[]{:S(2)}) copy-start(bf16[2048,2304]{1,0:T(8,128)(2,1)} %all-gather.3.cloned.1.call-done.toks) | copy-start | bytes 28311556
  80.5 33.3 %copy-start.15 = (bf16[2304,256]{1,0:T(8,128)(2,1)S(1)}, bf16[2304,256]{1,0:T(8,128)(2,1)}, u32[]{:S(2)}) copy-start(bf16[2304,256]{1,0:T(8,128)(2,1)} %param.14) | copy-start | bytes 3538948
  108.8 7.6 %copy-start.16 = (bf16[2304,256]{1,0:T(8,128)(2,1)S(1)}, bf16[2304,256]{1,0:T(8,128)(2,1)}, u32[]{:S(2)}) copy-start(bf16[2304,256]{1,0:T(8,128)(2,1)} %param.17) | copy-start | bytes 3538948
  108.8 10.3 %collective-permute-start.13 = (bf16[2,128,256]{2,1,0:T(8,128)(2,1)S(1)}, bf16[2,128,256]{2,1,0:T(8,128)(2,1)S(1)}, u32[]{:S(2)}, u32[]{:S(2)}) collective-permute-start(bf16[2,128,256]{2,1,0:T(8,128)(2,1)S(1)} %get-tuple-element.16), channel_id=1, source_target_pairs={{0,16},{16,32},{32,48},{48,0},{64,80},{80,96},{96,112},{112,64},{1... | collective-permute-start | bytes 393224 | tf_op jit(solution)/shard_map/ppermute | solution.py:376
  110.1 8.9 %collective-permute-start.14 = (bf16[2,128,256]{2,1,0:T(8,128)(2,1)S(1)}, bf16[2,128,256]{2,1,0:T(8,128)(2,1)S(1)}, u32[]{:S(2)}, u32[]{:S(2)}) collective-permute-start(bf16[2,128,256]{2,1,0:T(8,128)(2,1)S(1)} %get-tuple-element.16), channel_id=1, source_target_pairs={{0,32},{16,48},{32,0},{48,16},{64,96},{80,112},{96,64},{112,80},{1... | collective-permute-start | bytes 393224 | tf_op jit(solution)/shard_map/ppermute | solution.py:376
  112.6 6.5 %collective-permute-start.15 = (bf16[2,128,256]{2,1,0:T(8,128)(2,1)S(1)}, bf16[2,128,256]{2,1,0:T(8,128)(2,1)S(1)}, u32[]{:S(2)}, u32[]{:S(2)}) collective-permute-start(bf16[2,128,256]{2,1,0:T(8,128)(2,1)S(1)} %get-tuple-element.16), channel_id=1, source_target_pairs={{0,48},{16,0},{32,16},{48,32},{64,112},{80,64},{96,80},{112,96},{1... | collective-permute-start | bytes 393224 | tf_op jit(solution)/shard_map/ppermute | solution.py:376
  116.4 5.9 %copy-start.7 = (f32[2048,256]{1,0:T(8,128)S(1)}, f32[2048,256]{1,0:T(8,128)}, u32[]{:S(2)}) copy-start(f32[2048,256]{1,0:T(8,128)} %ld.3) | copy-start | bytes 6291460
  119.9 8.0 %collective-permute-start.16 = (bf16[2,128,256]{2,1,0:T(8,128)(2,1)S(1)}, bf16[2,128,256]{2,1,0:T(8,128)(2,1)S(1)}, u32[]{:S(2)}, u32[]{:S(2)}) collective-permute-start(bf16[2,128,256]{2,1,0:T(8,128)(2,1)S(1)} %get-tuple-element.18.own), channel_id=1, source_target_pairs={{0,64},{16,80},{32,96},{48,112},{64,128},{80,144},{96,160},{112,17... | collective-permute-start | bytes 393224 | tf_op jit(solution)/shard_map/ppermute | solution.py:376
  120.2 9.2 %collective-permute-start.17 = (bf16[2,128,256]{2,1,0:T(8,128)(2,1)S(1)}, bf16[2,128,256]{2,1,0:T(8,128)(2,1)S(1)}, u32[]{:S(2)}, u32[]{:S(2)}) collective-permute-start(bf16[2,128,256]{2,1,0:T(8,128)(2,1)S(1)} %get-tuple-element.18.own), channel_id=1, source_target_pairs={{0,128},{16,144},{32,160},{48,176},{64,192},{80,208},{96,224},{112... | collective-permute-start | bytes 393224 | tf_op jit(solution)/shard_map/ppermute | solution.py:376
  122.3 11.5 %collective-permute-start.18 = (bf16[2,128,256]{2,1,0:T(8,128)(2,1)S(1)}, bf16[2,128,256]{2,1,0:T(8,128)(2,1)S(1)}, u32[]{:S(2)}, u32[]{:S(2)}) collective-permute-start(bf16[2,128,256]{2,1,0:T(8,128)(2,1)S(1)} %get-tuple-element.18.own), channel_id=1, source_target_pairs={{0,192},{16,208},{32,224},{48,240},{64,0},{80,16},{96,32},{112,48}... | collective-permute-start | bytes 393224 | tf_op jit(solution)/shard_map/ppermute | solution.py:376
  122.3 11.5 %copy-start.4 = (f32[128]{0:T(128)S(1)}, f32[128]{0:T(128)}, u32[]{:S(2)}) copy-start(f32[128]{0:T(128)} %param.21) | copy-start | bytes 1540
  137.2 33.1 %all-to-all-start = ((bf16[8,256,256]{2,1,0:T(8,128)(2,1)}), bf16[8,256,256]{2,1,0:T(8,128)(2,1)S(1)}, u32[]{:S(2)}, u32[]{:S(2)}) async-start(bf16[8,256,256]{2,1,0:T(8,128)(2,1)} %bitcast.18), calls=%async_computation | async-start | bytes 2097152 | tf_op jit(solution)/shard_map/all_to_all | solution.py:487
  162.0 3.7 %copy-start.5 = (bf16[2048,2304]{1,0:T(8,128)(2,1)S(1)}, bf16[2048,2304]{1,0:T(8,128)(2,1)}, u32[]{:S(2)}) copy-start(bf16[2048,2304]{1,0:T(8,128)(2,1)} %all-gather.5.cloned.1.call-done) | copy-start | bytes 28311556
  166.3 3.6 %copy-start.1 = (bf16[16,8,16,2304]{3,2,1,0:T(8,128)(2,1)}, bf16[16,8,16,2304]{3,2,1,0:T(8,128)(2,1)S(1)}, u32[]{:S(2)}) copy-start(bf16[16,8,16,2304]{3,2,1,0:T(8,128)(2,1)S(1)} %fetched.1.w) | copy-start | bytes 28311556
  170.3 3.7 %copy-start.2 = (bf16[16,8,16,2304]{3,2,1,0:T(8,128)(2,1)S(1)}, bf16[16,8,16,2304]{3,2,1,0:T(8,128)(2,1)}, u32[]{:S(2)}) copy-start(bf16[16,8,16,2304]{3,2,1,0:T(8,128)(2,1)} %copy-done.1) | copy-start | bytes 28311556
  177.3 2.2 %collective-permute-start.19 = (bf16[128,2304]{1,0:T(8,128)(2,1)S(1)}, bf16[128,2304]{1,0:T(8,128)(2,1)S(1)}, u32[]{:S(2)}, u32[]{:S(2)}) collective-permute-start(bf16[128,2304]{1,0:T(8,128)(2,1)S(1)} %get-tuple-element.25), channel_id=1, source_target_pairs={{0,1},{1,0},{2,3},{3,2},{4,5},{5,4},{6,7},{7,6},{8,9},{9,8},{10,11... | collective-permute-start | bytes 1769480 | tf_op jit(solution)/shard_map/ppermute | solution.py:376
Sparse Core Ops, SparseCore 0:
  9.9 66.4 all-gather.2
  79.4 82.5 all-gather.4

commit v4 on v3

--- a/solution.py
+++ b/solution.py
@@ -10,7 +10,7 @@
 GUARD = 1e-06
 BF = jnp.bfloat16
 F32 = jnp.float32
-VMEM_BYTES = 36 * 1024 * 1024
+VMEM_BYTES = 24 * 1024 * 1024
 
 
 def dot(a, b, contract=((1,), (0,))):
@@ -71,14 +71,11 @@
 
 
 def delta_kernel(
-    group, toks, ld, wk, wv, wb, bias, k_out, w_out, s_out, x_out, low_out, proj, rate, held
+    group, proj, ld, bias, k_out, w_out, s_out, x_out, low_out, rate, held
 ):
     first = pl.program_id(0) == 0
     lanes2 = 2 * BLK
-    rows = toks[...]
-    proj[0] = dot(rows, wk[...])
-    proj[1] = dot(rows, wv[...])
-    rate[...] = jax.nn.sigmoid(dot(rows, wb[...]) + bias[...])
+    rate[...] = jax.nn.sigmoid(proj[:, 2 * lanes2 :] + bias[...])
 
     @pl.when(first)
     def start():
@@ -98,8 +95,8 @@
             pairs.append((blk, at, h, lanes, cum[:, lanes]))
     systems, targets, ends, finals = [], [], [], []
     for blk, at, h, lanes, c in pairs:
-        k = unit(proj[0, at, lanes])
-        v = proj[1, at, lanes]
+        k = unit(proj[at, lanes])
+        v = proj[at, lanes2 + h * BLK : lanes2 + (h + 1) * BLK]
         beta = rate[at, h : h + 1]
         final = c[BLK - 1 : BLK, :]
         grow = jnp.exp(c)
@@ -153,24 +150,20 @@
     return jnp.concatenate([moved[:, :BLK], moved[:, BLK:] + step[1]], axis=1)
 
 
-def delta_blocks(tokens, ld, wk, wv, wb, bias, group=4):
-    rows, width = tokens.shape
+def delta_blocks(projected, ld, bias, group=4):
+    rows, width = projected.shape
     blocks = rows // BLK
     lanes = 2 * BLK
     tall = pl.BlockSpec((group * BLK, lanes), lambda i: (i, 0))
     square = pl.BlockSpec((group, 2, BLK, lanes), lambda i: (i, 0, 0, 0))
     last = pl.BlockSpec((2, BLK, lanes), lambda i: (0, 0, 0))
-    whole = lambda a: pl.BlockSpec(a.shape, lambda i: (0, 0))
     return pl.pallas_call(
         functools.partial(delta_kernel, group),
         grid=(blocks // group,),
         in_specs=[
             pl.BlockSpec((group * BLK, width), lambda i: (i, 0)),
             tall,
-            whole(wk),
-            whole(wv),
-            whole(wb),
-            whole(bias),
+            pl.BlockSpec(bias.shape, lambda i: (0, 0)),
         ],
         out_specs=[tall, square, square, last, last],
         out_shape=[
@@ -181,7 +174,6 @@
             jax.ShapeDtypeStruct((2, BLK, lanes), BF),
         ],
         scratch_shapes=[
-            pltpu.VMEM((2, group * BLK, lanes), F32),
             pltpu.VMEM((group * BLK, BLK), F32),
             pltpu.VMEM((2, BLK, lanes), F32),
         ],
@@ -190,7 +182,7 @@
             flops=rows * 12 * 10**6, bytes_accessed=rows * 12000, transcendentals=0
         ),
         name="delta_blocks",
-    )(tokens, ld, wk, wv, wb, bias)
+    )(projected, ld, bias)
 
 
 def rise_kernel(group, q, ld, k, w, s, z_out, y_out):
@@ -327,27 +319,6 @@
     theirs[...] = total[pl.ds(pl.multiple_of((1 - core) * BLK, BLK), BLK), :].astype(BF)
 
 
-def fetch_kernel(far, near, sem):
-    copy = pltpu.make_async_copy(far, near, sem)
-    copy.start()
-    copy.wait()
-
-
-def fetched(array):
-    return pl.pallas_call(
-        fetch_kernel,
-        in_specs=[pl.BlockSpec(memory_space=pl.ANY)],
-        out_specs=pl.BlockSpec(memory_space=pltpu.VMEM),
-        out_shape=jax.ShapeDtypeStruct(array.shape, array.dtype),
-        scratch_shapes=[pltpu.SemaphoreType.DMA(())],
-        compiler_params=pltpu.CompilerParams(vmem_limit_bytes=16 * 1024 * 1024),
-        cost_estimate=pl.CostEstimate(
-            flops=10 * 10**9, bytes_accessed=4 * array.size, transcendentals=0
-        ),
-        name="fetched",
-    )(array)
-
-
 def output_rows(info, normed, weight):
     parts, levels, rows, width = weight.shape
     here = pl.BlockSpec(memory_space=pltpu.VMEM)
@@ -378,6 +349,10 @@
 
 def along_y(d):
     return [(4 * x + y, 4 * x + (y + d) % 4) for x in range(4) for y in range(4)]
+
+
+def down_x(d):
+    return [(4 * x + y, 4 * (x + d) + y) for x in range(4 - d) for y in range(4)]
 
 
 def along_x(d):
@@ -457,6 +432,7 @@
 
     gathered = lax.all_gather(tokens, "tp", axis=0, tiled=True)
     rate_weight = jnp.pad(beta_weight, ((0, 0), (0, spare)))
+    weights = jnp.concatenate([key_weight, values_projector_matrix, rate_weight], axis=1)
     bias = jnp.pad(beta_bias, (0, spare))[None]
     latent = latent_rows(tokens, kv_weight, kv_gain)
     tiles = jnp.stack([latent] + [turn(latent, "ctx", along_y(d)) for d in (1, 2, 3)])
@@ -470,17 +446,15 @@
         if s < 3:
             down.append(turn(down[-1], "tp", along_z(-1)))
     part = jnp.concatenate(up + down[:0:-1], axis=0)
-    gathered = after(gathered, cache, part, rate_weight)
+    gathered = after(gathered, cache, part, weights)
     all_parts = lax.all_gather(part, "ctx", axis=0, tiled=True)
     all_parts = all_parts.reshape(16, 8, 16, output_weight.shape[1])
 
-    fallen, solved, states, maps, low = delta_blocks(
-        gathered, log_decay, key_weight, values_projector_matrix, rate_weight, bias
-    )
+    fallen, solved, states, maps, low = delta_blocks(dot(gathered, weights), log_decay, bias)
     z, y = rise(dot(gathered, query_weight), log_decay, fallen, solved, states)
     two, one, three = [turn(low, "ctx", along_y(d)) for d in (2, 1, 3)]
     before, total = side_maps((ctx % 4)[None], maps, (one, two, three))
-    two, one, three = [turn(total, "ctx", along_x(d)) for d in (2, 1, 3)]
+    two, one, three = [turn(total, "ctx", down_x(d)) for d in (2, 1, 3)]
     gate = dot(gathered, gate_weight).astype(BF)
     normed = emit((ctx // 4)[None], before, total, (one, two, three), z, y, gate, head_gain[None])
 
@@ -488,7 +462,7 @@
         normed.reshape(8, 2 * BLK, 2 * BLK), "tp", 0, 0, tiled=True, axis_index_groups=SAME_CORE
     )
     info = jnp.stack([core] + [(level + 8 - i) % 8 for i in range(8)])
-    mine, theirs = output_rows(info, normed, fetched(all_parts))
+    mine, theirs = output_rows(info, normed, all_parts)
     theirs = turn(theirs, "tp", across())
     return (mine + theirs.astype(F32)).astype(BF), cache
 

time: 190 us -> 186 us (0.979); the launches traced: 187 us -> 186 us
  Pallas kernels: 41.6 us -> 29.2 us
  matrix products: 5.81 us -> 17 us
  waiting for transfers between devices: 69.7 us -> 78.9 us
  local copies, waits for them, and re-layouts: 20.4 us -> 12.1 us
  other arithmetic: 4.63 us -> 2.18 us
    pallas_call x1, Pallas kernels: 28.3 us -> 16.5 us  [delta_blocks(): pl.pallas_call(functools.partial(delta_kernel, group), grid=(blocks // gr...]
    dot_general x3 -> x4, matrix products: 5.81 us -> 17 us  [dot(): lax.dot_general(a, b, (contract, ((), ())), preferred_element_type=F32)]
    unnamed x51 -> x45, local copies, waits for them, and re-layouts: 20.2 us -> 11.2 us
    all_to_all x1, waiting for transfers between devices: 0.34 us -> 7.27 us  [body(): lax.all_to_all(normed.reshape(8, 2 * BLK, 2 * BLK), 'tp', 0, 0, tiled=Tru...]
    ppermute x20, waiting for transfers between devices: 40.1 us -> 42.5 us  [turn(): return lax.ppermute(array, axis, pairs)]
  transfers between devices with their start and end apart: 23 -> 23, of which waited for: 16 -> 16; matrix products, arithmetic and copies ran while one was open for 7% -> 13% of each run, Pallas kernels for 20% -> 14%
where the time goes in v4:
time: 186 us
  waiting for transfers between devices  78.9 us (42%)
  starting transfers between devices  32.1 us (17%)
  Pallas kernels  29.2 us (16%)
  matrix products  17 us (9%)
  between operations  14.4 us (8%)
  local copies, waits for them, and re-layouts  12.1 us (7%)
  other arithmetic  2.18 us (1%)
    ppermute x20, waiting for transfers between devices, turn(): return lax.ppermute(array, axis, pairs)  42.5 us
    ppermute x20, starting transfers between devices, turn(): return lax.ppermute(array, axis, pairs)  28.2 us
    all_gather x1, waiting for transfers between devices, body(): all_parts = lax.all_gather(part, 'ctx', axis=0, tiled=True)  21.8 us
    dot_general x4, matrix products, dot(): lax.dot_general(a, b, (contract, ((), ())), preferred_element_type=F32)  17 us
    pallas_call x1, Pallas kernels, delta_blocks(): pl.pallas_call(functools.partial(delta_kernel, group), grid=(blocks // gr...  16.5 us
    unnamed x45, local copies, waits for them, and re-layouts  11.2 us
    all_to_all x1, waiting for transfers between devices, body(): lax.all_to_all(normed.reshape(8, 2 * BLK, 2 * BLK), 'tp', 0, 0, tiled=Tru...  7.27 us
    all_gather x1, waiting for transfers between devices, body(): gathered = lax.all_gather(tokens, 'tp', axis=0, tiled=True)  6.6 us
  transfers between devices with their start and end apart: 23, of which 16 were waited for; matrix products, arithmetic and copies ran while one was open for 13% of the time, Pallas kernels for 14%

profile of v4, /device:TPU:7, one launch (start us, length us, event | category | flops | bytes accessed | tf_op | source)
XLA Modules:
  0.0 185.9 jit_solution(9114467817019547304)
XLA Ops:
  7.2 0.0 all-gather.3.cloned.1.call-start
  7.2 0.7 all-gather.3.cloned.1.call-update
  7.9 0.0 all-gather.5.cloned.1.call-start
  8.0 1.0 constant_dynamic-update-slice_fusion.14
  9.0 1.7 collective-permute-start.6
  10.7 4.0 %collective-permute-start.10 = (bf16[16,2304]{1,0:T(8,128)(2,1)S(1)}, bf16[16,2304]{1,0:T(8,128)(2,1)S(1)}, u32[]{:S(2)}, u32[]{:S(2)}) collective-permute-start(bf16[16,2304]{1,0:T(8,128)(2,1)S(1)} %get-tuple-element.29), channel_id=1, source_target_pairs={{0,14},{1,15},{2,0},{3,1},{4,2},{5,3},{6,4},{7,5},{8,6},{9,7},{10,... | collective-permute-start | bytes 221192 | tf_op jit(solution)/shard_map/ppermute | solution.py:347
  14.7 1.7 collective-permute-done.6
  16.4 2.7 %collective-permute-start.11 = (bf16[16,2304]{1,0:T(8,128)(2,1)S(1)}, bf16[16,2304]{1,0:T(8,128)(2,1)S(1)}, u32[]{:S(2)}, u32[]{:S(2)}) collective-permute-start(bf16[16,2304]{1,0:T(8,128)(2,1)S(1)} %collective-permute-done.10), channel_id=1, source_target_pairs={{0,14},{1,15},{2,0},{3,1},{4,2},{5,3},{6,4},{7,5},{8,6},{9,7},{10,... | collective-permute-start | bytes 221192 | tf_op jit(solution)/shard_map/ppermute | solution.py:347
  19.1 1.6 collective-permute-done.7
  20.8 2.7 %collective-permute-start.12 = (bf16[16,2304]{1,0:T(8,128)(2,1)S(1)}, bf16[16,2304]{1,0:T(8,128)(2,1)S(1)}, u32[]{:S(2)}, u32[]{:S(2)}) collective-permute-start(bf16[16,2304]{1,0:T(8,128)(2,1)S(1)} %collective-permute-done.11), channel_id=1, source_target_pairs={{0,14},{1,15},{2,0},{3,1},{4,2},{5,3},{6,4},{7,5},{8,6},{9,7},{10,... | collective-permute-start | bytes 221192 | tf_op jit(solution)/shard_map/ppermute | solution.py:347
  23.5 1.6 collective-permute-done.8
  25.2 6.4 %collective-permute-done.9 = bf16[16,2304]{1,0:T(8,128)(2,1)S(1)} collective-permute-done((bf16[16,2304]{1,0:T(8,128)(2,1)S(1)}, bf16[16,2304]{1,0:T(8,128)(2,1)S(1)}, u32[]{:S(2)}, u32[]{:S(2)}) %collective-permute-start.9) | collective-permute-done | bytes 73760 | tf_op jit(solution)/shard_map/ppermute | solution.py:347
  31.7 0.8 copy-done.6
  32.5 0.6 multiply_reduce_fusion
  33.1 0.8 constant_dynamic-update-slice_fusion.6
  33.9 1.4 collective-permute-start
  35.3 2.6 %collective-permute-start.1 = (bf16[128,512]{1,0:T(8,128)(2,1)S(1)}, bf16[128,512]{1,0:T(8,128)(2,1)S(1)}, u32[]{:S(2)}, u32[]{:S(2)}) collective-permute-start(bf16[128,512]{1,0:T(8,128)(2,1)S(1)} %get-tuple-element.31), channel_id=1, source_target_pairs={{0,32},{16,48},{32,0},{48,16},{64,96},{80,112},{96,64},{112,80},{1... | collective-permute-start | bytes 393224 | tf_op jit(solution)/shard_map/ppermute | solution.py:347
  37.9 1.1 collective-permute-start.2
  39.0 0.2 convert_reduce_fusion
  39.1 0.2 select_reduce_fusion
  39.4 0.4 copy.17
  39.8 0.1 pad_add_fusion.info
  39.8 1.9 collective-permute-done.1
  41.7 0.4 collective-permute-done.2
  42.1 0.1 pad_maximum_fusion
  42.2 0.3 collective-permute-start.3
  42.5 2.1 %collective-permute-start.4 = (bf16[4,128,512]{2,1,0:T(8,128)(2,1)S(1)}, bf16[4,128,512]{2,1,0:T(8,128)(2,1)S(1)}, u32[]{:S(2)}, u32[]{:S(2)}) collective-permute-start(bf16[4,128,512]{2,1,0:T(8,128)(2,1)S(1)} %pad_maximum_fusion), channel_id=1, source_target_pairs={{0,128},{16,144},{32,160},{48,176},{64,192},{80,208},{96,224},{112... | collective-permute-start | bytes 1572872 | tf_op jit(solution)/shard_map/ppermute | solution.py:347
  44.6 0.7 constant_dynamic-update-slice_fusion.5
  45.3 0.7 constant_dynamic-update-slice_fusion.4
  45.9 0.7 constant_dynamic-update-slice_fusion.3
  46.6 4.1 %collective-permute-done.3 = bf16[4,128,512]{2,1,0:T(8,128)(2,1)S(1)} collective-permute-done((bf16[4,128,512]{2,1,0:T(8,128)(2,1)S(1)}, bf16[4,128,512]{2,1,0:T(8,128)(2,1)S(1)}, u32[]{:S(2)}, u32[]{:S(2)}) %collective-permute-start.3) | collective-permute-done | bytes 524320 | tf_op jit(solution)/shard_map/ppermute | solution.py:347
  50.7 0.9 constant_dynamic-update-slice_fusion.2
  51.5 0.6 collective-permute-done.4
  52.1 0.8 constant_dynamic-update-slice_fusion.1
  52.9 12.4 %collective-permute-done.5 = bf16[4,128,512]{2,1,0:T(8,128)(2,1)S(1)} collective-permute-done((bf16[4,128,512]{2,1,0:T(8,128)(2,1)S(1)}, bf16[4,128,512]{2,1,0:T(8,128)(2,1)S(1)}, u32[]{:S(2)}, u32[]{:S(2)}) %collective-permute-start.5) | collective-permute-done | bytes 524320 | tf_op jit(solution)/shard_map/ppermute | solution.py:347
  65.3 0.8 constant_dynamic-update-slice_fusion.tile
  66.2 1.6 copy-done.2
  67.8 2.0 %picked.1 = bf16[4,128,512]{2,1,0:T(8,128)(2,1)} custom-call(s32[8]{0:T(128)S(1)} %pad_add_fusion.info, bf16[16,128,512]{2,1,0:T(8,128)(2,1)S(1)} %copy-done.2), custom_call_target="tpu_custom_call" | custom-call | tf_op jit(solution)/shard_map/picked/pallas_call | solution.py:399
  69.7 6.6 %all-gather.3.cloned.1.call-done = bf16[2048,2304]{1,0:T(8,128)(2,1)} async-done(((bf16[128,2304]{1,0:T(8,128)(2,1)}), bf16[2048,2304]{1,0:T(8,128)(2,1)}) %all-gather.3.cloned.1.call-update) | async-done | bytes 9437200 | tf_op jit(solution)/shard_map/all_gather | solution.py:433
  76.3 10.9 %fusion.10.proj = f32[2048,640]{1,0:T(8,128)S(1)} fusion(bf16[2048,2304]{1,0:T(8,128)(2,1)} %all-gather.3.cloned.1.call-done, bf16[2304,2]{1,0:T(8,128)(2,1)S(1)} %copy.17, bf16[2304,256]{1,0:T(8,128)(2,1)} %param.16, bf16[2304,256]{1,0:T(8,128)(2,1)} %param.15), kind=kOutput, calls=%fused_computation.52 | convolution fusion | flops 6051594240 | bytes 17048576 | tf_op jit(solution)/shard_map/dot_general | solution.py:17
  87.3 16.5 %delta_blocks.1 = (bf16[2048,256]{1,0:T(8,128)(2,1)S(1)}, bf16[16,2,128,256]{3,2,1,0:T(8,128)(2,1)S(1)}, bf16[16,2,128,256]{3,2,1,0:T(8,128)(2,1)S(1)}, f32[2,12...) custom-call(f32[2048,640]{1,0:T(8,128)S(1)} %fusion.10.proj, f32[2048,256]{1,0:T(8,128)S(1)} %copy-done.4, ...), custom_call_target="tpu_custom_call" | custom-call | flops 24576000000 | bytes 24576000 | tf_op jit(solution)/shard_map/delta_blocks/pallas_call | solution.py:160
  103.8 1.4 collective-permute-start.13
  105.2 2.5 %collective-permute-start.14 = (bf16[2,128,256]{2,1,0:T(8,128)(2,1)S(1)}, bf16[2,128,256]{2,1,0:T(8,128)(2,1)S(1)}, u32[]{:S(2)}, u32[]{:S(2)}) collective-permute-start(bf16[2,128,256]{2,1,0:T(8,128)(2,1)S(1)} %get-tuple-element.16), channel_id=1, source_target_pairs={{0,32},{16,48},{32,0},{48,16},{64,96},{80,112},{96,64},{112,80},{1... | collective-permute-start | bytes 393224 | tf_op jit(solution)/shard_map/ppermute | solution.py:347
  107.6 1.2 collective-permute-start.15
  108.8 2.8 %fusion.12.q = f32[2048,256]{1,0:T(8,128)S(1)} fusion(bf16[2048,2304]{1,0:T(8,128)(2,1)S(1)} %bitcast.40, bf16[2304,256]{1,0:T(8,128)(2,1)S(1)} %copy-done.9), kind=kOutput, calls=%fused_computation.53 | convolution fusion | flops 2415919104 | bytes 12713984 | tf_op jit(solution)/shard_map/dot_general | solution.py:17
  111.6 2.8 %convolution_convert_fusion.gate = bf16[2048,256]{1,0:T(8,128)(2,1)S(1)} fusion(bf16[2048,2304]{1,0:T(8,128)(2,1)S(1)} %bitcast.40, bf16[2304,256]{1,0:T(8,128)(2,1)S(1)} %copy-done.10), kind=kOutput, calls=%fused_computation.3 | convolution fusion | flops 2416443392 | bytes 11665408 | tf_op jit(solution)/shard_map/dot_general | solution.py:17
  114.4 0.8 side_maps.1
  115.3 1.3 collective-permute-start.16
  116.6 1.3 collective-permute-start.17
  117.9 1.3 collective-permute-start.18
  119.2 3.2 %rise.1 = (bf16[2048,256]{1,0:T(8,128)(2,1)S(1)}, f32[2048,256]{1,0:T(8,128)S(1)}) custom-call(f32[2048,256]{1,0:T(8,128)S(1)} %fusion.12.q, f32[2048,256]{1,0:T(8,128)S(1)} %copy-done.4, bf16[2048,256]{1,0:T(8,128)(2,1)S(1)} %get-tuple-element.19.k, bf16[16,2,128,256]{3,2,1,0:T(8,128)(2,1)S(1)} %get-tuple-element.20.w, ...), custom_call_target="tpu_custom_call" | custom-call | flops 6144000000 | bytes 12288000 | tf_op jit(solution)/shard_map/rise/pallas_call | solution.py:209
  122.4 2.2 %collective-permute-done.16.one = bf16[2,128,256]{2,1,0:T(8,128)(2,1)S(1)} collective-permute-done((bf16[2,128,256]{2,1,0:T(8,128)(2,1)S(1)}, bf16[2,128,256]{2,1,0:T(8,128)(2,1)S(1)}, u32[]{:S(2)}, u32[]{:S(2)}) %collective-permute-start.16) | collective-permute-done | bytes 131104 | tf_op jit(solution)/shard_map/ppermute | solution.py:347
  124.6 3.2 %collective-permute-done.17.two = bf16[2,128,256]{2,1,0:T(8,128)(2,1)S(1)} collective-permute-done((bf16[2,128,256]{2,1,0:T(8,128)(2,1)S(1)}, bf16[2,128,256]{2,1,0:T(8,128)(2,1)S(1)}, u32[]{:S(2)}, u32[]{:S(2)}) %collective-permute-start.17) | collective-permute-done | bytes 131104 | tf_op jit(solution)/shard_map/ppermute | solution.py:347
  127.7 4.8 %collective-permute-done.18.three = bf16[2,128,256]{2,1,0:T(8,128)(2,1)S(1)} collective-permute-done((bf16[2,128,256]{2,1,0:T(8,128)(2,1)S(1)}, bf16[2,128,256]{2,1,0:T(8,128)(2,1)S(1)}, u32[]{:S(2)}, u32[]{:S(2)}) %collective-permute-start.18) | collective-permute-done | bytes 131104 | tf_op jit(solution)/shard_map/ppermute | solution.py:347
  132.5 3.4 %emit.1 = bf16[2048,256]{1,0:T(8,128)(2,1)} custom-call(s32[1]{0:T(128)} %bitcast.9.place, f32[2,128,256]{2,1,0:T(8,128)S(1)} %get-tuple-element.17.before, bf16[2,128,256]{2,1,0:T(8,128)(2,1)S(1)} %get-tuple-element.18.own, bf16[2,128,256]{2,1,0:T(8,128)(2,1)S(1)} %collective-permute-done.16.one, bf16[2,128,256]{2,1,0:T(8,128)(2,1)S(1)} %collective-permute-done.17.two, ...), custom_call_target="tpu_custom_call" | custom-call | tf_op jit(solution)/shard_map/emit/pallas_call | solution.py:296
  135.9 3.8 %all-to-all-start = ((bf16[8,256,256]{2,1,0:T(8,128)(2,1)}), bf16[8,256,256]{2,1,0:T(8,128)(2,1)S(1)}, u32[]{:S(2)}, u32[]{:S(2)}) async-start(bf16[8,256,256]{2,1,0:T(8,128)(2,1)} %bitcast.18), calls=%async_computation | async-start | bytes 2097152 | tf_op jit(solution)/shard_map/all_to_all | solution.py:461
  139.8 0.1 stack.54.info
  139.9 21.8 %all-gather.5.cloned.1.call-done = bf16[2048,2304]{1,0:T(8,128)(2,1)} async-done(((bf16[128,2304]{1,0:T(8,128)(2,1)}), bf16[2048,2304]{1,0:T(8,128)(2,1)}) %all-gather.5.cloned.1.call-update) | async-done | bytes 9437200 | tf_op jit(solution)/shard_map/all_gather | solution.py:450
  161.7 7.3 %all-to-all-done.a = bf16[8,256,256]{2,1,0:T(8,128)(2,1)S(1)} async-done(((bf16[8,256,256]{2,1,0:T(8,128)(2,1)}), bf16[8,256,256]{2,1,0:T(8,128)(2,1)S(1)}, u32[]{:S(2)}, u32[]{:S(2)}) %all-to-all-start) | async-done | bytes 1048608 | tf_op jit(solution)/shard_map/all_to_all | solution.py:461
  169.0 3.7 %copy-done.1 = bf16[2048,2304]{1,0:T(8,128)(2,1)S(1)} copy-done((bf16[2048,2304]{1,0:T(8,128)(2,1)S(1)}, bf16[2048,2304]{1,0:T(8,128)(2,1)}, u32[]{:S(2)}) %copy-start.1) | copy-done | bytes 9437208
  172.6 3.3 %output_rows.1 = (f32[128,2304]{1,0:T(8,128)S(1)}, bf16[128,2304]{1,0:T(8,128)(2,1)S(1)}) custom-call(s32[9]{0:T(128)S(1)} %stack.54.info, bf16[8,256,256]{2,1,0:T(8,128)(2,1)S(1)} %all-to-all-done.a, bf16[16,8,16,2304]{3,2,1,0:T(8,128)(2,1)S(1)} %bitcast.33), custom_call_target="tpu_custom_call" | custom-call | flops 2415919104 | bytes 9437184 | tf_op jit(solution)/shard_map/output_rows/pallas_call | solution.py:325
  175.9 0.6 collective-permute-start.19
  176.5 1.6 collective-permute-done.19
  178.1 0.9 add_convert_fusion
  (53 shorter events, 0.2 us)
Async XLA Ops:
  7.2 25.3 %copy-start = (bf16[2304,512]{1,0:T(8,128)(2,1)S(1)}, bf16[2304,512]{1,0:T(8,128)(2,1)}, u32[]{:S(2)}) copy-start(bf16[2304,512]{1,0:T(8,128)(2,1)} %param.23) | copy-start | bytes 7077892
  7.2 25.3 %copy-start.5 = (bf16[128,2304]{1,0:T(8,128)(2,1)S(1)}, bf16[128,2304]{1,0:T(8,128)(2,1)}, u32[]{:S(2)}) copy-start(bf16[128,2304]{1,0:T(8,128)(2,1)} %param.13) | copy-start | bytes 1769476
  7.2 69.1 %all-gather.3.cloned.1.call-start = ((), (), s32[]{:S(2)}) async-start(), calls=%async_computation.1 | async-start | bytes 10027008 | tf_op jit(solution)/shard_map/all_gather | solution.py:433
  7.9 153.8 %all-gather.5.cloned.1.call-start = ((), (), s32[]{:S(2)}) async-start(), calls=%async_computation.2 | async-start | bytes 10027008 | tf_op jit(solution)/shard_map/all_gather | solution.py:450
  9.0 7.4 %collective-permute-start.6 = (bf16[16,2304]{1,0:T(8,128)(2,1)S(1)}, bf16[16,2304]{1,0:T(8,128)(2,1)S(1)}, u32[]{:S(2)}, u32[]{:S(2)}) collective-permute-start(bf16[16,2304]{1,0:T(8,128)(2,1)S(1)} %get-tuple-element.29), channel_id=1, source_target_pairs={{0,2},{1,3},{2,4},{3,5},{4,6},{5,7},{6,8},{7,9},{8,10},{9,11},{10,... | collective-permute-start | bytes 221192 | tf_op jit(solution)/shard_map/ppermute | solution.py:347
  10.7 5.7 %collective-permute-start.10 = (bf16[16,2304]{1,0:T(8,128)(2,1)S(1)}, bf16[16,2304]{1,0:T(8,128)(2,1)S(1)}, u32[]{:S(2)}, u32[]{:S(2)}) collective-permute-start(bf16[16,2304]{1,0:T(8,128)(2,1)S(1)} %get-tuple-element.29), channel_id=1, source_target_pairs={{0,14},{1,15},{2,0},{3,1},{4,2},{5,3},{6,4},{7,5},{8,6},{9,7},{10,... | collective-permute-start | bytes 221192 | tf_op jit(solution)/shard_map/ppermute | solution.py:347
  16.4 4.4 %collective-permute-start.7 = (bf16[16,2304]{1,0:T(8,128)(2,1)S(1)}, bf16[16,2304]{1,0:T(8,128)(2,1)S(1)}, u32[]{:S(2)}, u32[]{:S(2)}) collective-permute-start(bf16[16,2304]{1,0:T(8,128)(2,1)S(1)} %collective-permute-done.6), channel_id=1, source_target_pairs={{0,2},{1,3},{2,4},{3,5},{4,6},{5,7},{6,8},{7,9},{8,10},{9,11},{10,... | collective-permute-start | bytes 221192 | tf_op jit(solution)/shard_map/ppermute | solution.py:347
  16.4 4.4 %collective-permute-start.11 = (bf16[16,2304]{1,0:T(8,128)(2,1)S(1)}, bf16[16,2304]{1,0:T(8,128)(2,1)S(1)}, u32[]{:S(2)}, u32[]{:S(2)}) collective-permute-start(bf16[16,2304]{1,0:T(8,128)(2,1)S(1)} %collective-permute-done.10), channel_id=1, source_target_pairs={{0,14},{1,15},{2,0},{3,1},{4,2},{5,3},{6,4},{7,5},{8,6},{9,7},{10,... | collective-permute-start | bytes 221192 | tf_op jit(solution)/shard_map/ppermute | solution.py:347
  20.8 4.4 %collective-permute-start.8 = (bf16[16,2304]{1,0:T(8,128)(2,1)S(1)}, bf16[16,2304]{1,0:T(8,128)(2,1)S(1)}, u32[]{:S(2)}, u32[]{:S(2)}) collective-permute-start(bf16[16,2304]{1,0:T(8,128)(2,1)S(1)} %collective-permute-done.7), channel_id=1, source_target_pairs={{0,2},{1,3},{2,4},{3,5},{4,6},{5,7},{6,8},{7,9},{8,10},{9,11},{10,... | collective-permute-start | bytes 221192 | tf_op jit(solution)/shard_map/ppermute | solution.py:347
  20.8 10.8 %collective-permute-start.12 = (bf16[16,2304]{1,0:T(8,128)(2,1)S(1)}, bf16[16,2304]{1,0:T(8,128)(2,1)S(1)}, u32[]{:S(2)}, u32[]{:S(2)}) collective-permute-start(bf16[16,2304]{1,0:T(8,128)(2,1)S(1)} %collective-permute-done.11), channel_id=1, source_target_pairs={{0,14},{1,15},{2,0},{3,1},{4,2},{5,3},{6,4},{7,5},{8,6},{9,7},{10,... | collective-permute-start | bytes 221192 | tf_op jit(solution)/shard_map/ppermute | solution.py:347
  25.2 6.4 %collective-permute-start.9 = (bf16[16,2304]{1,0:T(8,128)(2,1)S(1)}, bf16[16,2304]{1,0:T(8,128)(2,1)S(1)}, u32[]{:S(2)}, u32[]{:S(2)}) collective-permute-start(bf16[16,2304]{1,0:T(8,128)(2,1)S(1)} %collective-permute-done.8), channel_id=1, source_target_pairs={{0,2},{1,3},{2,4},{3,5},{4,6},{5,7},{6,8},{7,9},{8,10},{9,11},{10,... | collective-permute-start | bytes 221192 | tf_op jit(solution)/shard_map/ppermute | solution.py:347
  31.6 1.5 copy-start.8
  31.7 0.8 copy-start.6
  31.7 7.7 %copy-start.7 = (bf16[2304,2]{0,1:T(2,128)(2,1)S(1)}, bf16[2304,2]{0,1:T(2,128)(2,1)}, u32[]{:S(2)}) copy-start(bf16[2304,2]{0,1:T(2,128)(2,1)} %param.18) | copy-start | bytes 27652
  32.5 6.4 %copy-start.11 = (s32[16,1]{0,1:T(1,128)S(1)}, s32[16,1]{0,1:T(1,128)}, u32[]{:S(2)}) copy-start(s32[16,1]{0,1:T(1,128)} %param.25) | copy-start | bytes 196
  32.5 6.8 %copy-start.12 = (f32[2]{0:T(128)S(1)}, f32[2]{0:T(128)}, u32[]{:S(2)}) copy-start(f32[2]{0:T(128)} %param.19) | copy-start | bytes 28
  33.9 6.0 %collective-permute-start = (bf16[128,512]{1,0:T(8,128)(2,1)S(1)}, bf16[128,512]{1,0:T(8,128)(2,1)S(1)}, u32[]{:S(2)}, u32[]{:S(2)}) collective-permute-start(bf16[128,512]{1,0:T(8,128)(2,1)S(1)} %get-tuple-element.31), channel_id=1, source_target_pairs={{0,16},{16,32},{32,48},{48,0},{64,80},{80,96},{96,112},{112,64},{1... | collective-permute-start | bytes 393224 | tf_op jit(solution)/shard_map/ppermute | solution.py:347
  35.3 6.4 %collective-permute-start.1 = (bf16[128,512]{1,0:T(8,128)(2,1)S(1)}, bf16[128,512]{1,0:T(8,128)(2,1)S(1)}, u32[]{:S(2)}, u32[]{:S(2)}) collective-permute-start(bf16[128,512]{1,0:T(8,128)(2,1)S(1)} %get-tuple-element.31), channel_id=1, source_target_pairs={{0,32},{16,48},{32,0},{48,16},{64,96},{80,112},{96,64},{112,80},{1... | collective-permute-start | bytes 393224 | tf_op jit(solution)/shard_map/ppermute | solution.py:347
  37.9 4.2 %collective-permute-start.2 = (bf16[128,512]{1,0:T(8,128)(2,1)S(1)}, bf16[128,512]{1,0:T(8,128)(2,1)S(1)}, u32[]{:S(2)}, u32[]{:S(2)}) collective-permute-start(bf16[128,512]{1,0:T(8,128)(2,1)S(1)} %get-tuple-element.31), channel_id=1, source_target_pairs={{0,48},{16,0},{32,16},{48,32},{64,112},{80,64},{96,80},{112,96},{1... | collective-permute-start | bytes 393224 | tf_op jit(solution)/shard_map/ppermute | solution.py:347
  42.2 8.5 %collective-permute-start.3 = (bf16[4,128,512]{2,1,0:T(8,128)(2,1)S(1)}, bf16[4,128,512]{2,1,0:T(8,128)(2,1)S(1)}, u32[]{:S(2)}, u32[]{:S(2)}) collective-permute-start(bf16[4,128,512]{2,1,0:T(8,128)(2,1)S(1)} %pad_maximum_fusion), channel_id=1, source_target_pairs={{0,64},{16,80},{32,96},{48,112},{64,128},{80,144},{96,160},{112,17... | collective-permute-start | bytes 1572872 | tf_op jit(solution)/shard_map/ppermute | solution.py:347
  42.5 9.6 %collective-permute-start.4 = (bf16[4,128,512]{2,1,0:T(8,128)(2,1)S(1)}, bf16[4,128,512]{2,1,0:T(8,128)(2,1)S(1)}, u32[]{:S(2)}, u32[]{:S(2)}) collective-permute-start(bf16[4,128,512]{2,1,0:T(8,128)(2,1)S(1)} %pad_maximum_fusion), channel_id=1, source_target_pairs={{0,128},{16,144},{32,160},{48,176},{64,192},{80,208},{96,224},{112... | collective-permute-start | bytes 1572872 | tf_op jit(solution)/shard_map/ppermute | solution.py:347
  44.6 20.8 %collective-permute-start.5 = (bf16[4,128,512]{2,1,0:T(8,128)(2,1)S(1)}, bf16[4,128,512]{2,1,0:T(8,128)(2,1)S(1)}, u32[]{:S(2)}, u32[]{:S(2)}) collective-permute-start(bf16[4,128,512]{2,1,0:T(8,128)(2,1)S(1)} %pad_maximum_fusion), channel_id=1, source_target_pairs={{0,192},{16,208},{32,224},{48,240},{64,0},{80,16},{96,32},{112,48}... | collective-permute-start | bytes 1572872 | tf_op jit(solution)/shard_map/ppermute | solution.py:347
  66.2 1.6 copy-start.2
  76.3 10.9 %copy-start.4 = (f32[2048,256]{1,0:T(8,128)S(1)}, f32[2048,256]{1,0:T(8,128)}, u32[]{:S(2)}) copy-start(f32[2048,256]{1,0:T(8,128)} %ld.3) | copy-start | bytes 6291460
  76.3 32.5 %slice-start = ((s8[9437184]{0:T(1024)(128)(4,1)}), s8[4194304]{0:T(1024)(128)(4,1)S(1)}, s32[]{:S(2)}) async-start(s8[9437184]{0:T(1024)(128)(4,1)} %bitcast.39), calls=%async_computation.3 | async-start | bytes 8388608
  87.2 21.5 %slice-start.1 = ((s8[9437184]{0:T(1024)(128)(4,1)}), s8[4194304]{0:T(1024)(128)(4,1)S(1)}, s32[]{:S(2)}) async-start(s8[9437184]{0:T(1024)(128)(4,1)} %bitcast.39), calls=%async_computation.4 | async-start | bytes 8388608
  87.3 21.5 %slice-start.2 = ((s8[9437184]{0:T(1024)(128)(4,1)}), s8[1048576]{0:T(1024)(128)(4,1)S(1)}, s32[]{:S(2)}) async-start(s8[9437184]{0:T(1024)(128)(4,1)} %bitcast.39), calls=%async_computation.5 | async-start | bytes 2097152
  87.3 21.5 %copy-start.9 = (bf16[2304,256]{1,0:T(8,128)(2,1)S(1)}, bf16[2304,256]{1,0:T(8,128)(2,1)}, u32[]{:S(2)}) copy-start(bf16[2304,256]{1,0:T(8,128)(2,1)} %param.14) | copy-start | bytes 3538948
  103.8 7.8 %copy-start.10 = (bf16[2304,256]{1,0:T(8,128)(2,1)S(1)}, bf16[2304,256]{1,0:T(8,128)(2,1)}, u32[]{:S(2)}) copy-start(bf16[2304,256]{1,0:T(8,128)(2,1)} %param.17) | copy-start | bytes 3538948
  103.8 10.6 %collective-permute-start.13 = (bf16[2,128,256]{2,1,0:T(8,128)(2,1)S(1)}, bf16[2,128,256]{2,1,0:T(8,128)(2,1)S(1)}, u32[]{:S(2)}, u32[]{:S(2)}) collective-permute-start(bf16[2,128,256]{2,1,0:T(8,128)(2,1)S(1)} %get-tuple-element.16), channel_id=1, source_target_pairs={{0,16},{16,32},{32,48},{48,0},{64,80},{80,96},{96,112},{112,64},{1... | collective-permute-start | bytes 393224 | tf_op jit(solution)/shard_map/ppermute | solution.py:347
  105.2 9.3 %collective-permute-start.14 = (bf16[2,128,256]{2,1,0:T(8,128)(2,1)S(1)}, bf16[2,128,256]{2,1,0:T(8,128)(2,1)S(1)}, u32[]{:S(2)}, u32[]{:S(2)}) collective-permute-start(bf16[2,128,256]{2,1,0:T(8,128)(2,1)S(1)} %get-tuple-element.16), channel_id=1, source_target_pairs={{0,32},{16,48},{32,0},{48,16},{64,96},{80,112},{96,64},{112,80},{1... | collective-permute-start | bytes 393224 | tf_op jit(solution)/shard_map/ppermute | solution.py:347
  107.6 6.8 %collective-permute-start.15 = (bf16[2,128,256]{2,1,0:T(8,128)(2,1)S(1)}, bf16[2,128,256]{2,1,0:T(8,128)(2,1)S(1)}, u32[]{:S(2)}, u32[]{:S(2)}) collective-permute-start(bf16[2,128,256]{2,1,0:T(8,128)(2,1)S(1)} %get-tuple-element.16), channel_id=1, source_target_pairs={{0,48},{16,0},{32,16},{48,32},{64,112},{80,64},{96,80},{112,96},{1... | collective-permute-start | bytes 393224 | tf_op jit(solution)/shard_map/ppermute | solution.py:347
  115.3 9.3 %collective-permute-start.16 = (bf16[2,128,256]{2,1,0:T(8,128)(2,1)S(1)}, bf16[2,128,256]{2,1,0:T(8,128)(2,1)S(1)}, u32[]{:S(2)}, u32[]{:S(2)}) collective-permute-start(bf16[2,128,256]{2,1,0:T(8,128)(2,1)S(1)} %get-tuple-element.18.own), channel_id=1, source_target_pairs={{0,64},{16,80},{32,96},{48,112},{64,128},{80,144},{96,160},{112,17... | collective-permute-start | bytes 393224 | tf_op jit(solution)/shard_map/ppermute | solution.py:347
  116.6 11.2 %collective-permute-start.17 = (bf16[2,128,256]{2,1,0:T(8,128)(2,1)S(1)}, bf16[2,128,256]{2,1,0:T(8,128)(2,1)S(1)}, u32[]{:S(2)}, u32[]{:S(2)}) collective-permute-start(bf16[2,128,256]{2,1,0:T(8,128)(2,1)S(1)} %get-tuple-element.18.own), channel_id=1, source_target_pairs={{0,128},{16,144},{32,160},{48,176},{64,192},{80,208},{96,224},{112... | collective-permute-start | bytes 393224 | tf_op jit(solution)/shard_map/ppermute | solution.py:347
  117.9 14.6 %collective-permute-start.18 = (bf16[2,128,256]{2,1,0:T(8,128)(2,1)S(1)}, bf16[2,128,256]{2,1,0:T(8,128)(2,1)S(1)}, u32[]{:S(2)}, u32[]{:S(2)}) collective-permute-start(bf16[2,128,256]{2,1,0:T(8,128)(2,1)S(1)} %get-tuple-element.18.own), channel_id=1, source_target_pairs={{0,192},{16,208},{32,224},{48,240},{1,193},{17,209},{33,225},{49,2... | collective-permute-start | bytes 393224 | tf_op jit(solution)/shard_map/ppermute | solution.py:347
  119.2 13.4 %copy-start.3 = (f32[128]{0:T(128)S(1)}, f32[128]{0:T(128)}, u32[]{:S(2)}) copy-start(f32[128]{0:T(128)} %param.21) | copy-start | bytes 1540
  135.9 33.0 %all-to-all-start = ((bf16[8,256,256]{2,1,0:T(8,128)(2,1)}), bf16[8,256,256]{2,1,0:T(8,128)(2,1)S(1)}, u32[]{:S(2)}, u32[]{:S(2)}) async-start(bf16[8,256,256]{2,1,0:T(8,128)(2,1)} %bitcast.18), calls=%async_computation | async-start | bytes 2097152 | tf_op jit(solution)/shard_map/all_to_all | solution.py:461
  169.0 3.7 %copy-start.1 = (bf16[2048,2304]{1,0:T(8,128)(2,1)S(1)}, bf16[2048,2304]{1,0:T(8,128)(2,1)}, u32[]{:S(2)}) copy-start(bf16[2048,2304]{1,0:T(8,128)(2,1)} %all-gather.5.cloned.1.call-done) | copy-start | bytes 28311556
  175.9 2.2 %collective-permute-start.19 = (bf16[128,2304]{1,0:T(8,128)(2,1)S(1)}, bf16[128,2304]{1,0:T(8,128)(2,1)S(1)}, u32[]{:S(2)}, u32[]{:S(2)}) collective-permute-start(bf16[128,2304]{1,0:T(8,128)(2,1)S(1)} %get-tuple-element.25), channel_id=1, source_target_pairs={{0,1},{1,0},{2,3},{3,2},{4,5},{5,4},{6,7},{7,6},{8,9},{9,8},{10,11... | collective-permute-start | bytes 1769480 | tf_op jit(solution)/shard_map/ppermute | solution.py:347
Sparse Core Ops, SparseCore 0:
  9.9 66.4 all-gather.2
  79.4 82.2 all-gather.4

commit v5 on v4

--- a/solution.py
+++ b/solution.py
@@ -262,8 +262,9 @@
     )(place, own, *received)
 
 
-def emit_kernel(group, place, before, own, one, two, three, z, y, gate, gain, out, slots, state):
-    me = place[0]
+def emit_kernel(together, info, before, own, one, two, three, gain, *refs):
+    ins, outs, (slots, state) = refs[: 3 * together], refs[3 * together : -2], refs[-2:]
+    me = info[0]
 
     @pl.when(pl.program_id(0) == 0)
     def enter():
@@ -280,51 +281,68 @@
             s = compose(before[h, :, :BLK], s) + before[h, :, BLK:]
             state[h] = s.astype(BF)
 
-    for j in range(group):
-        at = slice(j * BLK, (j + 1) * BLK)
+    made = []
+    for z, y, gate in zip(*(ins[j * together : (j + 1) * together] for j in range(3))):
+        done = []
         for h in range(2):
             lanes = slice(h * BLK, (h + 1) * BLK)
-            a = y[at, lanes] + dot(z[at, lanes], state[h])
+            a = y[:, lanes] + dot(z[:, lanes], state[h])
             scale = lax.rsqrt(jnp.mean(a * a, axis=-1, keepdims=True) + GUARD)
-            a = a * scale * gain[...] * jax.nn.sigmoid(gate[at, lanes].astype(F32))
-            out[at, lanes] = a.astype(BF)
-
-
-def emit(place, before, own, received, z, y, gate, gain, group=4):
-    small = pl.BlockSpec(own.shape, lambda i: (0, 0, 0))
-    tall = pl.BlockSpec((group * BLK, 2 * BLK), lambda i: (i, 0))
+            a = a * scale * gain[...] * jax.nn.sigmoid(gate[:, lanes].astype(F32))
+            done.append(a.astype(BF))
+        made.append(jnp.concatenate(done, axis=1))
+    for i in range(len(outs) // together):
+
+        @pl.when(pl.program_id(0) == i)
+        def put(i=i):
+            for j, rows in enumerate(made):
+                outs[i * together + j][...] = rows
+
+
+def emit(info, before, own, received, z, y, gate, gain, levels, together=2):
+    rows, lanes = z.shape
+    rows //= levels
+    small = pl.BlockSpec(own.shape, lambda i, info: (0, 0, 0))
+    tall = [
+        pl.BlockSpec((rows, lanes), lambda i, info, j=j: (lax.rem(info[1] + together * i + j, levels), 0))
+        for j in range(together)
+    ]
     return pl.pallas_call(
-        functools.partial(emit_kernel, group),
-        grid=(z.shape[0] // (group * BLK),),
-        in_specs=[pl.BlockSpec(memory_space=pltpu.SMEM)]
-        + [small] * 5
-        + [tall] * 3
-        + [pl.BlockSpec((1, BLK), lambda i: (0, 0))],
-        out_specs=tall,
-        out_shape=jax.ShapeDtypeStruct(z.shape, BF),
-        scratch_shapes=[pltpu.VMEM((4,) + own.shape, BF), pltpu.VMEM((2, BLK, BLK), BF)],
+        functools.partial(emit_kernel, together),
+        grid_spec=pltpu.PrefetchScalarGridSpec(
+            num_scalar_prefetch=1,
+            grid=(levels // together,),
+            in_specs=[small] * 5 + [pl.BlockSpec((1, BLK), lambda i, info: (0, 0))] + tall * 3,
+            out_specs=[pl.BlockSpec((rows, lanes), lambda i, info: (0, 0))] * levels,
+            scratch_shapes=[pltpu.VMEM((4,) + own.shape, BF), pltpu.VMEM((2, BLK, BLK), BF)],
+        ),
+        out_shape=[jax.ShapeDtypeStruct((rows, lanes), BF)] * levels,
         compiler_params=pltpu.CompilerParams(vmem_limit_bytes=VMEM_BYTES),
         name="emit",
-    )(place, before, own, *received, z, y, gate, gain)
-
-
-def output_kernel(info, a, w, mine, theirs, total):
+    )(info, before, own, *received, gain, *[z] * together, *[y] * together, *[gate] * together)
+
+
+def output_kernel(info, *refs):
+    blocks, (w, mine, theirs, total) = refs[:9], refs[9:]
     core = info[0]
     parts, levels, rows, width = w.shape
     depth = parts * rows
     for i in range(levels):
-        more = dot(a[info[1 + i]], w[:, i].reshape(depth, width))
+        a = blocks[i][...]
+        if i == 4:
+            a = jnp.where(core == 0, a, blocks[8][...])
+        more = dot(a, w[:, i].reshape(depth, width))
         total[...] = more if i == 0 else total[...] + more
     mine[...] = total[pl.ds(pl.multiple_of(core * BLK, BLK), BLK), :]
     theirs[...] = total[pl.ds(pl.multiple_of((1 - core) * BLK, BLK), BLK), :].astype(BF)
 
 
-def output_rows(info, normed, weight):
+def output_rows(info, blocks, weight):
     parts, levels, rows, width = weight.shape
     here = pl.BlockSpec(memory_space=pltpu.VMEM)
     return pl.pallas_call(
         output_kernel,
-        in_specs=[pl.BlockSpec(memory_space=pltpu.SMEM), here, here],
+        in_specs=[pl.BlockSpec(memory_space=pltpu.SMEM), here] + [here] * len(blocks),
         out_specs=[here, here],
         scratch_shapes=[
             pltpu.VMEM((2 * BLK, width), F32),
@@ -340,7 +358,7 @@
             transcendentals=0,
         ),
         name="output_rows",
-    )(info, normed, weight)
+    )(info, *blocks, weight)
 
 
 def turn(array, axis, pairs):
@@ -371,7 +389,12 @@
     return lax.optimization_barrier((array,) + others)[0]
 
 
-SAME_CORE = [[2 * z + k for z in range(8)] for k in range(2)]
+def half_way():
+    return [(2 * z + k, 2 * ((z + 4 - 6 * k + 8) % 8) + k) for z in range(8) for k in range(2)]
+
+
+def rest_of_way():
+    return [(2 * z + 1, 2 * ((z + 6) % 8) + 1) for z in range(8)]
 
 
 def latent_rows(tokens, kv_weight, kv_gain):
@@ -446,7 +469,7 @@
         if s < 3:
             down.append(turn(down[-1], "tp", along_z(-1)))
     part = jnp.concatenate(up + down[:0:-1], axis=0)
-    gathered = after(gathered, cache, part, weights)
+    gathered = after(gathered, tiles, part, weights)
     all_parts = lax.all_gather(part, "ctx", axis=0, tiled=True)
     all_parts = all_parts.reshape(16, 8, 16, output_weight.shape[1])
 
@@ -456,13 +479,15 @@
     before, total = side_maps((ctx % 4)[None], maps, (one, two, three))
     two, one, three = [turn(total, "ctx", down_x(d)) for d in (2, 1, 3)]
     gate = dot(gathered, gate_weight).astype(BF)
-    normed = emit((ctx // 4)[None], before, total, (one, two, three), z, y, gate, head_gain[None])
-
-    normed = lax.all_to_all(
-        normed.reshape(8, 2 * BLK, 2 * BLK), "tp", 0, 0, tiled=True, axis_index_groups=SAME_CORE
-    )
-    info = jnp.stack([core] + [(level + 8 - i) % 8 for i in range(8)])
-    mine, theirs = output_rows(info, normed, all_parts)
+    info = jnp.stack([ctx // 4, level])
+    normed = emit(info, before, total, (one, two, three), z, y, gate, head_gain[None], 8)
+
+    passing = turn(normed[4], "tp", half_way())
+    blocks = {0: normed[0], 4: passing}
+    for d in (3, 5, 2, 6, 1, 7):
+        blocks[d] = turn(normed[d], "tp", along_z(d))
+    blocks[8] = turn(passing, "tp", rest_of_way())
+    mine, theirs = output_rows(core[None], [blocks[d] for d in range(9)], after(all_parts, cache))
     theirs = turn(theirs, "tp", across())
     return (mine + theirs.astype(F32)).astype(BF), cache
 

time: 186 us -> 183 us (0.984)
  waiting for transfers between devices: 78.9 us -> 59.9 us
  starting transfers between devices: 32.1 us -> 41.5 us
  local copies, waits for them, and re-layouts: 12.1 us -> 17.2 us
    all_gather x1, waiting for transfers between devices: 21.8 us -> 5.78 us  [body(): all_parts = lax.all_gather(part, 'ctx', axis=0, tiled=True)]
    ppermute x20 -> x28, starting transfers between devices: 28.2 us -> 41.4 us  [turn(): return lax.ppermute(array, axis, pairs)]
    all_to_all x1 -> x0, waiting for transfers between devices: 7.27 us -> none  [body(): lax.all_to_all(normed.reshape(8, 2 * BLK, 2 * BLK), 'tp', 0, 0, tiled=Tru...]
    unnamed x45 -> x43, local copies, waits for them, and re-layouts: 11.2 us -> 15.7 us
    ppermute x20 -> x28, waiting for transfers between devices: 42.5 us -> 46.7 us  [turn(): return lax.ppermute(array, axis, pairs)]
    all_to_all x1 -> x0, starting transfers between devices: 3.83 us -> none  [body(): lax.all_to_all(normed.reshape(8, 2 * BLK, 2 * BLK), 'tp', 0, 0, tiled=Tru...]
  transfers between devices with their start and end apart: 23 -> 30, of which waited for: 16 -> 17; matrix products, arithmetic and copies ran while one was open for 13% -> 17% of each run, Pallas kernels for 14% -> 14%
where the time goes in v5:
time: 183 us; the launch traced here: 182 us
  waiting for transfers between devices  59.9 us (33%)
  starting transfers between devices  41.5 us (23%)
  Pallas kernels  29.2 us (16%)
  local copies, waits for them, and re-layouts  17.2 us (9%)
  matrix products  17 us (9%)
  between operations  14.4 us (8%)
  other arithmetic  3.15 us (2%)
    ppermute x28, waiting for transfers between devices, turn(): return lax.ppermute(array, axis, pairs)  46.7 us
    ppermute x28, starting transfers between devices, turn(): return lax.ppermute(array, axis, pairs)  41.4 us
    dot_general x4, matrix products, dot(): lax.dot_general(a, b, (contract, ((), ())), preferred_element_type=F32)  17 us
    pallas_call x1, Pallas kernels, delta_blocks(): pl.pallas_call(functools.partial(delta_kernel, group), grid=(blocks // gr...  16.5 us
    unnamed x43, local copies, waits for them, and re-layouts  15.7 us
    all_gather x1, waiting for transfers between devices, body(): gathered = lax.all_gather(tokens, 'tp', axis=0, tiled=True)  6.72 us
    all_gather x1, waiting for transfers between devices, body(): all_parts = lax.all_gather(part, 'ctx', axis=0, tiled=True)  5.78 us
    pallas_call x1, Pallas kernels, emit(): pl.pallas_call(functools.partial(emit_kernel, together), grid_spec=pltpu....  3.91 us
  transfers between devices with their start and end apart: 30, of which 17 were waited for; matrix products, arithmetic and copies ran while one was open for 17% of the time, Pallas kernels for 14%

profile of v5, /device:TPU:7, one launch (start us, length us, event | category | flops | bytes accessed | tf_op | source)
XLA Modules:
  0.0 182.4 jit_solution(16896760562829523000)
XLA Ops:
  7.2 0.7 all-gather.3.cloned.1.call-update
  8.0 1.6 constant_dynamic-update-slice_fusion.14
  9.6 1.6 collective-permute-start.6
  11.2 3.9 %collective-permute-start.10 = (bf16[16,2304]{1,0:T(8,128)(2,1)S(1)}, bf16[16,2304]{1,0:T(8,128)(2,1)S(1)}, u32[]{:S(2)}, u32[]{:S(2)}) collective-permute-start(bf16[16,2304]{1,0:T(8,128)(2,1)S(1)} %get-tuple-element.47), channel_id=1, source_target_pairs={{0,14},{1,15},{2,0},{3,1},{4,2},{5,3},{6,4},{7,5},{8,6},{9,7},{10,... | collective-permute-start | bytes 221192 | tf_op jit(solution)/shard_map/ppermute | solution.py:365
  15.2 1.7 collective-permute-done.6
  16.9 0.6 constant_dynamic-update-slice_fusion.13
  17.5 2.7 %collective-permute-start.11 = (bf16[16,2304]{1,0:T(8,128)(2,1)S(1)}, bf16[16,2304]{1,0:T(8,128)(2,1)S(1)}, u32[]{:S(2)}, u32[]{:S(2)}) collective-permute-start(bf16[16,2304]{1,0:T(8,128)(2,1)S(1)} %collective-permute-done.10), channel_id=1, source_target_pairs={{0,14},{1,15},{2,0},{3,1},{4,2},{5,3},{6,4},{7,5},{8,6},{9,7},{10,... | collective-permute-start | bytes 221192 | tf_op jit(solution)/shard_map/ppermute | solution.py:365
  20.2 1.1 collective-permute-done.7
  21.3 0.6 constant_dynamic-update-slice_fusion.12
  22.0 2.7 %collective-permute-start.12 = (bf16[16,2304]{1,0:T(8,128)(2,1)S(1)}, bf16[16,2304]{1,0:T(8,128)(2,1)S(1)}, u32[]{:S(2)}, u32[]{:S(2)}) collective-permute-start(bf16[16,2304]{1,0:T(8,128)(2,1)S(1)} %collective-permute-done.11), channel_id=1, source_target_pairs={{0,14},{1,15},{2,0},{3,1},{4,2},{5,3},{6,4},{7,5},{8,6},{9,7},{10,... | collective-permute-start | bytes 221192 | tf_op jit(solution)/shard_map/ppermute | solution.py:365
  24.6 1.1 collective-permute-done.8
  25.7 0.6 constant_dynamic-update-slice_fusion.11
  26.4 5.9 %collective-permute-done.9 = bf16[16,2304]{1,0:T(8,128)(2,1)S(1)} collective-permute-done((bf16[16,2304]{1,0:T(8,128)(2,1)S(1)}, bf16[16,2304]{1,0:T(8,128)(2,1)S(1)}, u32[]{:S(2)}, u32[]{:S(2)}) %collective-permute-start.9) | collective-permute-done | bytes 73760 | tf_op jit(solution)/shard_map/ppermute | solution.py:365
  32.3 0.6 constant_dynamic-update-slice_fusion.10
  32.9 0.6 constant_dynamic-update-slice_fusion.9
  33.6 0.6 constant_dynamic-update-slice_fusion.8
  34.2 0.6 constant_dynamic-update-slice_fusion.7
  35.5 0.8 constant_dynamic-update-slice_fusion.6
  36.2 1.3 collective-permute-start
  37.5 2.7 %collective-permute-start.1 = (bf16[128,512]{1,0:T(8,128)(2,1)S(1)}, bf16[128,512]{1,0:T(8,128)(2,1)S(1)}, u32[]{:S(2)}, u32[]{:S(2)}) collective-permute-start(bf16[128,512]{1,0:T(8,128)(2,1)S(1)} %get-tuple-element.49), channel_id=1, source_target_pairs={{0,32},{16,48},{32,0},{48,16},{64,96},{80,112},{96,64},{112,80},{1... | collective-permute-start | bytes 393224 | tf_op jit(solution)/shard_map/ppermute | solution.py:365
  40.2 1.0 collective-permute-start.2
  41.8 2.2 %collective-permute-done.1 = bf16[128,512]{1,0:T(8,128)(2,1)S(1)} collective-permute-done((bf16[128,512]{1,0:T(8,128)(2,1)S(1)}, bf16[128,512]{1,0:T(8,128)(2,1)S(1)}, u32[]{:S(2)}, u32[]{:S(2)}) %collective-permute-start.1) | collective-permute-done | bytes 131104 | tf_op jit(solution)/shard_map/ppermute | solution.py:365
  44.4 1.0 pad_maximum_fusion
  45.6 2.2 %collective-permute-start.4 = (bf16[4,128,512]{2,1,0:T(8,128)(2,1)S(1)}, bf16[4,128,512]{2,1,0:T(8,128)(2,1)S(1)}, u32[]{:S(2)}, u32[]{:S(2)}) collective-permute-start(bf16[4,128,512]{2,1,0:T(8,128)(2,1)S(1)} %pad_maximum_fusion), channel_id=1, source_target_pairs={{0,128},{16,144},{32,160},{48,176},{64,192},{80,208},{96,224},{112... | collective-permute-start | bytes 1572872 | tf_op jit(solution)/shard_map/ppermute | solution.py:365
  47.8 0.7 constant_dynamic-update-slice_fusion.5
  48.4 0.7 constant_dynamic-update-slice_fusion.4
  49.1 1.6 constant_dynamic-update-slice_fusion.3
  50.7 3.2 %collective-permute-done.3 = bf16[4,128,512]{2,1,0:T(8,128)(2,1)S(1)} collective-permute-done((bf16[4,128,512]{2,1,0:T(8,128)(2,1)S(1)}, bf16[4,128,512]{2,1,0:T(8,128)(2,1)S(1)}, u32[]{:S(2)}, u32[]{:S(2)}) %collective-permute-start.3) | collective-permute-done | bytes 524320 | tf_op jit(solution)/shard_map/ppermute | solution.py:365
  53.9 0.8 constant_dynamic-update-slice_fusion.2
  55.3 0.8 constant_dynamic-update-slice_fusion.1
  56.1 12.8 %collective-permute-done.5 = bf16[4,128,512]{2,1,0:T(8,128)(2,1)S(1)} collective-permute-done((bf16[4,128,512]{2,1,0:T(8,128)(2,1)S(1)}, bf16[4,128,512]{2,1,0:T(8,128)(2,1)S(1)}, u32[]{:S(2)}, u32[]{:S(2)}) %collective-permute-start.5) | collective-permute-done | bytes 524320 | tf_op jit(solution)/shard_map/ppermute | solution.py:365
  68.9 0.8 constant_dynamic-update-slice_fusion.tile
  69.7 6.7 %all-gather.3.cloned.1.call-done = bf16[2048,2304]{1,0:T(8,128)(2,1)} async-done(((bf16[128,2304]{1,0:T(8,128)(2,1)}), bf16[2048,2304]{1,0:T(8,128)(2,1)}) %all-gather.3.cloned.1.call-update) | async-done | bytes 9437200 | tf_op jit(solution)/shard_map/all_gather | solution.py:456
  76.4 10.9 %fusion.10.proj = f32[2048,640]{1,0:T(8,128)S(1)} fusion(bf16[2048,2304]{1,0:T(8,128)(2,1)} %all-gather.3.cloned.1.call-done, bf16[2304,2]{1,0:T(8,128)(2,1)S(1)} %copy.17, bf16[2304,256]{1,0:T(8,128)(2,1)} %param.16, bf16[2304,256]{1,0:T(8,128)(2,1)} %param.15), kind=kOutput, calls=%fused_computation.53 | convolution fusion | flops 6051594240 | bytes 17048576 | tf_op jit(solution)/shard_map/dot_general | solution.py:17
  87.4 16.5 %delta_blocks.1 = (bf16[2048,256]{1,0:T(8,128)(2,1)S(1)}, bf16[16,2,128,256]{3,2,1,0:T(8,128)(2,1)S(1)}, bf16[16,2,128,256]{3,2,1,0:T(8,128)(2,1)S(1)}, f32[2,12...) custom-call(f32[2048,640]{1,0:T(8,128)S(1)} %fusion.10.proj, f32[2048,256]{1,0:T(8,128)S(1)} %copy-done.4, ...), custom_call_target="tpu_custom_call" | custom-call | flops 24576000000 | bytes 24576000 | tf_op jit(solution)/shard_map/delta_blocks/pallas_call | solution.py:160
  103.9 1.3 collective-permute-start.13
  105.2 2.4 %collective-permute-start.14 = (bf16[2,128,256]{2,1,0:T(8,128)(2,1)S(1)}, bf16[2,128,256]{2,1,0:T(8,128)(2,1)S(1)}, u32[]{:S(2)}, u32[]{:S(2)}) collective-permute-start(bf16[2,128,256]{2,1,0:T(8,128)(2,1)S(1)} %get-tuple-element.25), channel_id=1, source_target_pairs={{0,32},{16,48},{32,0},{48,16},{64,96},{80,112},{96,64},{112,80},{1... | collective-permute-start | bytes 393224 | tf_op jit(solution)/shard_map/ppermute | solution.py:365
  107.6 1.2 collective-permute-start.15
  108.8 2.8 %fusion.12.q = f32[2048,256]{1,0:T(8,128)S(1)} fusion(bf16[2048,2304]{1,0:T(8,128)(2,1)S(1)} %bitcast.31, bf16[2304,256]{1,0:T(8,128)(2,1)S(1)} %copy-done.8), kind=kOutput, calls=%fused_computation.54 | convolution fusion | flops 2415919104 | bytes 12713984 | tf_op jit(solution)/shard_map/dot_general | solution.py:17
  111.6 2.8 %convolution_convert_fusion.refs_4_.refs_5_ = bf16[2048,256]{1,0:T(8,128)(2,1)S(1)} fusion(bf16[2048,2304]{1,0:T(8,128)(2,1)S(1)} %bitcast.31, bf16[2304,256]{1,0:T(8,128)(2,1)S(1)} %copy-done.9), kind=kOutput, calls=%fused_computation.3 | convolution fusion | flops 2416443392 | bytes 11665408 | tf_op jit(solution)/shard_map/dot_general | solution.py:17
  114.4 0.8 side_maps.1
  115.3 1.3 collective-permute-start.16
  116.6 1.3 collective-permute-start.17
  117.9 1.3 collective-permute-start.18
  119.2 3.2 %rise.1 = (bf16[2048,256]{1,0:T(8,128)(2,1)S(1)}, f32[2048,256]{1,0:T(8,128)S(1)}) custom-call(f32[2048,256]{1,0:T(8,128)S(1)} %fusion.12.q, f32[2048,256]{1,0:T(8,128)S(1)} %copy-done.4, bf16[2048,256]{1,0:T(8,128)(2,1)S(1)} %get-tuple-element.28.k, bf16[16,2,128,256]{3,2,1,0:T(8,128)(2,1)S(1)} %get-tuple-element.29.w, ...), custom_call_target="tpu_custom_call" | custom-call | flops 6144000000 | bytes 12288000 | tf_op jit(solution)/shard_map/rise/pallas_call | solution.py:209
  122.4 2.2 %collective-permute-done.16.one = bf16[2,128,256]{2,1,0:T(8,128)(2,1)S(1)} collective-permute-done((bf16[2,128,256]{2,1,0:T(8,128)(2,1)S(1)}, bf16[2,128,256]{2,1,0:T(8,128)(2,1)S(1)}, u32[]{:S(2)}, u32[]{:S(2)}) %collective-permute-start.16) | collective-permute-done | bytes 131104 | tf_op jit(solution)/shard_map/ppermute | solution.py:365
  124.6 3.1 %collective-permute-done.17.two = bf16[2,128,256]{2,1,0:T(8,128)(2,1)S(1)} collective-permute-done((bf16[2,128,256]{2,1,0:T(8,128)(2,1)S(1)}, bf16[2,128,256]{2,1,0:T(8,128)(2,1)S(1)}, u32[]{:S(2)}, u32[]{:S(2)}) %collective-permute-start.17) | collective-permute-done | bytes 131104 | tf_op jit(solution)/shard_map/ppermute | solution.py:365
  127.7 4.8 %collective-permute-done.18.three = bf16[2,128,256]{2,1,0:T(8,128)(2,1)S(1)} collective-permute-done((bf16[2,128,256]{2,1,0:T(8,128)(2,1)S(1)}, bf16[2,128,256]{2,1,0:T(8,128)(2,1)S(1)}, u32[]{:S(2)}, u32[]{:S(2)}) %collective-permute-start.18) | collective-permute-done | bytes 131104 | tf_op jit(solution)/shard_map/ppermute | solution.py:365
  132.5 3.9 %emit.1 = (bf16[256,256]{1,0:T(8,128)(2,1)S(1)}, bf16[256,256]{1,0:T(8,128)(2,1)S(1)}, bf16[256,256]{1,0:T(8,128)(2,1)S(1)}, bf16[256,256]{1,0:T(8,128)(2,1)}, b...) custom-call(s32[2]{0:T(128)S(1)} %pad_add_fusion.info, ...), custom_call_target="tpu_custom_call" | custom-call | tf_op jit(solution)/shard_map/emit/pallas_call | solution.py:310
  136.8 0.9 collective-permute-start.19
  137.7 1.1 collective-permute-start.20
  139.1 2.9 %collective-permute-start.21 = (bf16[256,256]{1,0:T(8,128)(2,1)}, bf16[256,256]{1,0:T(8,128)(2,1)S(1)}, u32[]{:S(2)}, u32[]{:S(2)}) collective-permute-start(bf16[256,256]{1,0:T(8,128)(2,1)} %get-tuple-element.36), channel_id=1, source_target_pairs={{0,6},{1,7},{2,8},{3,9},{4,10},{5,11},{6,12},{7,13},{8,14},{9,15},... | collective-permute-start | bytes 393224 | tf_op jit(solution)/shard_map/ppermute | solution.py:365
  142.0 1.7 collective-permute-start.23
  143.7 2.5 %collective-permute-start.24 = (bf16[256,256]{1,0:T(8,128)(2,1)}, bf16[256,256]{1,0:T(8,128)(2,1)S(1)}, u32[]{:S(2)}, u32[]{:S(2)}) collective-permute-start(bf16[256,256]{1,0:T(8,128)(2,1)} %get-tuple-element.39), channel_id=1, source_target_pairs={{0,12},{1,13},{2,14},{3,15},{4,0},{5,1},{6,2},{7,3},{8,4},{9,5},{1... | collective-permute-start | bytes 393224 | tf_op jit(solution)/shard_map/ppermute | solution.py:365
  146.7 1.4 collective-permute-done.20.refs_2_
  148.2 4.3 %collective-permute-start.26 = (bf16[256,256]{1,0:T(8,128)(2,1)S(1)}, bf16[256,256]{1,0:T(8,128)(2,1)S(1)}, u32[]{:S(2)}, u32[]{:S(2)}) collective-permute-start(bf16[256,256]{1,0:T(8,128)(2,1)S(1)} %collective-permute-done.22.refs_4_), channel_id=1, source_target_pairs={{1,13},{3,15},{5,1},{7,3},{9,5},{11,7},{13,9},{15,11},{17,29},{19,... | collective-permute-start | bytes 393224 | tf_op jit(solution)/shard_map/ppermute | solution.py:365
  152.6 1.6 copy-done.2
  154.2 2.0 %picked.1 = bf16[4,128,512]{2,1,0:T(8,128)(2,1)} custom-call(s32[8]{0:T(128)S(1)} %pad_add_fusion.1.info, bf16[16,128,512]{2,1,0:T(8,128)(2,1)S(1)} %copy-done.2), custom_call_target="tpu_custom_call" | custom-call | tf_op jit(solution)/shard_map/picked/pallas_call | solution.py:422
  156.1 5.8 %all-gather.5.cloned.1.call-done = bf16[2048,2304]{1,0:T(8,128)(2,1)} async-done(((bf16[128,2304]{1,0:T(8,128)(2,1)}), bf16[2048,2304]{1,0:T(8,128)(2,1)}) %all-gather.5.cloned.1.call-update) | async-done | bytes 9437200 | tf_op jit(solution)/shard_map/all_gather | solution.py:473
  161.9 4.1 %collective-permute-done.26.refs_8_ = bf16[256,256]{1,0:T(8,128)(2,1)S(1)} collective-permute-done((bf16[256,256]{1,0:T(8,128)(2,1)S(1)}, bf16[256,256]{1,0:T(8,128)(2,1)S(1)}, u32[]{:S(2)}, u32[]{:S(2)}) %collective-permute-start.26) | collective-permute-done | bytes 131104 | tf_op jit(solution)/shard_map/ppermute | solution.py:365
  166.0 3.7 %copy-done.1 = bf16[2048,2304]{1,0:T(8,128)(2,1)S(1)} copy-done((bf16[2048,2304]{1,0:T(8,128)(2,1)S(1)}, bf16[2048,2304]{1,0:T(8,128)(2,1)}, u32[]{:S(2)}) %copy-start.1) | copy-done | bytes 9437208
  169.7 2.8 %output_rows.1 = (f32[128,2304]{1,0:T(8,128)S(1)}, bf16[128,2304]{1,0:T(8,128)(2,1)S(1)}) custom-call(s32[1]{0:T(128)} %bitcast.info, bf16[256,256]{1,0:T(8,128)(2,1)S(1)} %get-tuple-element.33.refs_0_, bf16[256,256]{1,0:T(8,128)(2,1)S(1)} %collective-permute-done.19.refs_1_, bf16[256,256]{1,0:T(8,128)(2,1)S(1)} %collective-permute-done.20.refs_2_, ...), custom_call_target="tpu_custom_call" | custom-call | flops 2415919104 | bytes 9437184 | tf_op jit(solution)/shard_map/output_rows/pallas_call | solution.py:343
  172.6 2.0 %collective-permute-done.27 = bf16[128,2304]{1,0:T(8,128)(2,1)S(1)} collective-permute-done((bf16[128,2304]{1,0:T(8,128)(2,1)S(1)}, bf16[128,2304]{1,0:T(8,128)(2,1)S(1)}, u32[]{:S(2)}, u32[]{:S(2)}) %collective-permute-start.27) | collective-permute-done | bytes 589856 | tf_op jit(solution)/shard_map/ppermute | solution.py:365
  174.6 0.9 add_convert_fusion
  (65 shorter events, 3.9 us)
Async XLA Ops:
  7.2 27.7 %copy-start = (bf16[2304,512]{1,0:T(8,128)(2,1)S(1)}, bf16[2304,512]{1,0:T(8,128)(2,1)}, u32[]{:S(2)}) copy-start(bf16[2304,512]{1,0:T(8,128)(2,1)} %param.23) | copy-start | bytes 7077892
  7.2 27.7 %copy-start.5 = (bf16[128,2304]{1,0:T(8,128)(2,1)S(1)}, bf16[128,2304]{1,0:T(8,128)(2,1)}, u32[]{:S(2)}) copy-start(bf16[128,2304]{1,0:T(8,128)(2,1)} %param.13) | copy-start | bytes 1769476
  7.2 69.2 %all-gather.3.cloned.1.call-start = ((), (), s32[]{:S(2)}) async-start(), calls=%async_computation | async-start | bytes 10027008 | tf_op jit(solution)/shard_map/all_gather | solution.py:456
  7.9 154.0 %all-gather.5.cloned.1.call-start = ((), (), s32[]{:S(2)}) async-start(), calls=%async_computation.1 | async-start | bytes 10027008 | tf_op jit(solution)/shard_map/all_gather | solution.py:473
  9.6 7.3 %collective-permute-start.6 = (bf16[16,2304]{1,0:T(8,128)(2,1)S(1)}, bf16[16,2304]{1,0:T(8,128)(2,1)S(1)}, u32[]{:S(2)}, u32[]{:S(2)}) collective-permute-start(bf16[16,2304]{1,0:T(8,128)(2,1)S(1)} %get-tuple-element.47), channel_id=1, source_target_pairs={{0,2},{1,3},{2,4},{3,5},{4,6},{5,7},{6,8},{7,9},{8,10},{9,11},{10,... | collective-permute-start | bytes 221192 | tf_op jit(solution)/shard_map/ppermute | solution.py:365
  11.2 6.3 %collective-permute-start.10 = (bf16[16,2304]{1,0:T(8,128)(2,1)S(1)}, bf16[16,2304]{1,0:T(8,128)(2,1)S(1)}, u32[]{:S(2)}, u32[]{:S(2)}) collective-permute-start(bf16[16,2304]{1,0:T(8,128)(2,1)S(1)} %get-tuple-element.47), channel_id=1, source_target_pairs={{0,14},{1,15},{2,0},{3,1},{4,2},{5,3},{6,4},{7,5},{8,6},{9,7},{10,... | collective-permute-start | bytes 221192 | tf_op jit(solution)/shard_map/ppermute | solution.py:365
  16.9 4.4 %collective-permute-start.7 = (bf16[16,2304]{1,0:T(8,128)(2,1)S(1)}, bf16[16,2304]{1,0:T(8,128)(2,1)S(1)}, u32[]{:S(2)}, u32[]{:S(2)}) collective-permute-start(bf16[16,2304]{1,0:T(8,128)(2,1)S(1)} %collective-permute-done.6), channel_id=1, source_target_pairs={{0,2},{1,3},{2,4},{3,5},{4,6},{5,7},{6,8},{7,9},{8,10},{9,11},{10,... | collective-permute-start | bytes 221192 | tf_op jit(solution)/shard_map/ppermute | solution.py:365
  17.5 4.4 %collective-permute-start.11 = (bf16[16,2304]{1,0:T(8,128)(2,1)S(1)}, bf16[16,2304]{1,0:T(8,128)(2,1)S(1)}, u32[]{:S(2)}, u32[]{:S(2)}) collective-permute-start(bf16[16,2304]{1,0:T(8,128)(2,1)S(1)} %collective-permute-done.10), channel_id=1, source_target_pairs={{0,14},{1,15},{2,0},{3,1},{4,2},{5,3},{6,4},{7,5},{8,6},{9,7},{10,... | collective-permute-start | bytes 221192 | tf_op jit(solution)/shard_map/ppermute | solution.py:365
  21.3 4.4 %collective-permute-start.8 = (bf16[16,2304]{1,0:T(8,128)(2,1)S(1)}, bf16[16,2304]{1,0:T(8,128)(2,1)S(1)}, u32[]{:S(2)}, u32[]{:S(2)}) collective-permute-start(bf16[16,2304]{1,0:T(8,128)(2,1)S(1)} %collective-permute-done.7), channel_id=1, source_target_pairs={{0,2},{1,3},{2,4},{3,5},{4,6},{5,7},{6,8},{7,9},{8,10},{9,11},{10,... | collective-permute-start | bytes 221192 | tf_op jit(solution)/shard_map/ppermute | solution.py:365
  22.0 11.0 %collective-permute-start.12 = (bf16[16,2304]{1,0:T(8,128)(2,1)S(1)}, bf16[16,2304]{1,0:T(8,128)(2,1)S(1)}, u32[]{:S(2)}, u32[]{:S(2)}) collective-permute-start(bf16[16,2304]{1,0:T(8,128)(2,1)S(1)} %collective-permute-done.11), channel_id=1, source_target_pairs={{0,14},{1,15},{2,0},{3,1},{4,2},{5,3},{6,4},{7,5},{8,6},{9,7},{10,... | collective-permute-start | bytes 221192 | tf_op jit(solution)/shard_map/ppermute | solution.py:365
  25.7 6.6 %collective-permute-start.9 = (bf16[16,2304]{1,0:T(8,128)(2,1)S(1)}, bf16[16,2304]{1,0:T(8,128)(2,1)S(1)}, u32[]{:S(2)}, u32[]{:S(2)}) collective-permute-start(bf16[16,2304]{1,0:T(8,128)(2,1)S(1)} %collective-permute-done.8), channel_id=1, source_target_pairs={{0,2},{1,3},{2,4},{3,5},{4,6},{5,7},{6,8},{7,9},{8,10},{9,11},{10,... | collective-permute-start | bytes 221192 | tf_op jit(solution)/shard_map/ppermute | solution.py:365
  32.9 2.5 %copy-start.7 = (f32[512]{0:T(512)S(1)}, f32[512]{0:T(512)}, u32[]{:S(2)}) copy-start(f32[512]{0:T(512)} %param.24) | copy-start | bytes 6148
  34.9 6.4 %copy-start.11 = (s32[16,1]{0,1:T(1,128)S(1)}, s32[16,1]{0,1:T(1,128)}, u32[]{:S(2)}) copy-start(s32[16,1]{0,1:T(1,128)} %param.25) | copy-start | bytes 196
  34.9 6.4 %copy-start.10 = (f32[2]{0:T(128)S(1)}, f32[2]{0:T(128)}, u32[]{:S(2)}) copy-start(f32[2]{0:T(128)} %param.19) | copy-start | bytes 28
  34.9 6.4 %copy-start.6 = (bf16[2304,2]{0,1:T(2,128)(2,1)S(1)}, bf16[2304,2]{0,1:T(2,128)(2,1)}, u32[]{:S(2)}) copy-start(bf16[2304,2]{0,1:T(2,128)(2,1)} %param.18) | copy-start | bytes 27652
  36.2 5.5 %collective-permute-start = (bf16[128,512]{1,0:T(8,128)(2,1)S(1)}, bf16[128,512]{1,0:T(8,128)(2,1)S(1)}, u32[]{:S(2)}, u32[]{:S(2)}) collective-permute-start(bf16[128,512]{1,0:T(8,128)(2,1)S(1)} %get-tuple-element.49), channel_id=1, source_target_pairs={{0,16},{16,32},{32,48},{48,0},{64,80},{80,96},{96,112},{112,64},{1... | collective-permute-start | bytes 393224 | tf_op jit(solution)/shard_map/ppermute | solution.py:365
  37.5 6.5 %collective-permute-start.1 = (bf16[128,512]{1,0:T(8,128)(2,1)S(1)}, bf16[128,512]{1,0:T(8,128)(2,1)S(1)}, u32[]{:S(2)}, u32[]{:S(2)}) collective-permute-start(bf16[128,512]{1,0:T(8,128)(2,1)S(1)} %get-tuple-element.49), channel_id=1, source_target_pairs={{0,32},{16,48},{32,0},{48,16},{64,96},{80,112},{96,64},{112,80},{1... | collective-permute-start | bytes 393224 | tf_op jit(solution)/shard_map/ppermute | solution.py:365
  40.2 4.2 %collective-permute-start.2 = (bf16[128,512]{1,0:T(8,128)(2,1)S(1)}, bf16[128,512]{1,0:T(8,128)(2,1)}, u32[]{:S(2)}, u32[]{:S(2)}) collective-permute-start(bf16[128,512]{1,0:T(8,128)(2,1)S(1)} %get-tuple-element.49), channel_id=1, source_target_pairs={{0,48},{16,0},{32,16},{48,32},{64,112},{80,64},{96,80},{112,96},{1... | collective-permute-start | bytes 393224 | tf_op jit(solution)/shard_map/ppermute | solution.py:365
  45.4 8.5 %collective-permute-start.3 = (bf16[4,128,512]{2,1,0:T(8,128)(2,1)S(1)}, bf16[4,128,512]{2,1,0:T(8,128)(2,1)S(1)}, u32[]{:S(2)}, u32[]{:S(2)}) collective-permute-start(bf16[4,128,512]{2,1,0:T(8,128)(2,1)S(1)} %pad_maximum_fusion), channel_id=1, source_target_pairs={{0,64},{16,80},{32,96},{48,112},{64,128},{80,144},{96,160},{112,17... | collective-permute-start | bytes 1572872 | tf_op jit(solution)/shard_map/ppermute | solution.py:365
  45.6 9.6 %collective-permute-start.4 = (bf16[4,128,512]{2,1,0:T(8,128)(2,1)S(1)}, bf16[4,128,512]{2,1,0:T(8,128)(2,1)S(1)}, u32[]{:S(2)}, u32[]{:S(2)}) collective-permute-start(bf16[4,128,512]{2,1,0:T(8,128)(2,1)S(1)} %pad_maximum_fusion), channel_id=1, source_target_pairs={{0,128},{16,144},{32,160},{48,176},{64,192},{80,208},{96,224},{112... | collective-permute-start | bytes 1572872 | tf_op jit(solution)/shard_map/ppermute | solution.py:365
  47.8 21.1 %collective-permute-start.5 = (bf16[4,128,512]{2,1,0:T(8,128)(2,1)S(1)}, bf16[4,128,512]{2,1,0:T(8,128)(2,1)S(1)}, u32[]{:S(2)}, u32[]{:S(2)}) collective-permute-start(bf16[4,128,512]{2,1,0:T(8,128)(2,1)S(1)} %pad_maximum_fusion), channel_id=1, source_target_pairs={{0,192},{16,208},{32,224},{48,240},{64,0},{80,16},{96,32},{112,48}... | collective-permute-start | bytes 1572872 | tf_op jit(solution)/shard_map/ppermute | solution.py:365
  76.4 10.9 %copy-start.4 = (f32[2048,256]{1,0:T(8,128)S(1)}, f32[2048,256]{1,0:T(8,128)}, u32[]{:S(2)}) copy-start(f32[2048,256]{1,0:T(8,128)} %ld.3) | copy-start | bytes 6291460
  76.4 32.4 %slice-start = ((s8[9437184]{0:T(1024)(128)(4,1)}), s8[4194304]{0:T(1024)(128)(4,1)S(1)}, s32[]{:S(2)}) async-start(s8[9437184]{0:T(1024)(128)(4,1)} %bitcast.30), calls=%async_computation.2 | async-start | bytes 8388608
  87.3 21.4 %slice-start.1 = ((s8[9437184]{0:T(1024)(128)(4,1)}), s8[4194304]{0:T(1024)(128)(4,1)S(1)}, s32[]{:S(2)}) async-start(s8[9437184]{0:T(1024)(128)(4,1)} %bitcast.30), calls=%async_computation.3 | async-start | bytes 8388608
  87.4 21.4 %slice-start.2 = ((s8[9437184]{0:T(1024)(128)(4,1)}), s8[1048576]{0:T(1024)(128)(4,1)S(1)}, s32[]{:S(2)}) async-start(s8[9437184]{0:T(1024)(128)(4,1)} %bitcast.30), calls=%async_computation.4 | async-start | bytes 2097152
  87.4 21.4 %copy-start.8 = (bf16[2304,256]{1,0:T(8,128)(2,1)S(1)}, bf16[2304,256]{1,0:T(8,128)(2,1)}, u32[]{:S(2)}) copy-start(bf16[2304,256]{1,0:T(8,128)(2,1)} %param.14) | copy-start | bytes 3538948
  103.9 7.7 %copy-start.9 = (bf16[2304,256]{1,0:T(8,128)(2,1)S(1)}, bf16[2304,256]{1,0:T(8,128)(2,1)}, u32[]{:S(2)}) copy-start(bf16[2304,256]{1,0:T(8,128)(2,1)} %param.17) | copy-start | bytes 3538948
  103.9 10.5 %collective-permute-start.13 = (bf16[2,128,256]{2,1,0:T(8,128)(2,1)S(1)}, bf16[2,128,256]{2,1,0:T(8,128)(2,1)S(1)}, u32[]{:S(2)}, u32[]{:S(2)}) collective-permute-start(bf16[2,128,256]{2,1,0:T(8,128)(2,1)S(1)} %get-tuple-element.25), channel_id=1, source_target_pairs={{0,16},{16,32},{32,48},{48,0},{64,80},{80,96},{96,112},{112,64},{1... | collective-permute-start | bytes 393224 | tf_op jit(solution)/shard_map/ppermute | solution.py:365
  105.2 9.2 %collective-permute-start.14 = (bf16[2,128,256]{2,1,0:T(8,128)(2,1)S(1)}, bf16[2,128,256]{2,1,0:T(8,128)(2,1)S(1)}, u32[]{:S(2)}, u32[]{:S(2)}) collective-permute-start(bf16[2,128,256]{2,1,0:T(8,128)(2,1)S(1)} %get-tuple-element.25), channel_id=1, source_target_pairs={{0,32},{16,48},{32,0},{48,16},{64,96},{80,112},{96,64},{112,80},{1... | collective-permute-start | bytes 393224 | tf_op jit(solution)/shard_map/ppermute | solution.py:365
  107.6 6.8 %collective-permute-start.15 = (bf16[2,128,256]{2,1,0:T(8,128)(2,1)S(1)}, bf16[2,128,256]{2,1,0:T(8,128)(2,1)S(1)}, u32[]{:S(2)}, u32[]{:S(2)}) collective-permute-start(bf16[2,128,256]{2,1,0:T(8,128)(2,1)S(1)} %get-tuple-element.25), channel_id=1, source_target_pairs={{0,48},{16,0},{32,16},{48,32},{64,112},{80,64},{96,80},{112,96},{1... | collective-permute-start | bytes 393224 | tf_op jit(solution)/shard_map/ppermute | solution.py:365
  115.3 9.3 %collective-permute-start.16 = (bf16[2,128,256]{2,1,0:T(8,128)(2,1)S(1)}, bf16[2,128,256]{2,1,0:T(8,128)(2,1)S(1)}, u32[]{:S(2)}, u32[]{:S(2)}) collective-permute-start(bf16[2,128,256]{2,1,0:T(8,128)(2,1)S(1)} %get-tuple-element.27.own), channel_id=1, source_target_pairs={{0,64},{16,80},{32,96},{48,112},{64,128},{80,144},{96,160},{112,17... | collective-permute-start | bytes 393224 | tf_op jit(solution)/shard_map/ppermute | solution.py:365
  116.6 11.2 %collective-permute-start.17 = (bf16[2,128,256]{2,1,0:T(8,128)(2,1)S(1)}, bf16[2,128,256]{2,1,0:T(8,128)(2,1)S(1)}, u32[]{:S(2)}, u32[]{:S(2)}) collective-permute-start(bf16[2,128,256]{2,1,0:T(8,128)(2,1)S(1)} %get-tuple-element.27.own), channel_id=1, source_target_pairs={{0,128},{16,144},{32,160},{48,176},{64,192},{80,208},{96,224},{112... | collective-permute-start | bytes 393224 | tf_op jit(solution)/shard_map/ppermute | solution.py:365
  117.9 14.7 %collective-permute-start.18 = (bf16[2,128,256]{2,1,0:T(8,128)(2,1)S(1)}, bf16[2,128,256]{2,1,0:T(8,128)(2,1)S(1)}, u32[]{:S(2)}, u32[]{:S(2)}) collective-permute-start(bf16[2,128,256]{2,1,0:T(8,128)(2,1)S(1)} %get-tuple-element.27.own), channel_id=1, source_target_pairs={{0,192},{16,208},{32,224},{48,240},{1,193},{17,209},{33,225},{49,2... | collective-permute-start | bytes 393224 | tf_op jit(solution)/shard_map/ppermute | solution.py:365
  119.2 13.4 %copy-start.3 = (f32[128]{0:T(128)S(1)}, f32[128]{0:T(128)}, u32[]{:S(2)}) copy-start(f32[128]{0:T(128)} %param.21) | copy-start | bytes 1540
  136.4 7.3 %collective-permute-start.22 = (bf16[256,256]{1,0:T(8,128)(2,1)S(1)}, bf16[256,256]{1,0:T(8,128)(2,1)S(1)}, u32[]{:S(2)}, u32[]{:S(2)}) collective-permute-start(bf16[256,256]{1,0:T(8,128)(2,1)S(1)} %get-tuple-element.37), channel_id=1, source_target_pairs={{0,8},{1,13},{2,10},{3,15},{4,12},{5,1},{6,14},{7,3},{8,0},{9,5},{... | collective-permute-start | bytes 393224 | tf_op jit(solution)/shard_map/ppermute | solution.py:365
  136.8 9.4 %collective-permute-start.19 = (bf16[256,256]{1,0:T(8,128)(2,1)S(1)}, bf16[256,256]{1,0:T(8,128)(2,1)S(1)}, u32[]{:S(2)}, u32[]{:S(2)}) collective-permute-start(bf16[256,256]{1,0:T(8,128)(2,1)S(1)} %get-tuple-element.34), channel_id=1, source_target_pairs={{0,2},{1,3},{2,4},{3,5},{4,6},{5,7},{6,8},{7,9},{8,10},{9,11},{10,... | collective-permute-start | bytes 393224 | tf_op jit(solution)/shard_map/ppermute | solution.py:365
  137.7 10.5 %collective-permute-start.20 = (bf16[256,256]{1,0:T(8,128)(2,1)S(1)}, bf16[256,256]{1,0:T(8,128)(2,1)S(1)}, u32[]{:S(2)}, u32[]{:S(2)}) collective-permute-start(bf16[256,256]{1,0:T(8,128)(2,1)S(1)} %get-tuple-element.35), channel_id=1, source_target_pairs={{0,4},{1,5},{2,6},{3,7},{4,8},{5,9},{6,10},{7,11},{8,12},{9,13},{1... | collective-permute-start | bytes 393224 | tf_op jit(solution)/shard_map/ppermute | solution.py:365
  139.1 22.8 %collective-permute-start.21 = (bf16[256,256]{1,0:T(8,128)(2,1)}, bf16[256,256]{1,0:T(8,128)(2,1)S(1)}, u32[]{:S(2)}, u32[]{:S(2)}) collective-permute-start(bf16[256,256]{1,0:T(8,128)(2,1)} %get-tuple-element.36), channel_id=1, source_target_pairs={{0,6},{1,7},{2,8},{3,9},{4,10},{5,11},{6,12},{7,13},{8,14},{9,15},... | collective-permute-start | bytes 393224 | tf_op jit(solution)/shard_map/ppermute | solution.py:365
  142.0 19.9 %collective-permute-start.23 = (bf16[256,256]{1,0:T(8,128)(2,1)}, bf16[256,256]{1,0:T(8,128)(2,1)S(1)}, u32[]{:S(2)}, u32[]{:S(2)}) collective-permute-start(bf16[256,256]{1,0:T(8,128)(2,1)} %get-tuple-element.38), channel_id=1, source_target_pairs={{0,10},{1,11},{2,12},{3,13},{4,14},{5,15},{6,0},{7,1},{8,2},{9,3},... | collective-permute-start | bytes 393224 | tf_op jit(solution)/shard_map/ppermute | solution.py:365
  143.7 18.2 %collective-permute-start.24 = (bf16[256,256]{1,0:T(8,128)(2,1)}, bf16[256,256]{1,0:T(8,128)(2,1)S(1)}, u32[]{:S(2)}, u32[]{:S(2)}) collective-permute-start(bf16[256,256]{1,0:T(8,128)(2,1)} %get-tuple-element.39), channel_id=1, source_target_pairs={{0,12},{1,13},{2,14},{3,15},{4,0},{5,1},{6,2},{7,3},{8,4},{9,5},{1... | collective-permute-start | bytes 393224 | tf_op jit(solution)/shard_map/ppermute | solution.py:365
  146.2 15.7 %collective-permute-start.25 = (bf16[256,256]{1,0:T(8,128)(2,1)}, bf16[256,256]{1,0:T(8,128)(2,1)S(1)}, u32[]{:S(2)}, u32[]{:S(2)}) collective-permute-start(bf16[256,256]{1,0:T(8,128)(2,1)} %get-tuple-element.40), channel_id=1, source_target_pairs={{0,14},{1,15},{2,0},{3,1},{4,2},{5,3},{6,4},{7,5},{8,6},{9,7},{10,... | collective-permute-start | bytes 393224 | tf_op jit(solution)/shard_map/ppermute | solution.py:365
  148.2 17.8 %collective-permute-start.26 = (bf16[256,256]{1,0:T(8,128)(2,1)S(1)}, bf16[256,256]{1,0:T(8,128)(2,1)S(1)}, u32[]{:S(2)}, u32[]{:S(2)}) collective-permute-start(bf16[256,256]{1,0:T(8,128)(2,1)S(1)} %collective-permute-done.22.refs_4_), channel_id=1, source_target_pairs={{1,13},{3,15},{5,1},{7,3},{9,5},{11,7},{13,9},{15,11},{17,29},{19,... | collective-permute-start | bytes 393224 | tf_op jit(solution)/shard_map/ppermute | solution.py:365
  152.6 1.6 copy-start.2
  166.0 3.7 %copy-start.1 = (bf16[2048,2304]{1,0:T(8,128)(2,1)S(1)}, bf16[2048,2304]{1,0:T(8,128)(2,1)}, u32[]{:S(2)}) copy-start(bf16[2048,2304]{1,0:T(8,128)(2,1)} %all-gather.5.cloned.1.call-done) | copy-start | bytes 28311556
  172.5 2.1 %collective-permute-start.27 = (bf16[128,2304]{1,0:T(8,128)(2,1)S(1)}, bf16[128,2304]{1,0:T(8,128)(2,1)S(1)}, u32[]{:S(2)}, u32[]{:S(2)}) collective-permute-start(bf16[128,2304]{1,0:T(8,128)(2,1)S(1)} %get-tuple-element.43), channel_id=1, source_target_pairs={{0,1},{1,0},{2,3},{3,2},{4,5},{5,4},{6,7},{7,6},{8,9},{9,8},{10,11... | collective-permute-start | bytes 1769480 | tf_op jit(solution)/shard_map/ppermute | solution.py:365
Sparse Core Ops, SparseCore 0:
  9.9 66.5 all-gather.2
  79.5 82.3 all-gather.4

commit v6 on v5

--- a/solution.py
+++ b/solution.py
@@ -322,8 +322,11 @@
     )(info, before, own, *received, gain, *[z] * together, *[y] * together, *[gate] * together)
 
 
+ARRIVAL = (0, 4, 3, 5, 2, 6, 8, 1, 7)
+
+
 def output_kernel(info, *refs):
-    blocks, (w, mine, theirs, total) = refs[:9], refs[9:]
+    blocks, (w, mine, theirs, total) = dict(zip(ARRIVAL, refs[:9])), refs[9:]
     core = info[0]
     parts, levels, rows, width = w.shape
     depth = parts * rows
@@ -484,10 +487,12 @@
 
     passing = turn(normed[4], "tp", half_way())
     blocks = {0: normed[0], 4: passing}
-    for d in (3, 5, 2, 6, 1, 7):
+    for d in (3, 5, 2):
         blocks[d] = turn(normed[d], "tp", along_z(d))
     blocks[8] = turn(passing, "tp", rest_of_way())
-    mine, theirs = output_rows(core[None], [blocks[d] for d in range(9)], after(all_parts, cache))
+    for d in (6, 1, 7):
+        blocks[d] = turn(after(normed[d], passing if d == 6 else blocks[8]), "tp", along_z(d))
+    mine, theirs = output_rows(core[None], [blocks[d] for d in ARRIVAL], after(all_parts, cache))
     theirs = turn(theirs, "tp", across())
     return (mine + theirs.astype(F32)).astype(BF), cache
 

time: 183 us -> 186 us (1.016)
  starting transfers between devices: 41.5 us -> 45.6 us
    all_gather x1, waiting for transfers between devices: 5.78 us -> 0.55 us  [body(): all_parts = lax.all_gather(part, 'ctx', axis=0, tiled=True)]
    ppermute x28, waiting for transfers between devices: 46.7 us -> 51.2 us  [turn(): return lax.ppermute(array, axis, pairs)]
    ppermute x28, starting transfers between devices: 41.4 us -> 45.5 us  [turn(): return lax.ppermute(array, axis, pairs)]
  transfers between devices with their start and end apart: 30 -> 30, of which waited for: 17 -> 19; matrix products, arithmetic and copies ran while one was open for 17% -> 17% of each run, Pallas kernels for 14% -> 14%
where the time goes in v6:
time: 186 us
  waiting for transfers between devices  59.2 us (32%)
  starting transfers between devices  45.6 us (25%)
  Pallas kernels  29.2 us (16%)
  local copies, waits for them, and re-layouts  17.1 us (9%)
  matrix products  17 us (9%)
  between operations  14.4 us (8%)
  other arithmetic  3.15 us (2%)
    ppermute x28, waiting for transfers between devices, turn(): return lax.ppermute(array, axis, pairs)  51.2 us
    ppermute x28, starting transfers between devices, turn(): return lax.ppermute(array, axis, pairs)  45.5 us
    dot_general x4, matrix products, dot(): lax.dot_general(a, b, (contract, ((), ())), preferred_element_type=F32)  17 us
    pallas_call x1, Pallas kernels, delta_blocks(): pl.pallas_call(functools.partial(delta_kernel, group), grid=(blocks // gr...  16.5 us
    unnamed x43, local copies, waits for them, and re-layouts  15.7 us
    all_gather x1, waiting for transfers between devices, body(): gathered = lax.all_gather(tokens, 'tp', axis=0, tiled=True)  6.73 us
    pallas_call x1, Pallas kernels, emit(): pl.pallas_call(functools.partial(emit_kernel, together), grid_spec=pltpu....  3.95 us
  transfers between devices with their start and end apart: 30, of which 19 were waited for; matrix products, arithmetic and copies ran while one was open for 17% of the time, Pallas kernels for 14%

profile of v6, /device:TPU:7, one launch (start us, length us, event | category | flops | bytes accessed | tf_op | source)
XLA Modules:
  0.0 185.6 jit_solution(5124570498140826486)
XLA Ops:
  7.2 0.7 all-gather.3.cloned.1.call-update
  8.0 1.6 constant_dynamic-update-slice_fusion.14
  9.6 1.6 collective-permute-start.6
  11.2 3.9 %collective-permute-start.10 = (bf16[16,2304]{1,0:T(8,128)(2,1)S(1)}, bf16[16,2304]{1,0:T(8,128)(2,1)S(1)}, u32[]{:S(2)}, u32[]{:S(2)}) collective-permute-start(bf16[16,2304]{1,0:T(8,128)(2,1)S(1)} %get-tuple-element.53), channel_id=1, source_target_pairs={{0,14},{1,15},{2,0},{3,1},{4,2},{5,3},{6,4},{7,5},{8,6},{9,7},{10,... | collective-permute-start | bytes 221192 | tf_op jit(solution)/shard_map/ppermute | solution.py:368
  15.2 1.7 collective-permute-done.6
  16.9 0.6 constant_dynamic-update-slice_fusion.13
  17.5 2.7 %collective-permute-start.11 = (bf16[16,2304]{1,0:T(8,128)(2,1)S(1)}, bf16[16,2304]{1,0:T(8,128)(2,1)S(1)}, u32[]{:S(2)}, u32[]{:S(2)}) collective-permute-start(bf16[16,2304]{1,0:T(8,128)(2,1)S(1)} %collective-permute-done.10), channel_id=1, source_target_pairs={{0,14},{1,15},{2,0},{3,1},{4,2},{5,3},{6,4},{7,5},{8,6},{9,7},{10,... | collective-permute-start | bytes 221192 | tf_op jit(solution)/shard_map/ppermute | solution.py:368
  20.2 1.1 collective-permute-done.7
  21.3 0.6 constant_dynamic-update-slice_fusion.12
  22.0 2.7 %collective-permute-start.12 = (bf16[16,2304]{1,0:T(8,128)(2,1)S(1)}, bf16[16,2304]{1,0:T(8,128)(2,1)S(1)}, u32[]{:S(2)}, u32[]{:S(2)}) collective-permute-start(bf16[16,2304]{1,0:T(8,128)(2,1)S(1)} %collective-permute-done.11), channel_id=1, source_target_pairs={{0,14},{1,15},{2,0},{3,1},{4,2},{5,3},{6,4},{7,5},{8,6},{9,7},{10,... | collective-permute-start | bytes 221192 | tf_op jit(solution)/shard_map/ppermute | solution.py:368
  24.6 1.1 collective-permute-done.8
  25.7 0.6 constant_dynamic-update-slice_fusion.11
  26.4 5.9 %collective-permute-done.9 = bf16[16,2304]{1,0:T(8,128)(2,1)S(1)} collective-permute-done((bf16[16,2304]{1,0:T(8,128)(2,1)S(1)}, bf16[16,2304]{1,0:T(8,128)(2,1)S(1)}, u32[]{:S(2)}, u32[]{:S(2)}) %collective-permute-start.9) | collective-permute-done | bytes 73760 | tf_op jit(solution)/shard_map/ppermute | solution.py:368
  32.3 0.6 constant_dynamic-update-slice_fusion.10
  32.9 0.6 constant_dynamic-update-slice_fusion.9
  33.6 0.6 constant_dynamic-update-slice_fusion.8
  34.2 0.6 constant_dynamic-update-slice_fusion.7
  35.5 0.8 constant_dynamic-update-slice_fusion.6
  36.2 1.3 collective-permute-start
  37.5 2.7 %collective-permute-start.1 = (bf16[128,512]{1,0:T(8,128)(2,1)S(1)}, bf16[128,512]{1,0:T(8,128)(2,1)S(1)}, u32[]{:S(2)}, u32[]{:S(2)}) collective-permute-start(bf16[128,512]{1,0:T(8,128)(2,1)S(1)} %get-tuple-element.55), channel_id=1, source_target_pairs={{0,32},{16,48},{32,0},{48,16},{64,96},{80,112},{96,64},{112,80},{1... | collective-permute-start | bytes 393224 | tf_op jit(solution)/shard_map/ppermute | solution.py:368
  40.2 1.0 collective-permute-start.2
  41.8 2.2 %collective-permute-done.1 = bf16[128,512]{1,0:T(8,128)(2,1)S(1)} collective-permute-done((bf16[128,512]{1,0:T(8,128)(2,1)S(1)}, bf16[128,512]{1,0:T(8,128)(2,1)S(1)}, u32[]{:S(2)}, u32[]{:S(2)}) %collective-permute-start.1) | collective-permute-done | bytes 131104 | tf_op jit(solution)/shard_map/ppermute | solution.py:368
  44.4 1.0 pad_maximum_fusion
  45.6 2.2 %collective-permute-start.4 = (bf16[4,128,512]{2,1,0:T(8,128)(2,1)S(1)}, bf16[4,128,512]{2,1,0:T(8,128)(2,1)S(1)}, u32[]{:S(2)}, u32[]{:S(2)}) collective-permute-start(bf16[4,128,512]{2,1,0:T(8,128)(2,1)S(1)} %pad_maximum_fusion), channel_id=1, source_target_pairs={{0,128},{16,144},{32,160},{48,176},{64,192},{80,208},{96,224},{112... | collective-permute-start | bytes 1572872 | tf_op jit(solution)/shard_map/ppermute | solution.py:368
  47.8 0.7 constant_dynamic-update-slice_fusion.5
  48.4 0.7 constant_dynamic-update-slice_fusion.4
  49.1 1.6 constant_dynamic-update-slice_fusion.3
  50.7 3.2 %collective-permute-done.3 = bf16[4,128,512]{2,1,0:T(8,128)(2,1)S(1)} collective-permute-done((bf16[4,128,512]{2,1,0:T(8,128)(2,1)S(1)}, bf16[4,128,512]{2,1,0:T(8,128)(2,1)S(1)}, u32[]{:S(2)}, u32[]{:S(2)}) %collective-permute-start.3) | collective-permute-done | bytes 524320 | tf_op jit(solution)/shard_map/ppermute | solution.py:368
  53.9 0.8 constant_dynamic-update-slice_fusion.2
  55.2 0.8 constant_dynamic-update-slice_fusion.1
  56.1 12.8 %collective-permute-done.5 = bf16[4,128,512]{2,1,0:T(8,128)(2,1)S(1)} collective-permute-done((bf16[4,128,512]{2,1,0:T(8,128)(2,1)S(1)}, bf16[4,128,512]{2,1,0:T(8,128)(2,1)S(1)}, u32[]{:S(2)}, u32[]{:S(2)}) %collective-permute-start.5) | collective-permute-done | bytes 524320 | tf_op jit(solution)/shard_map/ppermute | solution.py:368
  68.9 0.8 constant_dynamic-update-slice_fusion.tile
  69.7 6.7 %all-gather.3.cloned.1.call-done = bf16[2048,2304]{1,0:T(8,128)(2,1)} async-done(((bf16[128,2304]{1,0:T(8,128)(2,1)}), bf16[2048,2304]{1,0:T(8,128)(2,1)}) %all-gather.3.cloned.1.call-update) | async-done | bytes 9437200 | tf_op jit(solution)/shard_map/all_gather | solution.py:459
  76.4 10.9 %fusion.10.proj = f32[2048,640]{1,0:T(8,128)S(1)} fusion(bf16[2048,2304]{1,0:T(8,128)(2,1)} %all-gather.3.cloned.1.call-done, bf16[2304,2]{1,0:T(8,128)(2,1)S(1)} %copy.17, bf16[2304,256]{1,0:T(8,128)(2,1)} %param.16, bf16[2304,256]{1,0:T(8,128)(2,1)} %param.15), kind=kOutput, calls=%fused_computation.53 | convolution fusion | flops 6051594240 | bytes 17048576 | tf_op jit(solution)/shard_map/dot_general | solution.py:17
  87.4 16.5 %delta_blocks.1 = (bf16[2048,256]{1,0:T(8,128)(2,1)S(1)}, bf16[16,2,128,256]{3,2,1,0:T(8,128)(2,1)S(1)}, bf16[16,2,128,256]{3,2,1,0:T(8,128)(2,1)S(1)}, f32[2,12...) custom-call(f32[2048,640]{1,0:T(8,128)S(1)} %fusion.10.proj, f32[2048,256]{1,0:T(8,128)S(1)} %copy-done.4, ...), custom_call_target="tpu_custom_call" | custom-call | flops 24576000000 | bytes 24576000 | tf_op jit(solution)/shard_map/delta_blocks/pallas_call | solution.py:160
  103.9 1.3 collective-permute-start.13
  105.2 2.4 %collective-permute-start.14 = (bf16[2,128,256]{2,1,0:T(8,128)(2,1)S(1)}, bf16[2,128,256]{2,1,0:T(8,128)(2,1)S(1)}, u32[]{:S(2)}, u32[]{:S(2)}) collective-permute-start(bf16[2,128,256]{2,1,0:T(8,128)(2,1)S(1)} %get-tuple-element.28), channel_id=1, source_target_pairs={{0,32},{16,48},{32,0},{48,16},{64,96},{80,112},{96,64},{112,80},{1... | collective-permute-start | bytes 393224 | tf_op jit(solution)/shard_map/ppermute | solution.py:368
  107.6 1.2 collective-permute-start.15
  108.8 2.8 %fusion.12.q = f32[2048,256]{1,0:T(8,128)S(1)} fusion(bf16[2048,2304]{1,0:T(8,128)(2,1)S(1)} %bitcast.31, bf16[2304,256]{1,0:T(8,128)(2,1)S(1)} %copy-done.8), kind=kOutput, calls=%fused_computation.54 | convolution fusion | flops 2415919104 | bytes 12713984 | tf_op jit(solution)/shard_map/dot_general | solution.py:17
  111.6 2.8 %convolution_convert_fusion.refs_4_.refs_5_ = bf16[2048,256]{1,0:T(8,128)(2,1)S(1)} fusion(bf16[2048,2304]{1,0:T(8,128)(2,1)S(1)} %bitcast.31, bf16[2304,256]{1,0:T(8,128)(2,1)S(1)} %copy-done.9), kind=kOutput, calls=%fused_computation.3 | convolution fusion | flops 2416443392 | bytes 11665408 | tf_op jit(solution)/shard_map/dot_general | solution.py:17
  114.4 0.8 side_maps.1
  115.3 1.3 collective-permute-start.16
  116.6 1.3 collective-permute-start.17
  117.9 1.3 collective-permute-start.18
  119.2 3.2 %rise.1 = (bf16[2048,256]{1,0:T(8,128)(2,1)S(1)}, f32[2048,256]{1,0:T(8,128)S(1)}) custom-call(f32[2048,256]{1,0:T(8,128)S(1)} %fusion.12.q, f32[2048,256]{1,0:T(8,128)S(1)} %copy-done.4, bf16[2048,256]{1,0:T(8,128)(2,1)S(1)} %get-tuple-element.31.k, bf16[16,2,128,256]{3,2,1,0:T(8,128)(2,1)S(1)} %get-tuple-element.32.w, ...), custom_call_target="tpu_custom_call" | custom-call | flops 6144000000 | bytes 12288000 | tf_op jit(solution)/shard_map/rise/pallas_call | solution.py:209
  122.4 2.2 %collective-permute-done.16.one = bf16[2,128,256]{2,1,0:T(8,128)(2,1)S(1)} collective-permute-done((bf16[2,128,256]{2,1,0:T(8,128)(2,1)S(1)}, bf16[2,128,256]{2,1,0:T(8,128)(2,1)S(1)}, u32[]{:S(2)}, u32[]{:S(2)}) %collective-permute-start.16) | collective-permute-done | bytes 131104 | tf_op jit(solution)/shard_map/ppermute | solution.py:368
  124.6 3.1 %collective-permute-done.17.two = bf16[2,128,256]{2,1,0:T(8,128)(2,1)S(1)} collective-permute-done((bf16[2,128,256]{2,1,0:T(8,128)(2,1)S(1)}, bf16[2,128,256]{2,1,0:T(8,128)(2,1)S(1)}, u32[]{:S(2)}, u32[]{:S(2)}) %collective-permute-start.17) | collective-permute-done | bytes 131104 | tf_op jit(solution)/shard_map/ppermute | solution.py:368
  127.7 4.8 %collective-permute-done.18.three = bf16[2,128,256]{2,1,0:T(8,128)(2,1)S(1)} collective-permute-done((bf16[2,128,256]{2,1,0:T(8,128)(2,1)S(1)}, bf16[2,128,256]{2,1,0:T(8,128)(2,1)S(1)}, u32[]{:S(2)}, u32[]{:S(2)}) %collective-permute-start.18) | collective-permute-done | bytes 131104 | tf_op jit(solution)/shard_map/ppermute | solution.py:368
  132.5 4.0 %emit.1 = (bf16[256,256]{1,0:T(8,128)(2,1)S(1)}, bf16[256,256]{1,0:T(8,128)(2,1)}, bf16[256,256]{1,0:T(8,128)(2,1)}, bf16[256,256]{1,0:T(8,128)(2,1)S(1)}, bf16[...) custom-call(s32[2]{0:T(128)S(1)} %pad_add_fusion.info, ...), custom_call_target="tpu_custom_call" | custom-call | tf_op jit(solution)/shard_map/emit/pallas_call | solution.py:310
  136.9 1.1 collective-permute-start.20
  138.0 4.0 %collective-permute-done.19.refs_1_ = bf16[256,256]{1,0:T(8,128)(2,1)S(1)} collective-permute-done((bf16[256,256]{1,0:T(8,128)(2,1)S(1)}, bf16[256,256]{1,0:T(8,128)(2,1)S(1)}, u32[]{:S(2)}, u32[]{:S(2)}) %collective-permute-start.19) | collective-permute-done | bytes 131104 | tf_op jit(solution)/shard_map/ppermute | solution.py:368
  141.9 4.2 %collective-permute-start.24 = (bf16[256,256]{1,0:T(8,128)(2,1)S(1)}, bf16[256,256]{1,0:T(8,128)(2,1)S(1)}, u32[]{:S(2)}, u32[]{:S(2)}) collective-permute-start(bf16[256,256]{1,0:T(8,128)(2,1)S(1)} %collective-permute-done.19.refs_1_), channel_id=1, source_target_pairs={{1,13},{3,15},{5,1},{7,3},{9,5},{11,7},{13,9},{15,11},{17,29},{19,... | collective-permute-start | bytes 393224 | tf_op jit(solution)/shard_map/ppermute | solution.py:368
  146.5 6.2 %collective-permute-start.21 = (bf16[256,256]{1,0:T(8,128)(2,1)}, bf16[256,256]{1,0:T(8,128)(2,1)S(1)}, u32[]{:S(2)}, u32[]{:S(2)}) collective-permute-start(bf16[256,256]{1,0:T(8,128)(2,1)} %get-tuple-element.39), channel_id=1, source_target_pairs={{0,10},{1,11},{2,12},{3,13},{4,14},{5,15},{6,0},{7,1},{8,2},{9,3},... | collective-permute-start | bytes 393224 | tf_op jit(solution)/shard_map/ppermute | solution.py:368
  152.7 3.6 %collective-permute-start.23 = (bf16[256,256]{1,0:T(8,128)(2,1)}, bf16[256,256]{1,0:T(8,128)(2,1)S(1)}, u32[]{:S(2)}, u32[]{:S(2)}) collective-permute-start(bf16[256,256]{1,0:T(8,128)(2,1)} %get-tuple-element.42), channel_id=1, source_target_pairs={{0,12},{1,13},{2,14},{3,15},{4,0},{5,1},{6,2},{7,3},{8,4},{9,5},{1... | collective-permute-start | bytes 393224 | tf_op jit(solution)/shard_map/ppermute | solution.py:368
  156.2 1.5 collective-permute-start.25
  157.8 1.6 copy-done.2
  159.4 2.0 %picked.1 = bf16[4,128,512]{2,1,0:T(8,128)(2,1)} custom-call(s32[8]{0:T(128)S(1)} %pad_add_fusion.1.info, bf16[16,128,512]{2,1,0:T(8,128)(2,1)S(1)} %copy-done.2), custom_call_target="tpu_custom_call" | custom-call | tf_op jit(solution)/shard_map/picked/pallas_call | solution.py:425
  161.9 4.5 %collective-permute-done.23.refs_5_ = bf16[256,256]{1,0:T(8,128)(2,1)S(1)} collective-permute-done((bf16[256,256]{1,0:T(8,128)(2,1)}, bf16[256,256]{1,0:T(8,128)(2,1)S(1)}, u32[]{:S(2)}, u32[]{:S(2)}) %collective-permute-start.23) | collective-permute-done | bytes 131104 | tf_op jit(solution)/shard_map/ppermute | solution.py:368
  166.5 1.8 collective-permute-done.26.refs_8_
  168.2 3.7 %copy-done.1 = bf16[2048,2304]{1,0:T(8,128)(2,1)S(1)} copy-done((bf16[2048,2304]{1,0:T(8,128)(2,1)S(1)}, bf16[2048,2304]{1,0:T(8,128)(2,1)}, u32[]{:S(2)}) %copy-start.1) | copy-done | bytes 9437208
  171.9 2.8 %output_rows.1 = (f32[128,2304]{1,0:T(8,128)S(1)}, bf16[128,2304]{1,0:T(8,128)(2,1)S(1)}) custom-call(s32[1]{0:T(128)} %bitcast.info, bf16[256,256]{1,0:T(8,128)(2,1)S(1)} %get-tuple-element.36.refs_0_, bf16[256,256]{1,0:T(8,128)(2,1)S(1)} %collective-permute-done.19.refs_1_, bf16[256,256]{1,0:T(8,128)(2,1)S(1)} %collective-permute-done.20.refs_2_, ...), custom_call_target="tpu_custom_call" | custom-call | flops 2415919104 | bytes 9437184 | tf_op jit(solution)/shard_map/output_rows/pallas_call | solution.py:346
  174.7 1.6 collective-permute-start.27
  176.3 1.6 collective-permute-done.27
  177.9 0.9 add_convert_fusion
  (65 shorter events, 3.8 us)
Async XLA Ops:
  7.2 27.7 %copy-start = (bf16[2304,512]{1,0:T(8,128)(2,1)S(1)}, bf16[2304,512]{1,0:T(8,128)(2,1)}, u32[]{:S(2)}) copy-start(bf16[2304,512]{1,0:T(8,128)(2,1)} %param.23) | copy-start | bytes 7077892
  7.2 27.7 %copy-start.5 = (bf16[128,2304]{1,0:T(8,128)(2,1)S(1)}, bf16[128,2304]{1,0:T(8,128)(2,1)}, u32[]{:S(2)}) copy-start(bf16[128,2304]{1,0:T(8,128)(2,1)} %param.13) | copy-start | bytes 1769476
  7.2 69.2 %all-gather.3.cloned.1.call-start = ((), (), s32[]{:S(2)}) async-start(), calls=%async_computation | async-start | bytes 10027008 | tf_op jit(solution)/shard_map/all_gather | solution.py:459
  7.9 154.0 %all-gather.5.cloned.1.call-start = ((), (), s32[]{:S(2)}) async-start(), calls=%async_computation.1 | async-start | bytes 10027008 | tf_op jit(solution)/shard_map/all_gather | solution.py:476
  9.6 7.3 %collective-permute-start.6 = (bf16[16,2304]{1,0:T(8,128)(2,1)S(1)}, bf16[16,2304]{1,0:T(8,128)(2,1)S(1)}, u32[]{:S(2)}, u32[]{:S(2)}) collective-permute-start(bf16[16,2304]{1,0:T(8,128)(2,1)S(1)} %get-tuple-element.53), channel_id=1, source_target_pairs={{0,2},{1,3},{2,4},{3,5},{4,6},{5,7},{6,8},{7,9},{8,10},{9,11},{10,... | collective-permute-start | bytes 221192 | tf_op jit(solution)/shard_map/ppermute | solution.py:368
  11.2 6.3 %collective-permute-start.10 = (bf16[16,2304]{1,0:T(8,128)(2,1)S(1)}, bf16[16,2304]{1,0:T(8,128)(2,1)S(1)}, u32[]{:S(2)}, u32[]{:S(2)}) collective-permute-start(bf16[16,2304]{1,0:T(8,128)(2,1)S(1)} %get-tuple-element.53), channel_id=1, source_target_pairs={{0,14},{1,15},{2,0},{3,1},{4,2},{5,3},{6,4},{7,5},{8,6},{9,7},{10,... | collective-permute-start | bytes 221192 | tf_op jit(solution)/shard_map/ppermute | solution.py:368
  16.9 4.4 %collective-permute-start.7 = (bf16[16,2304]{1,0:T(8,128)(2,1)S(1)}, bf16[16,2304]{1,0:T(8,128)(2,1)S(1)}, u32[]{:S(2)}, u32[]{:S(2)}) collective-permute-start(bf16[16,2304]{1,0:T(8,128)(2,1)S(1)} %collective-permute-done.6), channel_id=1, source_target_pairs={{0,2},{1,3},{2,4},{3,5},{4,6},{5,7},{6,8},{7,9},{8,10},{9,11},{10,... | collective-permute-start | bytes 221192 | tf_op jit(solution)/shard_map/ppermute | solution.py:368
  17.5 4.4 %collective-permute-start.11 = (bf16[16,2304]{1,0:T(8,128)(2,1)S(1)}, bf16[16,2304]{1,0:T(8,128)(2,1)S(1)}, u32[]{:S(2)}, u32[]{:S(2)}) collective-permute-start(bf16[16,2304]{1,0:T(8,128)(2,1)S(1)} %collective-permute-done.10), channel_id=1, source_target_pairs={{0,14},{1,15},{2,0},{3,1},{4,2},{5,3},{6,4},{7,5},{8,6},{9,7},{10,... | collective-permute-start | bytes 221192 | tf_op jit(solution)/shard_map/ppermute | solution.py:368
  21.3 4.4 %collective-permute-start.8 = (bf16[16,2304]{1,0:T(8,128)(2,1)S(1)}, bf16[16,2304]{1,0:T(8,128)(2,1)S(1)}, u32[]{:S(2)}, u32[]{:S(2)}) collective-permute-start(bf16[16,2304]{1,0:T(8,128)(2,1)S(1)} %collective-permute-done.7), channel_id=1, source_target_pairs={{0,2},{1,3},{2,4},{3,5},{4,6},{5,7},{6,8},{7,9},{8,10},{9,11},{10,... | collective-permute-start | bytes 221192 | tf_op jit(solution)/shard_map/ppermute | solution.py:368
  22.0 11.0 %collective-permute-start.12 = (bf16[16,2304]{1,0:T(8,128)(2,1)S(1)}, bf16[16,2304]{1,0:T(8,128)(2,1)S(1)}, u32[]{:S(2)}, u32[]{:S(2)}) collective-permute-start(bf16[16,2304]{1,0:T(8,128)(2,1)S(1)} %collective-permute-done.11), channel_id=1, source_target_pairs={{0,14},{1,15},{2,0},{3,1},{4,2},{5,3},{6,4},{7,5},{8,6},{9,7},{10,... | collective-permute-start | bytes 221192 | tf_op jit(solution)/shard_map/ppermute | solution.py:368
  25.7 6.6 %collective-permute-start.9 = (bf16[16,2304]{1,0:T(8,128)(2,1)S(1)}, bf16[16,2304]{1,0:T(8,128)(2,1)S(1)}, u32[]{:S(2)}, u32[]{:S(2)}) collective-permute-start(bf16[16,2304]{1,0:T(8,128)(2,1)S(1)} %collective-permute-done.8), channel_id=1, source_target_pairs={{0,2},{1,3},{2,4},{3,5},{4,6},{5,7},{6,8},{7,9},{8,10},{9,11},{10,... | collective-permute-start | bytes 221192 | tf_op jit(solution)/shard_map/ppermute | solution.py:368
  32.9 2.5 %copy-start.7 = (f32[512]{0:T(512)S(1)}, f32[512]{0:T(512)}, u32[]{:S(2)}) copy-start(f32[512]{0:T(512)} %param.24) | copy-start | bytes 6148
  34.9 6.4 %copy-start.10 = (f32[2]{0:T(128)S(1)}, f32[2]{0:T(128)}, u32[]{:S(2)}) copy-start(f32[2]{0:T(128)} %param.19) | copy-start | bytes 28
  34.9 6.4 %copy-start.6 = (bf16[2304,2]{0,1:T(2,128)(2,1)S(1)}, bf16[2304,2]{0,1:T(2,128)(2,1)}, u32[]{:S(2)}) copy-start(bf16[2304,2]{0,1:T(2,128)(2,1)} %param.18) | copy-start | bytes 27652
  36.2 5.5 %collective-permute-start = (bf16[128,512]{1,0:T(8,128)(2,1)S(1)}, bf16[128,512]{1,0:T(8,128)(2,1)S(1)}, u32[]{:S(2)}, u32[]{:S(2)}) collective-permute-start(bf16[128,512]{1,0:T(8,128)(2,1)S(1)} %get-tuple-element.55), channel_id=1, source_target_pairs={{0,16},{16,32},{32,48},{48,0},{64,80},{80,96},{96,112},{112,64},{1... | collective-permute-start | bytes 393224 | tf_op jit(solution)/shard_map/ppermute | solution.py:368
  37.5 6.5 %collective-permute-start.1 = (bf16[128,512]{1,0:T(8,128)(2,1)S(1)}, bf16[128,512]{1,0:T(8,128)(2,1)S(1)}, u32[]{:S(2)}, u32[]{:S(2)}) collective-permute-start(bf16[128,512]{1,0:T(8,128)(2,1)S(1)} %get-tuple-element.55), channel_id=1, source_target_pairs={{0,32},{16,48},{32,0},{48,16},{64,96},{80,112},{96,64},{112,80},{1... | collective-permute-start | bytes 393224 | tf_op jit(solution)/shard_map/ppermute | solution.py:368
  40.2 4.2 %collective-permute-start.2 = (bf16[128,512]{1,0:T(8,128)(2,1)S(1)}, bf16[128,512]{1,0:T(8,128)(2,1)}, u32[]{:S(2)}, u32[]{:S(2)}) collective-permute-start(bf16[128,512]{1,0:T(8,128)(2,1)S(1)} %get-tuple-element.55), channel_id=1, source_target_pairs={{0,48},{16,0},{32,16},{48,32},{64,112},{80,64},{96,80},{112,96},{1... | collective-permute-start | bytes 393224 | tf_op jit(solution)/shard_map/ppermute | solution.py:368
  45.4 8.5 %collective-permute-start.3 = (bf16[4,128,512]{2,1,0:T(8,128)(2,1)S(1)}, bf16[4,128,512]{2,1,0:T(8,128)(2,1)S(1)}, u32[]{:S(2)}, u32[]{:S(2)}) collective-permute-start(bf16[4,128,512]{2,1,0:T(8,128)(2,1)S(1)} %pad_maximum_fusion), channel_id=1, source_target_pairs={{0,64},{16,80},{32,96},{48,112},{64,128},{80,144},{96,160},{112,17... | collective-permute-start | bytes 1572872 | tf_op jit(solution)/shard_map/ppermute | solution.py:368
  45.6 9.6 %collective-permute-start.4 = (bf16[4,128,512]{2,1,0:T(8,128)(2,1)S(1)}, bf16[4,128,512]{2,1,0:T(8,128)(2,1)S(1)}, u32[]{:S(2)}, u32[]{:S(2)}) collective-permute-start(bf16[4,128,512]{2,1,0:T(8,128)(2,1)S(1)} %pad_maximum_fusion), channel_id=1, source_target_pairs={{0,128},{16,144},{32,160},{48,176},{64,192},{80,208},{96,224},{112... | collective-permute-start | bytes 1572872 | tf_op jit(solution)/shard_map/ppermute | solution.py:368
  47.8 21.1 %collective-permute-start.5 = (bf16[4,128,512]{2,1,0:T(8,128)(2,1)S(1)}, bf16[4,128,512]{2,1,0:T(8,128)(2,1)S(1)}, u32[]{:S(2)}, u32[]{:S(2)}) collective-permute-start(bf16[4,128,512]{2,1,0:T(8,128)(2,1)S(1)} %pad_maximum_fusion), channel_id=1, source_target_pairs={{0,192},{16,208},{32,224},{48,240},{64,0},{80,16},{96,32},{112,48}... | collective-permute-start | bytes 1572872 | tf_op jit(solution)/shard_map/ppermute | solution.py:368
  76.4 10.9 %copy-start.4 = (f32[2048,256]{1,0:T(8,128)S(1)}, f32[2048,256]{1,0:T(8,128)}, u32[]{:S(2)}) copy-start(f32[2048,256]{1,0:T(8,128)} %ld.3) | copy-start | bytes 6291460
  76.4 32.4 %slice-start = ((s8[9437184]{0:T(1024)(128)(4,1)}), s8[4194304]{0:T(1024)(128)(4,1)S(1)}, s32[]{:S(2)}) async-start(s8[9437184]{0:T(1024)(128)(4,1)} %bitcast.30), calls=%async_computation.2 | async-start | bytes 8388608
  87.3 21.4 %slice-start.1 = ((s8[9437184]{0:T(1024)(128)(4,1)}), s8[4194304]{0:T(1024)(128)(4,1)S(1)}, s32[]{:S(2)}) async-start(s8[9437184]{0:T(1024)(128)(4,1)} %bitcast.30), calls=%async_computation.3 | async-start | bytes 8388608
  87.4 21.4 %slice-start.2 = ((s8[9437184]{0:T(1024)(128)(4,1)}), s8[1048576]{0:T(1024)(128)(4,1)S(1)}, s32[]{:S(2)}) async-start(s8[9437184]{0:T(1024)(128)(4,1)} %bitcast.30), calls=%async_computation.4 | async-start | bytes 2097152
  87.4 21.4 %copy-start.8 = (bf16[2304,256]{1,0:T(8,128)(2,1)S(1)}, bf16[2304,256]{1,0:T(8,128)(2,1)}, u32[]{:S(2)}) copy-start(bf16[2304,256]{1,0:T(8,128)(2,1)} %param.14) | copy-start | bytes 3538948
  103.9 7.7 %copy-start.9 = (bf16[2304,256]{1,0:T(8,128)(2,1)S(1)}, bf16[2304,256]{1,0:T(8,128)(2,1)}, u32[]{:S(2)}) copy-start(bf16[2304,256]{1,0:T(8,128)(2,1)} %param.17) | copy-start | bytes 3538948
  103.9 10.5 %collective-permute-start.13 = (bf16[2,128,256]{2,1,0:T(8,128)(2,1)S(1)}, bf16[2,128,256]{2,1,0:T(8,128)(2,1)S(1)}, u32[]{:S(2)}, u32[]{:S(2)}) collective-permute-start(bf16[2,128,256]{2,1,0:T(8,128)(2,1)S(1)} %get-tuple-element.28), channel_id=1, source_target_pairs={{0,16},{16,32},{32,48},{48,0},{64,80},{80,96},{96,112},{112,64},{1... | collective-permute-start | bytes 393224 | tf_op jit(solution)/shard_map/ppermute | solution.py:368
  105.2 9.2 %collective-permute-start.14 = (bf16[2,128,256]{2,1,0:T(8,128)(2,1)S(1)}, bf16[2,128,256]{2,1,0:T(8,128)(2,1)S(1)}, u32[]{:S(2)}, u32[]{:S(2)}) collective-permute-start(bf16[2,128,256]{2,1,0:T(8,128)(2,1)S(1)} %get-tuple-element.28), channel_id=1, source_target_pairs={{0,32},{16,48},{32,0},{48,16},{64,96},{80,112},{96,64},{112,80},{1... | collective-permute-start | bytes 393224 | tf_op jit(solution)/shard_map/ppermute | solution.py:368
  107.6 6.8 %collective-permute-start.15 = (bf16[2,128,256]{2,1,0:T(8,128)(2,1)S(1)}, bf16[2,128,256]{2,1,0:T(8,128)(2,1)S(1)}, u32[]{:S(2)}, u32[]{:S(2)}) collective-permute-start(bf16[2,128,256]{2,1,0:T(8,128)(2,1)S(1)} %get-tuple-element.28), channel_id=1, source_target_pairs={{0,48},{16,0},{32,16},{48,32},{64,112},{80,64},{96,80},{112,96},{1... | collective-permute-start | bytes 393224 | tf_op jit(solution)/shard_map/ppermute | solution.py:368
  115.3 9.3 %collective-permute-start.16 = (bf16[2,128,256]{2,1,0:T(8,128)(2,1)S(1)}, bf16[2,128,256]{2,1,0:T(8,128)(2,1)S(1)}, u32[]{:S(2)}, u32[]{:S(2)}) collective-permute-start(bf16[2,128,256]{2,1,0:T(8,128)(2,1)S(1)} %get-tuple-element.30.own), channel_id=1, source_target_pairs={{0,64},{16,80},{32,96},{48,112},{64,128},{80,144},{96,160},{112,17... | collective-permute-start | bytes 393224 | tf_op jit(solution)/shard_map/ppermute | solution.py:368
  116.6 11.2 %collective-permute-start.17 = (bf16[2,128,256]{2,1,0:T(8,128)(2,1)S(1)}, bf16[2,128,256]{2,1,0:T(8,128)(2,1)S(1)}, u32[]{:S(2)}, u32[]{:S(2)}) collective-permute-start(bf16[2,128,256]{2,1,0:T(8,128)(2,1)S(1)} %get-tuple-element.30.own), channel_id=1, source_target_pairs={{0,128},{16,144},{32,160},{48,176},{64,192},{80,208},{96,224},{112... | collective-permute-start | bytes 393224 | tf_op jit(solution)/shard_map/ppermute | solution.py:368
  117.9 14.6 %collective-permute-start.18 = (bf16[2,128,256]{2,1,0:T(8,128)(2,1)S(1)}, bf16[2,128,256]{2,1,0:T(8,128)(2,1)S(1)}, u32[]{:S(2)}, u32[]{:S(2)}) collective-permute-start(bf16[2,128,256]{2,1,0:T(8,128)(2,1)S(1)} %get-tuple-element.30.own), channel_id=1, source_target_pairs={{0,192},{16,208},{32,224},{48,240},{1,193},{17,209},{33,225},{49,2... | collective-permute-start | bytes 393224 | tf_op jit(solution)/shard_map/ppermute | solution.py:368
  119.2 13.4 %copy-start.3 = (f32[128]{0:T(128)S(1)}, f32[128]{0:T(128)}, u32[]{:S(2)}) copy-start(f32[128]{0:T(128)} %param.21) | copy-start | bytes 1540
  132.5 4.3 %copy-start.11 = (s32[16,1]{0,1:T(1,128)S(1)}, s32[16,1]{0,1:T(1,128)}, u32[]{:S(2)}) copy-start(s32[16,1]{0,1:T(1,128)} %param.25) | copy-start | bytes 196
  136.5 5.5 %collective-permute-start.19 = (bf16[256,256]{1,0:T(8,128)(2,1)S(1)}, bf16[256,256]{1,0:T(8,128)(2,1)S(1)}, u32[]{:S(2)}, u32[]{:S(2)}) collective-permute-start(bf16[256,256]{1,0:T(8,128)(2,1)S(1)} %get-tuple-element.37), channel_id=1, source_target_pairs={{0,8},{1,13},{2,10},{3,15},{4,12},{5,1},{6,14},{7,3},{8,0},{9,5},{... | collective-permute-start | bytes 393224 | tf_op jit(solution)/shard_map/ppermute | solution.py:368
  136.9 19.4 %collective-permute-start.20 = (bf16[256,256]{1,0:T(8,128)(2,1)S(1)}, bf16[256,256]{1,0:T(8,128)(2,1)S(1)}, u32[]{:S(2)}, u32[]{:S(2)}) collective-permute-start(bf16[256,256]{1,0:T(8,128)(2,1)S(1)} %get-tuple-element.38), channel_id=1, source_target_pairs={{0,6},{1,7},{2,8},{3,9},{4,10},{5,11},{6,12},{7,13},{8,14},{9,15},... | collective-permute-start | bytes 393224 | tf_op jit(solution)/shard_map/ppermute | solution.py:368
  141.9 14.3 %collective-permute-start.24 = (bf16[256,256]{1,0:T(8,128)(2,1)S(1)}, bf16[256,256]{1,0:T(8,128)(2,1)S(1)}, u32[]{:S(2)}, u32[]{:S(2)}) collective-permute-start(bf16[256,256]{1,0:T(8,128)(2,1)S(1)} %collective-permute-done.19.refs_1_), channel_id=1, source_target_pairs={{1,13},{3,15},{5,1},{7,3},{9,5},{11,7},{13,9},{15,11},{17,29},{19,... | collective-permute-start | bytes 393224 | tf_op jit(solution)/shard_map/ppermute | solution.py:368
  146.5 15.4 %collective-permute-start.21 = (bf16[256,256]{1,0:T(8,128)(2,1)}, bf16[256,256]{1,0:T(8,128)(2,1)S(1)}, u32[]{:S(2)}, u32[]{:S(2)}) collective-permute-start(bf16[256,256]{1,0:T(8,128)(2,1)} %get-tuple-element.39), channel_id=1, source_target_pairs={{0,10},{1,11},{2,12},{3,13},{4,14},{5,15},{6,0},{7,1},{8,2},{9,3},... | collective-permute-start | bytes 393224 | tf_op jit(solution)/shard_map/ppermute | solution.py:368
  152.7 9.3 %collective-permute-start.22 = (bf16[256,256]{1,0:T(8,128)(2,1)}, bf16[256,256]{1,0:T(8,128)(2,1)S(1)}, u32[]{:S(2)}, u32[]{:S(2)}) collective-permute-start(bf16[256,256]{1,0:T(8,128)(2,1)} %get-tuple-element.40), channel_id=1, source_target_pairs={{0,4},{1,5},{2,6},{3,7},{4,8},{5,9},{6,10},{7,11},{8,12},{9,13},{1... | collective-permute-start | bytes 393224 | tf_op jit(solution)/shard_map/ppermute | solution.py:368
  152.7 13.8 %collective-permute-start.23 = (bf16[256,256]{1,0:T(8,128)(2,1)}, bf16[256,256]{1,0:T(8,128)(2,1)S(1)}, u32[]{:S(2)}, u32[]{:S(2)}) collective-permute-start(bf16[256,256]{1,0:T(8,128)(2,1)} %get-tuple-element.42), channel_id=1, source_target_pairs={{0,12},{1,13},{2,14},{3,15},{4,0},{5,1},{6,2},{7,3},{8,4},{9,5},{1... | collective-permute-start | bytes 393224 | tf_op jit(solution)/shard_map/ppermute | solution.py:368
  156.2 12.0 %collective-permute-start.26 = (bf16[256,256]{1,0:T(8,128)(2,1)}, bf16[256,256]{1,0:T(8,128)(2,1)S(1)}, u32[]{:S(2)}, u32[]{:S(2)}) collective-permute-start(bf16[256,256]{1,0:T(8,128)(2,1)} %get-tuple-element.46), channel_id=1, source_target_pairs={{0,14},{1,15},{2,0},{3,1},{4,2},{5,3},{6,4},{7,5},{8,6},{9,7},{10,... | collective-permute-start | bytes 393224 | tf_op jit(solution)/shard_map/ppermute | solution.py:368
  156.2 12.0 %collective-permute-start.25 = (bf16[256,256]{1,0:T(8,128)(2,1)}, bf16[256,256]{1,0:T(8,128)(2,1)S(1)}, u32[]{:S(2)}, u32[]{:S(2)}) collective-permute-start(bf16[256,256]{1,0:T(8,128)(2,1)} %get-tuple-element.44), channel_id=1, source_target_pairs={{0,2},{1,3},{2,4},{3,5},{4,6},{5,7},{6,8},{7,9},{8,10},{9,11},{10,... | collective-permute-start | bytes 393224 | tf_op jit(solution)/shard_map/ppermute | solution.py:368
  157.8 1.6 copy-start.2
  168.2 3.7 %copy-start.1 = (bf16[2048,2304]{1,0:T(8,128)(2,1)S(1)}, bf16[2048,2304]{1,0:T(8,128)(2,1)}, u32[]{:S(2)}) copy-start(bf16[2048,2304]{1,0:T(8,128)(2,1)} %all-gather.5.cloned.1.call-done) | copy-start | bytes 28311556
  174.7 3.2 %collective-permute-start.27 = (bf16[128,2304]{1,0:T(8,128)(2,1)S(1)}, bf16[128,2304]{1,0:T(8,128)(2,1)S(1)}, u32[]{:S(2)}, u32[]{:S(2)}) collective-permute-start(bf16[128,2304]{1,0:T(8,128)(2,1)S(1)} %get-tuple-element.49), channel_id=1, source_target_pairs={{0,1},{1,0},{2,3},{3,2},{4,5},{5,4},{6,7},{7,6},{8,9},{9,8},{10,11... | collective-permute-start | bytes 1769480 | tf_op jit(solution)/shard_map/ppermute | solution.py:368
Sparse Core Ops, SparseCore 0:
  9.9 66.5 all-gather.2
  79.5 82.3 all-gather.4

commit v7 on v6

--- a/solution.py
+++ b/solution.py
@@ -487,11 +487,9 @@
 
     passing = turn(normed[4], "tp", half_way())
     blocks = {0: normed[0], 4: passing}
-    for d in (3, 5, 2):
+    for d in (3, 5, 2, 6, 1, 7):
         blocks[d] = turn(normed[d], "tp", along_z(d))
     blocks[8] = turn(passing, "tp", rest_of_way())
-    for d in (6, 1, 7):
-        blocks[d] = turn(after(normed[d], passing if d == 6 else blocks[8]), "tp", along_z(d))
     mine, theirs = output_rows(core[None], [blocks[d] for d in ARRIVAL], after(all_parts, cache))
     theirs = turn(theirs, "tp", across())
     return (mine + theirs.astype(F32)).astype(BF), cache

time: 186 us -> 181 us (0.973)
  starting transfers between devices: 45.6 us -> 42.2 us
    ppermute x28, starting transfers between devices: 45.5 us -> 42.1 us  [turn(): return lax.ppermute(array, axis, pairs)]
    ppermute x28, waiting for transfers between devices: 51.2 us -> 48.1 us  [turn(): return lax.ppermute(array, axis, pairs)]
  transfers between devices with their start and end apart: 30 -> 30, of which waited for: 19 -> 17; matrix products, arithmetic and copies ran while one was open for 17% -> 17% of each run, Pallas kernels for 14% -> 15%
where the time goes in v7:
time: 181 us
  waiting for transfers between devices  57.6 us (32%)
  starting transfers between devices  42.2 us (23%)
  Pallas kernels  29.2 us (16%)
  local copies, waits for them, and re-layouts  17.2 us (10%)
  matrix products  17 us (9%)
  between operations  14.4 us (8%)
  other arithmetic  3.15 us (2%)
    ppermute x28, waiting for transfers between devices, turn(): return lax.ppermute(array, axis, pairs)  48.1 us
    ppermute x28, starting transfers between devices, turn(): return lax.ppermute(array, axis, pairs)  42.1 us
    dot_general x4, matrix products, dot(): lax.dot_general(a, b, (contract, ((), ())), preferred_element_type=F32)  17 us
    pallas_call x1, Pallas kernels, delta_blocks(): pl.pallas_call(functools.partial(delta_kernel, group), grid=(blocks // gr...  16.5 us
    unnamed x43, local copies, waits for them, and re-layouts  15.7 us
    all_gather x1, waiting for transfers between devices, body(): gathered = lax.all_gather(tokens, 'tp', axis=0, tiled=True)  6.72 us
    pallas_call x1, Pallas kernels, emit(): pl.pallas_call(functools.partial(emit_kernel, together), grid_spec=pltpu....  3.92 us
  transfers between devices with their start and end apart: 30, of which 17 were waited for; matrix products, arithmetic and copies ran while one was open for 17% of the time, Pallas kernels for 15%

profile of v7, /device:TPU:7, one launch (start us, length us, event | category | flops | bytes accessed | tf_op | source)
XLA Modules:
  0.0 180.7 jit_solution(17803968409056814790)
XLA Ops:
  7.2 0.7 all-gather.3.cloned.1.call-update
  8.0 1.6 constant_dynamic-update-slice_fusion.14
  9.6 1.6 collective-permute-start.6
  11.2 3.9 %collective-permute-start.10 = (bf16[16,2304]{1,0:T(8,128)(2,1)S(1)}, bf16[16,2304]{1,0:T(8,128)(2,1)S(1)}, u32[]{:S(2)}, u32[]{:S(2)}) collective-permute-start(bf16[16,2304]{1,0:T(8,128)(2,1)S(1)} %get-tuple-element.47), channel_id=1, source_target_pairs={{0,14},{1,15},{2,0},{3,1},{4,2},{5,3},{6,4},{7,5},{8,6},{9,7},{10,... | collective-permute-start | bytes 221192 | tf_op jit(solution)/shard_map/ppermute | solution.py:368
  15.2 1.7 collective-permute-done.6
  16.9 0.6 constant_dynamic-update-slice_fusion.13
  17.5 2.7 %collective-permute-start.11 = (bf16[16,2304]{1,0:T(8,128)(2,1)S(1)}, bf16[16,2304]{1,0:T(8,128)(2,1)S(1)}, u32[]{:S(2)}, u32[]{:S(2)}) collective-permute-start(bf16[16,2304]{1,0:T(8,128)(2,1)S(1)} %collective-permute-done.10), channel_id=1, source_target_pairs={{0,14},{1,15},{2,0},{3,1},{4,2},{5,3},{6,4},{7,5},{8,6},{9,7},{10,... | collective-permute-start | bytes 221192 | tf_op jit(solution)/shard_map/ppermute | solution.py:368
  20.2 1.1 collective-permute-done.7
  21.3 0.6 constant_dynamic-update-slice_fusion.12
  22.0 2.7 %collective-permute-start.12 = (bf16[16,2304]{1,0:T(8,128)(2,1)S(1)}, bf16[16,2304]{1,0:T(8,128)(2,1)S(1)}, u32[]{:S(2)}, u32[]{:S(2)}) collective-permute-start(bf16[16,2304]{1,0:T(8,128)(2,1)S(1)} %collective-permute-done.11), channel_id=1, source_target_pairs={{0,14},{1,15},{2,0},{3,1},{4,2},{5,3},{6,4},{7,5},{8,6},{9,7},{10,... | collective-permute-start | bytes 221192 | tf_op jit(solution)/shard_map/ppermute | solution.py:368
  24.6 1.1 collective-permute-done.8
  25.7 0.6 constant_dynamic-update-slice_fusion.11
  26.4 5.9 %collective-permute-done.9 = bf16[16,2304]{1,0:T(8,128)(2,1)S(1)} collective-permute-done((bf16[16,2304]{1,0:T(8,128)(2,1)S(1)}, bf16[16,2304]{1,0:T(8,128)(2,1)S(1)}, u32[]{:S(2)}, u32[]{:S(2)}) %collective-permute-start.9) | collective-permute-done | bytes 73760 | tf_op jit(solution)/shard_map/ppermute | solution.py:368
  32.3 0.6 constant_dynamic-update-slice_fusion.10
  32.9 0.6 constant_dynamic-update-slice_fusion.9
  33.6 0.6 constant_dynamic-update-slice_fusion.8
  34.2 0.6 constant_dynamic-update-slice_fusion.7
  35.5 0.8 constant_dynamic-update-slice_fusion.6
  36.2 1.3 collective-permute-start
  37.5 2.7 %collective-permute-start.1 = (bf16[128,512]{1,0:T(8,128)(2,1)S(1)}, bf16[128,512]{1,0:T(8,128)(2,1)S(1)}, u32[]{:S(2)}, u32[]{:S(2)}) collective-permute-start(bf16[128,512]{1,0:T(8,128)(2,1)S(1)} %get-tuple-element.49), channel_id=1, source_target_pairs={{0,32},{16,48},{32,0},{48,16},{64,96},{80,112},{96,64},{112,80},{1... | collective-permute-start | bytes 393224 | tf_op jit(solution)/shard_map/ppermute | solution.py:368
  40.2 1.0 collective-permute-start.2
  41.8 2.2 %collective-permute-done.1 = bf16[128,512]{1,0:T(8,128)(2,1)S(1)} collective-permute-done((bf16[128,512]{1,0:T(8,128)(2,1)S(1)}, bf16[128,512]{1,0:T(8,128)(2,1)S(1)}, u32[]{:S(2)}, u32[]{:S(2)}) %collective-permute-start.1) | collective-permute-done | bytes 131104 | tf_op jit(solution)/shard_map/ppermute | solution.py:368
  44.4 1.0 pad_maximum_fusion
  45.6 2.2 %collective-permute-start.4 = (bf16[4,128,512]{2,1,0:T(8,128)(2,1)S(1)}, bf16[4,128,512]{2,1,0:T(8,128)(2,1)S(1)}, u32[]{:S(2)}, u32[]{:S(2)}) collective-permute-start(bf16[4,128,512]{2,1,0:T(8,128)(2,1)S(1)} %pad_maximum_fusion), channel_id=1, source_target_pairs={{0,128},{16,144},{32,160},{48,176},{64,192},{80,208},{96,224},{112... | collective-permute-start | bytes 1572872 | tf_op jit(solution)/shard_map/ppermute | solution.py:368
  47.8 0.7 constant_dynamic-update-slice_fusion.5
  48.4 0.7 constant_dynamic-update-slice_fusion.4
  49.1 1.6 constant_dynamic-update-slice_fusion.3
  50.7 3.2 %collective-permute-done.3 = bf16[4,128,512]{2,1,0:T(8,128)(2,1)S(1)} collective-permute-done((bf16[4,128,512]{2,1,0:T(8,128)(2,1)S(1)}, bf16[4,128,512]{2,1,0:T(8,128)(2,1)S(1)}, u32[]{:S(2)}, u32[]{:S(2)}) %collective-permute-start.3) | collective-permute-done | bytes 524320 | tf_op jit(solution)/shard_map/ppermute | solution.py:368
  53.9 0.8 constant_dynamic-update-slice_fusion.2
  55.3 0.8 constant_dynamic-update-slice_fusion.1
  56.1 12.8 %collective-permute-done.5 = bf16[4,128,512]{2,1,0:T(8,128)(2,1)S(1)} collective-permute-done((bf16[4,128,512]{2,1,0:T(8,128)(2,1)S(1)}, bf16[4,128,512]{2,1,0:T(8,128)(2,1)S(1)}, u32[]{:S(2)}, u32[]{:S(2)}) %collective-permute-start.5) | collective-permute-done | bytes 524320 | tf_op jit(solution)/shard_map/ppermute | solution.py:368
  68.9 0.8 constant_dynamic-update-slice_fusion.tile
  69.7 6.7 %all-gather.3.cloned.1.call-done = bf16[2048,2304]{1,0:T(8,128)(2,1)} async-done(((bf16[128,2304]{1,0:T(8,128)(2,1)}), bf16[2048,2304]{1,0:T(8,128)(2,1)}) %all-gather.3.cloned.1.call-update) | async-done | bytes 9437200 | tf_op jit(solution)/shard_map/all_gather | solution.py:459
  76.4 10.9 %fusion.10.proj = f32[2048,640]{1,0:T(8,128)S(1)} fusion(bf16[2048,2304]{1,0:T(8,128)(2,1)} %all-gather.3.cloned.1.call-done, bf16[2304,2]{1,0:T(8,128)(2,1)S(1)} %copy.17, bf16[2304,256]{1,0:T(8,128)(2,1)} %param.16, bf16[2304,256]{1,0:T(8,128)(2,1)} %param.15), kind=kOutput, calls=%fused_computation.53 | convolution fusion | flops 6051594240 | bytes 17048576 | tf_op jit(solution)/shard_map/dot_general | solution.py:17
  87.4 16.5 %delta_blocks.1 = (bf16[2048,256]{1,0:T(8,128)(2,1)S(1)}, bf16[16,2,128,256]{3,2,1,0:T(8,128)(2,1)S(1)}, bf16[16,2,128,256]{3,2,1,0:T(8,128)(2,1)S(1)}, f32[2,12...) custom-call(f32[2048,640]{1,0:T(8,128)S(1)} %fusion.10.proj, f32[2048,256]{1,0:T(8,128)S(1)} %copy-done.4, ...), custom_call_target="tpu_custom_call" | custom-call | flops 24576000000 | bytes 24576000 | tf_op jit(solution)/shard_map/delta_blocks/pallas_call | solution.py:160
  103.9 1.3 collective-permute-start.13
  105.2 2.4 %collective-permute-start.14 = (bf16[2,128,256]{2,1,0:T(8,128)(2,1)S(1)}, bf16[2,128,256]{2,1,0:T(8,128)(2,1)S(1)}, u32[]{:S(2)}, u32[]{:S(2)}) collective-permute-start(bf16[2,128,256]{2,1,0:T(8,128)(2,1)S(1)} %get-tuple-element.25), channel_id=1, source_target_pairs={{0,32},{16,48},{32,0},{48,16},{64,96},{80,112},{96,64},{112,80},{1... | collective-permute-start | bytes 393224 | tf_op jit(solution)/shard_map/ppermute | solution.py:368
  107.6 1.2 collective-permute-start.15
  108.8 2.8 %fusion.12.q = f32[2048,256]{1,0:T(8,128)S(1)} fusion(bf16[2048,2304]{1,0:T(8,128)(2,1)S(1)} %bitcast.31, bf16[2304,256]{1,0:T(8,128)(2,1)S(1)} %copy-done.8), kind=kOutput, calls=%fused_computation.54 | convolution fusion | flops 2415919104 | bytes 12713984 | tf_op jit(solution)/shard_map/dot_general | solution.py:17
  111.6 2.8 %convolution_convert_fusion.refs_4_.refs_5_ = bf16[2048,256]{1,0:T(8,128)(2,1)S(1)} fusion(bf16[2048,2304]{1,0:T(8,128)(2,1)S(1)} %bitcast.31, bf16[2304,256]{1,0:T(8,128)(2,1)S(1)} %copy-done.9), kind=kOutput, calls=%fused_computation.3 | convolution fusion | flops 2416443392 | bytes 11665408 | tf_op jit(solution)/shard_map/dot_general | solution.py:17
  114.4 0.8 side_maps.1
  115.3 1.3 collective-permute-start.16
  116.6 1.3 collective-permute-start.17
  117.9 1.3 collective-permute-start.18
  119.2 3.2 %rise.1 = (bf16[2048,256]{1,0:T(8,128)(2,1)S(1)}, f32[2048,256]{1,0:T(8,128)S(1)}) custom-call(f32[2048,256]{1,0:T(8,128)S(1)} %fusion.12.q, f32[2048,256]{1,0:T(8,128)S(1)} %copy-done.4, bf16[2048,256]{1,0:T(8,128)(2,1)S(1)} %get-tuple-element.28.k, bf16[16,2,128,256]{3,2,1,0:T(8,128)(2,1)S(1)} %get-tuple-element.29.w, ...), custom_call_target="tpu_custom_call" | custom-call | flops 6144000000 | bytes 12288000 | tf_op jit(solution)/shard_map/rise/pallas_call | solution.py:209
  122.4 2.2 %collective-permute-done.16.one = bf16[2,128,256]{2,1,0:T(8,128)(2,1)S(1)} collective-permute-done((bf16[2,128,256]{2,1,0:T(8,128)(2,1)S(1)}, bf16[2,128,256]{2,1,0:T(8,128)(2,1)S(1)}, u32[]{:S(2)}, u32[]{:S(2)}) %collective-permute-start.16) | collective-permute-done | bytes 131104 | tf_op jit(solution)/shard_map/ppermute | solution.py:368
  124.6 3.1 %collective-permute-done.17.two = bf16[2,128,256]{2,1,0:T(8,128)(2,1)S(1)} collective-permute-done((bf16[2,128,256]{2,1,0:T(8,128)(2,1)S(1)}, bf16[2,128,256]{2,1,0:T(8,128)(2,1)S(1)}, u32[]{:S(2)}, u32[]{:S(2)}) %collective-permute-start.17) | collective-permute-done | bytes 131104 | tf_op jit(solution)/shard_map/ppermute | solution.py:368
  127.7 4.8 %collective-permute-done.18.three = bf16[2,128,256]{2,1,0:T(8,128)(2,1)S(1)} collective-permute-done((bf16[2,128,256]{2,1,0:T(8,128)(2,1)S(1)}, bf16[2,128,256]{2,1,0:T(8,128)(2,1)S(1)}, u32[]{:S(2)}, u32[]{:S(2)}) %collective-permute-start.18) | collective-permute-done | bytes 131104 | tf_op jit(solution)/shard_map/ppermute | solution.py:368
  132.5 3.9 %emit.1 = (bf16[256,256]{1,0:T(8,128)(2,1)S(1)}, bf16[256,256]{1,0:T(8,128)(2,1)}, bf16[256,256]{1,0:T(8,128)(2,1)}, bf16[256,256]{1,0:T(8,128)(2,1)S(1)}, bf16[...) custom-call(s32[2]{0:T(128)S(1)} %pad_add_fusion.info, ...), custom_call_target="tpu_custom_call" | custom-call | tf_op jit(solution)/shard_map/emit/pallas_call | solution.py:310
  136.8 1.0 collective-permute-start.20
  137.8 3.5 %collective-permute-start.21 = (bf16[256,256]{1,0:T(8,128)(2,1)S(1)}, bf16[256,256]{1,0:T(8,128)(2,1)S(1)}, u32[]{:S(2)}, u32[]{:S(2)}) collective-permute-start(bf16[256,256]{1,0:T(8,128)(2,1)S(1)} %get-tuple-element.36), channel_id=1, source_target_pairs={{0,10},{1,11},{2,12},{3,13},{4,14},{5,15},{6,0},{7,1},{8,2},{9,3},... | collective-permute-start | bytes 393224 | tf_op jit(solution)/shard_map/ppermute | solution.py:368
  141.6 2.1 %collective-permute-start.22 = (bf16[256,256]{1,0:T(8,128)(2,1)}, bf16[256,256]{1,0:T(8,128)(2,1)S(1)}, u32[]{:S(2)}, u32[]{:S(2)}) collective-permute-start(bf16[256,256]{1,0:T(8,128)(2,1)} %get-tuple-element.37), channel_id=1, source_target_pairs={{0,4},{1,5},{2,6},{3,7},{4,8},{5,9},{6,10},{7,11},{8,12},{9,13},{1... | collective-permute-start | bytes 393224 | tf_op jit(solution)/shard_map/ppermute | solution.py:368
  143.7 1.6 collective-permute-start.23
  145.3 0.9 collective-permute-start.25
  146.2 4.8 %collective-permute-done.20.refs_2_ = bf16[256,256]{1,0:T(8,128)(2,1)S(1)} collective-permute-done((bf16[256,256]{1,0:T(8,128)(2,1)S(1)}, bf16[256,256]{1,0:T(8,128)(2,1)S(1)}, u32[]{:S(2)}, u32[]{:S(2)}) %collective-permute-start.20) | collective-permute-done | bytes 131104 | tf_op jit(solution)/shard_map/ppermute | solution.py:368
  151.0 5.2 %collective-permute-start.24 = (bf16[256,256]{1,0:T(8,128)(2,1)S(1)}, bf16[256,256]{1,0:T(8,128)(2,1)S(1)}, u32[]{:S(2)}, u32[]{:S(2)}) collective-permute-start(bf16[256,256]{1,0:T(8,128)(2,1)S(1)} %collective-permute-done.19.refs_1_), channel_id=1, source_target_pairs={{1,13},{3,15},{5,1},{7,3},{9,5},{11,7},{13,9},{15,11},{17,29},{19,... | collective-permute-start | bytes 393224 | tf_op jit(solution)/shard_map/ppermute | solution.py:368
  156.3 1.6 copy-done.2
  157.9 2.0 %picked.1 = bf16[4,128,512]{2,1,0:T(8,128)(2,1)} custom-call(s32[8]{0:T(128)S(1)} %pad_add_fusion.1.info, bf16[16,128,512]{2,1,0:T(8,128)(2,1)S(1)} %copy-done.2), custom_call_target="tpu_custom_call" | custom-call | tf_op jit(solution)/shard_map/picked/pallas_call | solution.py:425
  159.8 2.1 %all-gather.5.cloned.1.call-done = bf16[2048,2304]{1,0:T(8,128)(2,1)} async-done(((bf16[128,2304]{1,0:T(8,128)(2,1)}), bf16[2048,2304]{1,0:T(8,128)(2,1)}) %all-gather.5.cloned.1.call-update) | async-done | bytes 9437200 | tf_op jit(solution)/shard_map/all_gather | solution.py:476
  161.9 2.5 %collective-permute-done.24.refs_6_ = bf16[256,256]{1,0:T(8,128)(2,1)S(1)} collective-permute-done((bf16[256,256]{1,0:T(8,128)(2,1)S(1)}, bf16[256,256]{1,0:T(8,128)(2,1)S(1)}, u32[]{:S(2)}, u32[]{:S(2)}) %collective-permute-start.24) | collective-permute-done | bytes 131104 | tf_op jit(solution)/shard_map/ppermute | solution.py:368
  164.4 3.7 %copy-done.1 = bf16[2048,2304]{1,0:T(8,128)(2,1)S(1)} copy-done((bf16[2048,2304]{1,0:T(8,128)(2,1)S(1)}, bf16[2048,2304]{1,0:T(8,128)(2,1)}, u32[]{:S(2)}) %copy-start.1) | copy-done | bytes 9437208
  168.1 2.8 %output_rows.1 = (f32[128,2304]{1,0:T(8,128)S(1)}, bf16[128,2304]{1,0:T(8,128)(2,1)S(1)}) custom-call(s32[1]{0:T(128)} %bitcast.info, bf16[256,256]{1,0:T(8,128)(2,1)S(1)} %get-tuple-element.33.refs_0_, bf16[256,256]{1,0:T(8,128)(2,1)S(1)} %collective-permute-done.19.refs_1_, bf16[256,256]{1,0:T(8,128)(2,1)S(1)} %collective-permute-done.20.refs_2_, ...), custom_call_target="tpu_custom_call" | custom-call | flops 2415919104 | bytes 9437184 | tf_op jit(solution)/shard_map/output_rows/pallas_call | solution.py:346
  171.3 1.6 collective-permute-done.27
  173.0 0.9 add_convert_fusion
  (65 shorter events, 3.7 us)
Async XLA Ops:
  7.2 27.7 %copy-start = (bf16[2304,512]{1,0:T(8,128)(2,1)S(1)}, bf16[2304,512]{1,0:T(8,128)(2,1)}, u32[]{:S(2)}) copy-start(bf16[2304,512]{1,0:T(8,128)(2,1)} %param.23) | copy-start | bytes 7077892
  7.2 27.7 %copy-start.5 = (bf16[128,2304]{1,0:T(8,128)(2,1)S(1)}, bf16[128,2304]{1,0:T(8,128)(2,1)}, u32[]{:S(2)}) copy-start(bf16[128,2304]{1,0:T(8,128)(2,1)} %param.13) | copy-start | bytes 1769476
  7.2 69.2 %all-gather.3.cloned.1.call-start = ((), (), s32[]{:S(2)}) async-start(), calls=%async_computation | async-start | bytes 10027008 | tf_op jit(solution)/shard_map/all_gather | solution.py:459
  7.9 154.0 %all-gather.5.cloned.1.call-start = ((), (), s32[]{:S(2)}) async-start(), calls=%async_computation.1 | async-start | bytes 10027008 | tf_op jit(solution)/shard_map/all_gather | solution.py:476
  9.6 7.3 %collective-permute-start.6 = (bf16[16,2304]{1,0:T(8,128)(2,1)S(1)}, bf16[16,2304]{1,0:T(8,128)(2,1)S(1)}, u32[]{:S(2)}, u32[]{:S(2)}) collective-permute-start(bf16[16,2304]{1,0:T(8,128)(2,1)S(1)} %get-tuple-element.47), channel_id=1, source_target_pairs={{0,2},{1,3},{2,4},{3,5},{4,6},{5,7},{6,8},{7,9},{8,10},{9,11},{10,... | collective-permute-start | bytes 221192 | tf_op jit(solution)/shard_map/ppermute | solution.py:368
  11.2 6.3 %collective-permute-start.10 = (bf16[16,2304]{1,0:T(8,128)(2,1)S(1)}, bf16[16,2304]{1,0:T(8,128)(2,1)S(1)}, u32[]{:S(2)}, u32[]{:S(2)}) collective-permute-start(bf16[16,2304]{1,0:T(8,128)(2,1)S(1)} %get-tuple-element.47), channel_id=1, source_target_pairs={{0,14},{1,15},{2,0},{3,1},{4,2},{5,3},{6,4},{7,5},{8,6},{9,7},{10,... | collective-permute-start | bytes 221192 | tf_op jit(solution)/shard_map/ppermute | solution.py:368
  16.9 4.4 %collective-permute-start.7 = (bf16[16,2304]{1,0:T(8,128)(2,1)S(1)}, bf16[16,2304]{1,0:T(8,128)(2,1)S(1)}, u32[]{:S(2)}, u32[]{:S(2)}) collective-permute-start(bf16[16,2304]{1,0:T(8,128)(2,1)S(1)} %collective-permute-done.6), channel_id=1, source_target_pairs={{0,2},{1,3},{2,4},{3,5},{4,6},{5,7},{6,8},{7,9},{8,10},{9,11},{10,... | collective-permute-start | bytes 221192 | tf_op jit(solution)/shard_map/ppermute | solution.py:368
  17.5 4.4 %collective-permute-start.11 = (bf16[16,2304]{1,0:T(8,128)(2,1)S(1)}, bf16[16,2304]{1,0:T(8,128)(2,1)S(1)}, u32[]{:S(2)}, u32[]{:S(2)}) collective-permute-start(bf16[16,2304]{1,0:T(8,128)(2,1)S(1)} %collective-permute-done.10), channel_id=1, source_target_pairs={{0,14},{1,15},{2,0},{3,1},{4,2},{5,3},{6,4},{7,5},{8,6},{9,7},{10,... | collective-permute-start | bytes 221192 | tf_op jit(solution)/shard_map/ppermute | solution.py:368
  21.3 4.4 %collective-permute-start.8 = (bf16[16,2304]{1,0:T(8,128)(2,1)S(1)}, bf16[16,2304]{1,0:T(8,128)(2,1)S(1)}, u32[]{:S(2)}, u32[]{:S(2)}) collective-permute-start(bf16[16,2304]{1,0:T(8,128)(2,1)S(1)} %collective-permute-done.7), channel_id=1, source_target_pairs={{0,2},{1,3},{2,4},{3,5},{4,6},{5,7},{6,8},{7,9},{8,10},{9,11},{10,... | collective-permute-start | bytes 221192 | tf_op jit(solution)/shard_map/ppermute | solution.py:368
  22.0 11.0 %collective-permute-start.12 = (bf16[16,2304]{1,0:T(8,128)(2,1)S(1)}, bf16[16,2304]{1,0:T(8,128)(2,1)S(1)}, u32[]{:S(2)}, u32[]{:S(2)}) collective-permute-start(bf16[16,2304]{1,0:T(8,128)(2,1)S(1)} %collective-permute-done.11), channel_id=1, source_target_pairs={{0,14},{1,15},{2,0},{3,1},{4,2},{5,3},{6,4},{7,5},{8,6},{9,7},{10,... | collective-permute-start | bytes 221192 | tf_op jit(solution)/shard_map/ppermute | solution.py:368
  25.7 6.6 %collective-permute-start.9 = (bf16[16,2304]{1,0:T(8,128)(2,1)S(1)}, bf16[16,2304]{1,0:T(8,128)(2,1)S(1)}, u32[]{:S(2)}, u32[]{:S(2)}) collective-permute-start(bf16[16,2304]{1,0:T(8,128)(2,1)S(1)} %collective-permute-done.8), channel_id=1, source_target_pairs={{0,2},{1,3},{2,4},{3,5},{4,6},{5,7},{6,8},{7,9},{8,10},{9,11},{10,... | collective-permute-start | bytes 221192 | tf_op jit(solution)/shard_map/ppermute | solution.py:368
  32.9 2.5 %copy-start.7 = (f32[512]{0:T(512)S(1)}, f32[512]{0:T(512)}, u32[]{:S(2)}) copy-start(f32[512]{0:T(512)} %param.24) | copy-start | bytes 6148
  34.9 6.4 %copy-start.11 = (s32[16,1]{0,1:T(1,128)S(1)}, s32[16,1]{0,1:T(1,128)}, u32[]{:S(2)}) copy-start(s32[16,1]{0,1:T(1,128)} %param.25) | copy-start | bytes 196
  34.9 6.4 %copy-start.10 = (f32[2]{0:T(128)S(1)}, f32[2]{0:T(128)}, u32[]{:S(2)}) copy-start(f32[2]{0:T(128)} %param.19) | copy-start | bytes 28
  34.9 6.4 %copy-start.6 = (bf16[2304,2]{0,1:T(2,128)(2,1)S(1)}, bf16[2304,2]{0,1:T(2,128)(2,1)}, u32[]{:S(2)}) copy-start(bf16[2304,2]{0,1:T(2,128)(2,1)} %param.18) | copy-start | bytes 27652
  36.2 5.5 %collective-permute-start = (bf16[128,512]{1,0:T(8,128)(2,1)S(1)}, bf16[128,512]{1,0:T(8,128)(2,1)S(1)}, u32[]{:S(2)}, u32[]{:S(2)}) collective-permute-start(bf16[128,512]{1,0:T(8,128)(2,1)S(1)} %get-tuple-element.49), channel_id=1, source_target_pairs={{0,16},{16,32},{32,48},{48,0},{64,80},{80,96},{96,112},{112,64},{1... | collective-permute-start | bytes 393224 | tf_op jit(solution)/shard_map/ppermute | solution.py:368
  37.5 6.5 %collective-permute-start.1 = (bf16[128,512]{1,0:T(8,128)(2,1)S(1)}, bf16[128,512]{1,0:T(8,128)(2,1)S(1)}, u32[]{:S(2)}, u32[]{:S(2)}) collective-permute-start(bf16[128,512]{1,0:T(8,128)(2,1)S(1)} %get-tuple-element.49), channel_id=1, source_target_pairs={{0,32},{16,48},{32,0},{48,16},{64,96},{80,112},{96,64},{112,80},{1... | collective-permute-start | bytes 393224 | tf_op jit(solution)/shard_map/ppermute | solution.py:368
  40.2 4.2 %collective-permute-start.2 = (bf16[128,512]{1,0:T(8,128)(2,1)S(1)}, bf16[128,512]{1,0:T(8,128)(2,1)}, u32[]{:S(2)}, u32[]{:S(2)}) collective-permute-start(bf16[128,512]{1,0:T(8,128)(2,1)S(1)} %get-tuple-element.49), channel_id=1, source_target_pairs={{0,48},{16,0},{32,16},{48,32},{64,112},{80,64},{96,80},{112,96},{1... | collective-permute-start | bytes 393224 | tf_op jit(solution)/shard_map/ppermute | solution.py:368
  45.4 8.5 %collective-permute-start.3 = (bf16[4,128,512]{2,1,0:T(8,128)(2,1)S(1)}, bf16[4,128,512]{2,1,0:T(8,128)(2,1)S(1)}, u32[]{:S(2)}, u32[]{:S(2)}) collective-permute-start(bf16[4,128,512]{2,1,0:T(8,128)(2,1)S(1)} %pad_maximum_fusion), channel_id=1, source_target_pairs={{0,64},{16,80},{32,96},{48,112},{64,128},{80,144},{96,160},{112,17... | collective-permute-start | bytes 1572872 | tf_op jit(solution)/shard_map/ppermute | solution.py:368
  45.6 9.6 %collective-permute-start.4 = (bf16[4,128,512]{2,1,0:T(8,128)(2,1)S(1)}, bf16[4,128,512]{2,1,0:T(8,128)(2,1)S(1)}, u32[]{:S(2)}, u32[]{:S(2)}) collective-permute-start(bf16[4,128,512]{2,1,0:T(8,128)(2,1)S(1)} %pad_maximum_fusion), channel_id=1, source_target_pairs={{0,128},{16,144},{32,160},{48,176},{64,192},{80,208},{96,224},{112... | collective-permute-start | bytes 1572872 | tf_op jit(solution)/shard_map/ppermute | solution.py:368
  47.8 21.1 %collective-permute-start.5 = (bf16[4,128,512]{2,1,0:T(8,128)(2,1)S(1)}, bf16[4,128,512]{2,1,0:T(8,128)(2,1)S(1)}, u32[]{:S(2)}, u32[]{:S(2)}) collective-permute-start(bf16[4,128,512]{2,1,0:T(8,128)(2,1)S(1)} %pad_maximum_fusion), channel_id=1, source_target_pairs={{0,192},{16,208},{32,224},{48,240},{64,0},{80,16},{96,32},{112,48}... | collective-permute-start | bytes 1572872 | tf_op jit(solution)/shard_map/ppermute | solution.py:368
  76.4 10.9 %copy-start.4 = (f32[2048,256]{1,0:T(8,128)S(1)}, f32[2048,256]{1,0:T(8,128)}, u32[]{:S(2)}) copy-start(f32[2048,256]{1,0:T(8,128)} %ld.3) | copy-start | bytes 6291460
  76.4 32.4 %slice-start = ((s8[9437184]{0:T(1024)(128)(4,1)}), s8[4194304]{0:T(1024)(128)(4,1)S(1)}, s32[]{:S(2)}) async-start(s8[9437184]{0:T(1024)(128)(4,1)} %bitcast.30), calls=%async_computation.2 | async-start | bytes 8388608
  87.3 21.4 %slice-start.1 = ((s8[9437184]{0:T(1024)(128)(4,1)}), s8[4194304]{0:T(1024)(128)(4,1)S(1)}, s32[]{:S(2)}) async-start(s8[9437184]{0:T(1024)(128)(4,1)} %bitcast.30), calls=%async_computation.3 | async-start | bytes 8388608
  87.4 21.4 %slice-start.2 = ((s8[9437184]{0:T(1024)(128)(4,1)}), s8[1048576]{0:T(1024)(128)(4,1)S(1)}, s32[]{:S(2)}) async-start(s8[9437184]{0:T(1024)(128)(4,1)} %bitcast.30), calls=%async_computation.4 | async-start | bytes 2097152
  87.4 21.4 %copy-start.8 = (bf16[2304,256]{1,0:T(8,128)(2,1)S(1)}, bf16[2304,256]{1,0:T(8,128)(2,1)}, u32[]{:S(2)}) copy-start(bf16[2304,256]{1,0:T(8,128)(2,1)} %param.14) | copy-start | bytes 3538948
  103.9 7.7 %copy-start.9 = (bf16[2304,256]{1,0:T(8,128)(2,1)S(1)}, bf16[2304,256]{1,0:T(8,128)(2,1)}, u32[]{:S(2)}) copy-start(bf16[2304,256]{1,0:T(8,128)(2,1)} %param.17) | copy-start | bytes 3538948
  103.9 10.5 %collective-permute-start.13 = (bf16[2,128,256]{2,1,0:T(8,128)(2,1)S(1)}, bf16[2,128,256]{2,1,0:T(8,128)(2,1)S(1)}, u32[]{:S(2)}, u32[]{:S(2)}) collective-permute-start(bf16[2,128,256]{2,1,0:T(8,128)(2,1)S(1)} %get-tuple-element.25), channel_id=1, source_target_pairs={{0,16},{16,32},{32,48},{48,0},{64,80},{80,96},{96,112},{112,64},{1... | collective-permute-start | bytes 393224 | tf_op jit(solution)/shard_map/ppermute | solution.py:368
  105.2 9.2 %collective-permute-start.14 = (bf16[2,128,256]{2,1,0:T(8,128)(2,1)S(1)}, bf16[2,128,256]{2,1,0:T(8,128)(2,1)S(1)}, u32[]{:S(2)}, u32[]{:S(2)}) collective-permute-start(bf16[2,128,256]{2,1,0:T(8,128)(2,1)S(1)} %get-tuple-element.25), channel_id=1, source_target_pairs={{0,32},{16,48},{32,0},{48,16},{64,96},{80,112},{96,64},{112,80},{1... | collective-permute-start | bytes 393224 | tf_op jit(solution)/shard_map/ppermute | solution.py:368
  107.6 6.8 %collective-permute-start.15 = (bf16[2,128,256]{2,1,0:T(8,128)(2,1)S(1)}, bf16[2,128,256]{2,1,0:T(8,128)(2,1)S(1)}, u32[]{:S(2)}, u32[]{:S(2)}) collective-permute-start(bf16[2,128,256]{2,1,0:T(8,128)(2,1)S(1)} %get-tuple-element.25), channel_id=1, source_target_pairs={{0,48},{16,0},{32,16},{48,32},{64,112},{80,64},{96,80},{112,96},{1... | collective-permute-start | bytes 393224 | tf_op jit(solution)/shard_map/ppermute | solution.py:368
  115.3 9.3 %collective-permute-start.16 = (bf16[2,128,256]{2,1,0:T(8,128)(2,1)S(1)}, bf16[2,128,256]{2,1,0:T(8,128)(2,1)S(1)}, u32[]{:S(2)}, u32[]{:S(2)}) collective-permute-start(bf16[2,128,256]{2,1,0:T(8,128)(2,1)S(1)} %get-tuple-element.27.own), channel_id=1, source_target_pairs={{0,64},{16,80},{32,96},{48,112},{64,128},{80,144},{96,160},{112,17... | collective-permute-start | bytes 393224 | tf_op jit(solution)/shard_map/ppermute | solution.py:368
  116.6 11.2 %collective-permute-start.17 = (bf16[2,128,256]{2,1,0:T(8,128)(2,1)S(1)}, bf16[2,128,256]{2,1,0:T(8,128)(2,1)S(1)}, u32[]{:S(2)}, u32[]{:S(2)}) collective-permute-start(bf16[2,128,256]{2,1,0:T(8,128)(2,1)S(1)} %get-tuple-element.27.own), channel_id=1, source_target_pairs={{0,128},{16,144},{32,160},{48,176},{64,192},{80,208},{96,224},{112... | collective-permute-start | bytes 393224 | tf_op jit(solution)/shard_map/ppermute | solution.py:368
  117.9 14.7 %collective-permute-start.18 = (bf16[2,128,256]{2,1,0:T(8,128)(2,1)S(1)}, bf16[2,128,256]{2,1,0:T(8,128)(2,1)S(1)}, u32[]{:S(2)}, u32[]{:S(2)}) collective-permute-start(bf16[2,128,256]{2,1,0:T(8,128)(2,1)S(1)} %get-tuple-element.27.own), channel_id=1, source_target_pairs={{0,192},{16,208},{32,224},{48,240},{1,193},{17,209},{33,225},{49,2... | collective-permute-start | bytes 393224 | tf_op jit(solution)/shard_map/ppermute | solution.py:368
  119.2 13.4 %copy-start.3 = (f32[128]{0:T(128)S(1)}, f32[128]{0:T(128)}, u32[]{:S(2)}) copy-start(f32[128]{0:T(128)} %param.21) | copy-start | bytes 1540
  136.4 8.9 %collective-permute-start.19 = (bf16[256,256]{1,0:T(8,128)(2,1)S(1)}, bf16[256,256]{1,0:T(8,128)(2,1)S(1)}, u32[]{:S(2)}, u32[]{:S(2)}) collective-permute-start(bf16[256,256]{1,0:T(8,128)(2,1)S(1)} %get-tuple-element.34), channel_id=1, source_target_pairs={{0,8},{1,13},{2,10},{3,15},{4,12},{5,1},{6,14},{7,3},{8,0},{9,5},{... | collective-permute-start | bytes 393224 | tf_op jit(solution)/shard_map/ppermute | solution.py:368
  136.8 14.2 %collective-permute-start.20 = (bf16[256,256]{1,0:T(8,128)(2,1)S(1)}, bf16[256,256]{1,0:T(8,128)(2,1)S(1)}, u32[]{:S(2)}, u32[]{:S(2)}) collective-permute-start(bf16[256,256]{1,0:T(8,128)(2,1)S(1)} %get-tuple-element.35), channel_id=1, source_target_pairs={{0,6},{1,7},{2,8},{3,9},{4,10},{5,11},{6,12},{7,13},{8,14},{9,15},... | collective-permute-start | bytes 393224 | tf_op jit(solution)/shard_map/ppermute | solution.py:368
  137.8 13.2 %collective-permute-start.21 = (bf16[256,256]{1,0:T(8,128)(2,1)S(1)}, bf16[256,256]{1,0:T(8,128)(2,1)S(1)}, u32[]{:S(2)}, u32[]{:S(2)}) collective-permute-start(bf16[256,256]{1,0:T(8,128)(2,1)S(1)} %get-tuple-element.36), channel_id=1, source_target_pairs={{0,10},{1,11},{2,12},{3,13},{4,14},{5,15},{6,0},{7,1},{8,2},{9,3},... | collective-permute-start | bytes 393224 | tf_op jit(solution)/shard_map/ppermute | solution.py:368
  141.6 20.3 %collective-permute-start.22 = (bf16[256,256]{1,0:T(8,128)(2,1)}, bf16[256,256]{1,0:T(8,128)(2,1)S(1)}, u32[]{:S(2)}, u32[]{:S(2)}) collective-permute-start(bf16[256,256]{1,0:T(8,128)(2,1)} %get-tuple-element.37), channel_id=1, source_target_pairs={{0,4},{1,5},{2,6},{3,7},{4,8},{5,9},{6,10},{7,11},{8,12},{9,13},{1... | collective-permute-start | bytes 393224 | tf_op jit(solution)/shard_map/ppermute | solution.py:368
  143.7 18.2 %collective-permute-start.23 = (bf16[256,256]{1,0:T(8,128)(2,1)}, bf16[256,256]{1,0:T(8,128)(2,1)S(1)}, u32[]{:S(2)}, u32[]{:S(2)}) collective-permute-start(bf16[256,256]{1,0:T(8,128)(2,1)} %get-tuple-element.38), channel_id=1, source_target_pairs={{0,12},{1,13},{2,14},{3,15},{4,0},{5,1},{6,2},{7,3},{8,4},{9,5},{1... | collective-permute-start | bytes 393224 | tf_op jit(solution)/shard_map/ppermute | solution.py:368
  145.3 16.6 %collective-permute-start.25 = (bf16[256,256]{1,0:T(8,128)(2,1)}, bf16[256,256]{1,0:T(8,128)(2,1)S(1)}, u32[]{:S(2)}, u32[]{:S(2)}) collective-permute-start(bf16[256,256]{1,0:T(8,128)(2,1)} %get-tuple-element.39), channel_id=1, source_target_pairs={{0,2},{1,3},{2,4},{3,5},{4,6},{5,7},{6,8},{7,9},{8,10},{9,11},{10,... | collective-permute-start | bytes 393224 | tf_op jit(solution)/shard_map/ppermute | solution.py:368
  151.0 10.9 %collective-permute-start.26 = (bf16[256,256]{1,0:T(8,128)(2,1)}, bf16[256,256]{1,0:T(8,128)(2,1)S(1)}, u32[]{:S(2)}, u32[]{:S(2)}) collective-permute-start(bf16[256,256]{1,0:T(8,128)(2,1)} %get-tuple-element.40), channel_id=1, source_target_pairs={{0,14},{1,15},{2,0},{3,1},{4,2},{5,3},{6,4},{7,5},{8,6},{9,7},{10,... | collective-permute-start | bytes 393224 | tf_op jit(solution)/shard_map/ppermute | solution.py:368
  151.0 13.4 %collective-permute-start.24 = (bf16[256,256]{1,0:T(8,128)(2,1)S(1)}, bf16[256,256]{1,0:T(8,128)(2,1)S(1)}, u32[]{:S(2)}, u32[]{:S(2)}) collective-permute-start(bf16[256,256]{1,0:T(8,128)(2,1)S(1)} %collective-permute-done.19.refs_1_), channel_id=1, source_target_pairs={{1,13},{3,15},{5,1},{7,3},{9,5},{11,7},{13,9},{15,11},{17,29},{19,... | collective-permute-start | bytes 393224 | tf_op jit(solution)/shard_map/ppermute | solution.py:368
  156.3 1.6 copy-start.2
  164.4 3.7 %copy-start.1 = (bf16[2048,2304]{1,0:T(8,128)(2,1)S(1)}, bf16[2048,2304]{1,0:T(8,128)(2,1)}, u32[]{:S(2)}) copy-start(bf16[2048,2304]{1,0:T(8,128)(2,1)} %all-gather.5.cloned.1.call-done) | copy-start | bytes 28311556
  170.9 2.1 %collective-permute-start.27 = (bf16[128,2304]{1,0:T(8,128)(2,1)S(1)}, bf16[128,2304]{1,0:T(8,128)(2,1)S(1)}, u32[]{:S(2)}, u32[]{:S(2)}) collective-permute-start(bf16[128,2304]{1,0:T(8,128)(2,1)S(1)} %get-tuple-element.43), channel_id=1, source_target_pairs={{0,1},{1,0},{2,3},{3,2},{4,5},{5,4},{6,7},{7,6},{8,9},{9,8},{10,11... | collective-permute-start | bytes 1769480 | tf_op jit(solution)/shard_map/ppermute | solution.py:368
Sparse Core Ops, SparseCore 0:
  9.9 66.5 all-gather.2
  79.5 82.3 all-gather.4
